TPU v7x, 32 devices: a whole 2x2x4 slice. The times are simulated.
32 devices in a mesh: ga: 4 (over y, x), ea: 8 (over z, core).
Axes of the slice: x: 2, y: 2, z: 4, core: 2. Of those that a mesh axis runs over, the one named last changes fastest.
Arguments:
- layer_input: bfloat16 [8192, 2048], P(('ga', 'ea')), may hold values from -6 to 6
- w_query: bfloat16 [2048, 4096], P('ga'), may hold values from -0.125 to 0.125
- w_key: bfloat16 [2048, 512], P('ga'), may hold values from -0.125 to 0.125
- w_value: bfloat16 [2048, 512], P('ga'), may hold values from -0.125 to 0.125
- w_out: bfloat16 [4096, 2048], P('ga'), may hold values from -1 to 1
- attn_gain: bfloat16 [2048], P('ga'), may hold values from 0.5 to 1.5
- query_gain: bfloat16 [128], P('ga'), may hold values from 0.5 to 1.5
- key_gain: bfloat16 [128], P('ga'), may hold values from 0.5 to 1.5
- ffn_gain: bfloat16 [2048], P('ga'), may hold values from 0.5 to 1.5
- w_router: bfloat16 [2048, 16], P('ga'), may hold values from -0.0625 to 0.0625
- w_gate: bfloat16 [16, 2048, 768], P('ea', 'ga'), may hold values from -0.125 to 0.125
- w_up: bfloat16 [16, 2048, 768], P('ea', 'ga'), may hold values from -0.125 to 0.125
- w_down: bfloat16 [16, 768, 2048], P('ea', None, 'ga'), may hold values from -0.875 to 0.875
- routes: int32 [8192, 8], P(('ga', 'ea')), may hold values from 0 to 15, all different within a row; in each aligned block of 256 rows (0 to 255, 256 to 511, ...) at most 144 rows name the same one
- pic_starts: int32 [4, 4], P('ga'), may hold values from -1 to 1792, as said below
- cotangent: bfloat16 [8192, 2048], P(('ga', 'ea')), may hold values from -6 to 6
Outputs:
- layer_output: bfloat16 [8192, 2048], P(('ga', 'ea'))
- input_grad: bfloat16 [8192, 2048], P(('ga', 'ea'))
- w_query_grad: float32 [2048, 4096], P('ga')
- w_key_grad: float32 [2048, 512], P('ga')
- w_value_grad: float32 [2048, 512], P('ga')
- w_out_grad: float32 [4096, 2048], P('ga')
- attn_gain_grad: float32 [2048], P('ga')
- query_gain_grad: float32 [128], P('ga')
- key_gain_grad: float32 [128], P('ga')
- ffn_gain_grad: float32 [2048], P('ga')
- w_router_grad: float32 [2048, 16], P('ga')
- w_gate_grad: float32 [16, 2048, 768], P('ea', 'ga')
- w_up_grad: float32 [16, 2048, 768], P('ea', 'ga')
- w_down_grad: float32 [16, 768, 2048], P('ea', None, 'ga')
Inputs may be any that keep to these rules, and one draw needn't show every extreme that they name: `routes`: each row names 8 different experts. In each aligned block of 256 rows (the rows of one device) no expert is named by more than 144 rows. `pic_starts`: row s lists the first positions of sequence s's picture pieces, each of 256 positions; entry j, if present, lies between j * 512 and (j + 1) * 512 - 256; present entries come first, at least one is present, and -1 marks an absent one.
All inputs are finite; a program needn't handle non-finite values.
Results may differ from a plain program's by a relative error of at most 0.025.
Values may be sent and summed in bfloat16 or wider, within the bound.
No kernel may reach another device: no remote copies, remote signals or barrier semaphores. Data moves between devices by JAX's collectives and lax.ppermute only.
A program may use at most 320 MiB of HBM per device.

v0:
```python
import jax
import jax.numpy as jnp
from jax import lax
from jax.sharding import PartitionSpec as P

HEADS = 32
KV = 4
HD = 128
PIC = 256


NORM_EPS = 1e-06
ROPE_THETA = 1000000.0
MASKED_SCORE = -1e30
PRECISE = lax.Precision.HIGHEST


def rms_norm(values, norm_gain):
    inverse = lax.rsqrt(jnp.mean(values * values, axis=-1, keepdims=True) + NORM_EPS)
    return values * inverse * norm_gain


def rotate(values, positions):
    half_dim = values.shape[-1] // 2
    frequency = ROPE_THETA ** (-jnp.arange(half_dim, dtype=jnp.float32) * 2.0 / values.shape[-1])
    angles = positions.astype(jnp.float32)[:, None] * frequency[None, :]
    cosine = jnp.cos(angles)[:, None, :]
    sine_part = jnp.sin(angles)[:, None, :]
    first_half = values[..., :half_dim]
    second_half = values[..., half_dim:]
    return jnp.concatenate(
        [
            first_half * cosine - second_half * sine_part,
            second_half * cosine + first_half * sine_part,
        ],
        axis=-1,
    )


def swiglu(gate_pre, up_pre):
    return gate_pre / (1.0 + jnp.exp(-gate_pre)) * up_pre


def softmax_last(scores):
    row_peak = jnp.max(scores, axis=-1, keepdims=True)
    weights = jnp.exp(scores - row_peak)
    return weights / jnp.sum(weights, axis=-1, keepdims=True)


def piece_ids(starts, positions):
    inside = (
        (starts[:, None] >= 0)
        & (positions[None, :] >= starts[:, None])
        & (positions[None, :] < starts[:, None] + PIC)
    )
    labels = jnp.arange(1, starts.shape[0] + 1, dtype=jnp.int32)[:, None]
    return jnp.sum(jnp.where(inside, labels, 0), axis=0)


def allowed_mask(starts, query_pos, key_pos):
    query_piece = piece_ids(starts, query_pos)
    key_piece = piece_ids(starts, key_pos)
    causal = key_pos[None, :] <= query_pos[:, None]
    shared = (query_piece[:, None] == key_piece[None, :]) & (query_piece[:, None] > 0)
    return causal | shared


def route_slots(routes, expert_total, capacity, owner_count, local_experts):
    flat_routes = routes.reshape(-1)
    onehot = (flat_routes[:, None] == jnp.arange(expert_total, dtype=jnp.int32)[None, :]).astype(
        jnp.int32
    )
    slot_rank = jnp.sum((jnp.cumsum(onehot, axis=0) - onehot) * onehot, axis=1)
    owner_dev = flat_routes // local_experts
    local_expert = flat_routes % local_experts
    route_slot = (local_expert * owner_count + owner_dev) * capacity + slot_rank
    route_count = flat_routes.shape[0]
    source = (
        jnp.full((expert_total * capacity,), route_count, jnp.int32)
        .at[route_slot]
        .set(jnp.arange(route_count, dtype=jnp.int32))
    )
    return (route_slot, source)


def contract_rows(left, right):
    return lax.dot_general(
        left, right, (((0,), (0,)), ((), ())), preferred_element_type=jnp.float32
    )


def contract_cols(left, right):
    return lax.dot_general(
        left, right, (((1,), (1,)), ((), ())), preferred_element_type=jnp.float32
    )


def body(
    layer_input,
    w_query,
    w_key,
    w_value,
    w_out,
    attn_gain,
    query_gain,
    key_gain,
    ffn_gain,
    w_router,
    w_gate,
    w_up,
    w_down,
    routes,
    pic_starts,
    cotangent,
):
    tok_count = layer_input.shape[0]
    model_width = layer_input.shape[1]
    top_count = routes.shape[1]
    owner_count = lax.axis_size("ea")
    local_experts = w_gate.shape[0]
    expert_total = local_experts * owner_count
    capacity = max(2, 9 * tok_count * top_count // (8 * expert_total))
    route_count = tok_count * top_count
    group_size = HEADS // KV
    score_scale = HD ** (-0.5)
    gathered = (
        lax.all_gather(attn_gain, "ga", axis=0, tiled=True),
        lax.all_gather(w_query, "ga", axis=0, tiled=True),
        lax.all_gather(w_key, "ga", axis=0, tiled=True),
        lax.all_gather(w_value, "ga", axis=0, tiled=True),
        lax.all_gather(w_out, "ga", axis=0, tiled=True),
        lax.all_gather(query_gain, "ga", axis=0, tiled=True),
        lax.all_gather(key_gain, "ga", axis=0, tiled=True),
        lax.all_gather(ffn_gain, "ga", axis=0, tiled=True),
        lax.all_gather(w_router, "ga", axis=0, tiled=True),
    )
    (
        attn_gain_full,
        query_full,
        key_full,
        value_full,
        out_full,
        query_gain_full,
        key_gain_full,
        ffn_gain_full,
        router_full,
    ) = gathered
    attn_gain_f = attn_gain_full.astype(jnp.float32)
    query_gain_f = query_gain_full.astype(jnp.float32)
    key_gain_f = key_gain_full.astype(jnp.float32)
    ffn_gain_f = ffn_gain_full.astype(jnp.float32)
    positions = lax.axis_index("ea") * tok_count + jnp.arange(tok_count, dtype=jnp.int32)
    key_pos = jnp.arange(tok_count * owner_count, dtype=jnp.int32)
    allowed = allowed_mask(pic_starts[0], positions, key_pos)

    def prep_heads(raw_heads, norm_gain):
        return rotate(rms_norm(raw_heads, norm_gain), positions)

    input_f = layer_input.astype(jnp.float32)
    normed = rms_norm(input_f, attn_gain_f).astype(jnp.bfloat16)
    q_raw = jnp.dot(normed, query_full, preferred_element_type=jnp.float32).reshape(
        tok_count, HEADS, HD
    )
    k_raw = jnp.dot(normed, key_full, preferred_element_type=jnp.float32).reshape(tok_count, KV, HD)
    value_loc = jnp.dot(normed, value_full, preferred_element_type=jnp.float32).astype(jnp.bfloat16)
    q_use = prep_heads(q_raw, query_gain_f).astype(jnp.bfloat16)
    k_use = prep_heads(k_raw, key_gain_f).astype(jnp.bfloat16)
    key_heads = jnp.transpose(k_use, (1, 0, 2))
    value_heads = jnp.transpose(value_loc.reshape(tok_count, KV, HD), (1, 0, 2))
    key_all, value_all = (
        lax.all_gather(key_heads, "ea", axis=1, tiled=True),
        lax.all_gather(value_heads, "ea", axis=1, tiled=True),
    )
    query_heads = jnp.transpose(q_use.reshape(tok_count, KV, group_size, HD), (1, 0, 2, 3))

    def masked_scores(query_blk, key_blk):
        scores = (
            jnp.einsum("tgh,kh->tgk", query_blk, key_blk, preferred_element_type=jnp.float32)
            * score_scale
        )
        return jnp.where(allowed[:, None, :], scores, MASKED_SCORE)

    def forward_head(operands):
        query_blk, key_blk, value_blk = operands
        scores = masked_scores(query_blk, key_blk)
        row_peak = jnp.max(scores, axis=-1, keepdims=True)
        weights = jnp.exp(scores - row_peak)
        row_total = jnp.sum(weights, axis=-1, keepdims=True)
        attn_probs = (weights / row_total).astype(jnp.bfloat16)
        head_out = jnp.einsum(
            "tgk,kh->tgh", attn_probs, value_blk, preferred_element_type=jnp.float32
        )
        return (head_out.astype(jnp.bfloat16), (row_peak + jnp.log(row_total))[..., 0])

    head_outs, log_total = lax.map(forward_head, (query_heads, key_all, value_all))
    attended = jnp.transpose(head_outs, (1, 0, 2, 3)).reshape(tok_count, HEADS * HD)
    hidden = input_f + jnp.dot(attended, out_full, preferred_element_type=jnp.float32)
    ffn_in = rms_norm(hidden, ffn_gain_f).astype(jnp.bfloat16)
    logits = jnp.dot(ffn_in, router_full, preferred_element_type=jnp.float32)
    chosen = jnp.take_along_axis(logits, routes, axis=1)
    gates = softmax_last(chosen)
    route_slot, source = route_slots(routes, expert_total, capacity, owner_count, local_experts)
    slot_live = source < route_count
    source_route = jnp.minimum(source, route_count - 1)
    send_rows = jnp.where(
        slot_live[:, None], ffn_in[source_route // top_count], jnp.zeros((), jnp.bfloat16)
    )
    send_rows = send_rows.reshape(local_experts, owner_count, capacity, model_width)
    received = lax.all_to_all(send_rows, "ea", split_axis=1, concat_axis=1, tiled=True).reshape(
        local_experts, owner_count * capacity, model_width
    )
    gate_w, up_w, down_w = (
        lax.all_gather(w_gate, "ga", axis=1, tiled=True),
        lax.all_gather(w_up, "ga", axis=1, tiled=True),
        lax.all_gather(w_down, "ga", axis=2, tiled=True),
    )
    gate_pre = jnp.einsum("erd,edf->erf", received, gate_w, preferred_element_type=jnp.float32)
    up_pre = jnp.einsum("erd,edf->erf", received, up_w, preferred_element_type=jnp.float32)
    act = swiglu(gate_pre, up_pre).astype(jnp.bfloat16)
    expert_out = jnp.einsum("erf,efd->erd", act, down_w, preferred_element_type=jnp.float32).astype(
        jnp.bfloat16
    )
    returned = lax.all_to_all(
        expert_out.reshape(local_experts, owner_count, capacity, model_width),
        "ea",
        split_axis=1,
        concat_axis=1,
        tiled=True,
    )
    returned = returned.reshape(expert_total * capacity, model_width)
    route_out = returned[route_slot].reshape(tok_count, top_count, model_width)
    mixture = jnp.sum(gates[:, :, None] * route_out, axis=1)
    layer_output = (hidden + mixture).astype(jnp.bfloat16)
    grad_out = cotangent.astype(jnp.float32)
    route_grad = (
        (gates[:, :, None] * grad_out[:, None, :])
        .astype(jnp.bfloat16)
        .reshape(route_count, model_width)
    )
    gate_grad = jnp.einsum("tkd,td->tk", route_out, cotangent, preferred_element_type=jnp.float32)
    send_grads = jnp.where(
        slot_live[:, None], route_grad[source_route], jnp.zeros((), jnp.bfloat16)
    )
    send_grads = send_grads.reshape(local_experts, owner_count, capacity, model_width)
    grad_rows = lax.all_to_all(send_grads, "ea", split_axis=1, concat_axis=1, tiled=True).reshape(
        local_experts, owner_count * capacity, model_width
    )
    act_grad = jnp.einsum("erd,efd->erf", grad_rows, down_w, preferred_element_type=jnp.float32)
    unused, swiglu_back = jax.vjp(swiglu, gate_pre, up_pre)
    gate_pre_grad, up_pre_grad = swiglu_back(act_grad)
    gate_pre_grad = gate_pre_grad.astype(jnp.bfloat16)
    up_pre_grad = up_pre_grad.astype(jnp.bfloat16)
    down_grad = jnp.einsum("erf,erd->efd", act, grad_rows, preferred_element_type=jnp.float32)
    gate_weight_grad = jnp.einsum(
        "erd,erf->edf", received, gate_pre_grad, preferred_element_type=jnp.float32
    )
    up_weight_grad = jnp.einsum(
        "erd,erf->edf", received, up_pre_grad, preferred_element_type=jnp.float32
    )
    row_grad = jnp.einsum("erf,edf->erd", gate_pre_grad, gate_w, preferred_element_type=jnp.float32)
    row_grad = (
        row_grad + jnp.einsum("erf,edf->erd", up_pre_grad, up_w, preferred_element_type=jnp.float32)
    ).astype(jnp.bfloat16)
    back_rows = lax.all_to_all(
        row_grad.reshape(local_experts, owner_count, capacity, model_width),
        "ea",
        split_axis=1,
        concat_axis=1,
        tiled=True,
    )
    back_rows = back_rows.reshape(expert_total * capacity, model_width)
    gate_sum, upw_sum, down_sum = (
        lax.psum_scatter(
            gate_weight_grad.astype(jnp.bfloat16), "ga", scatter_dimension=1, tiled=True
        ).astype(jnp.float32),
        lax.psum_scatter(
            up_weight_grad.astype(jnp.bfloat16), "ga", scatter_dimension=1, tiled=True
        ).astype(jnp.float32),
        lax.psum_scatter(
            down_grad.astype(jnp.bfloat16), "ga", scatter_dimension=2, tiled=True
        ).astype(jnp.float32),
    )
    unused, gate_back = jax.vjp(softmax_last, chosen)
    (chosen_grad,) = gate_back(gate_grad)
    picks = (routes[:, :, None] == jnp.arange(expert_total, dtype=jnp.int32)[None, None, :]).astype(
        jnp.float32
    )
    logit_grad = jnp.einsum("tk,tke->te", chosen_grad, picks)
    router_grad = lax.dot_general(
        ffn_in.astype(jnp.float32), logit_grad, (((0,), (0,)), ((), ())), precision=PRECISE
    )
    ffn_in_grad = jnp.sum(
        back_rows[route_slot].reshape(tok_count, top_count, model_width).astype(jnp.float32), axis=1
    )
    ffn_in_grad = ffn_in_grad + jnp.dot(
        logit_grad, router_full.astype(jnp.float32).T, precision=PRECISE
    )
    unused, ffn_back = jax.vjp(rms_norm, hidden, ffn_gain_f)
    hidden_part, ffn_gain_grad = ffn_back(ffn_in_grad)
    hidden_grad = grad_out + hidden_part
    branch_grad = hidden_grad.astype(jnp.bfloat16)
    out_grad = contract_rows(attended, branch_grad)
    attended_grad = contract_cols(branch_grad, out_full).astype(jnp.bfloat16)
    grad_heads = jnp.transpose(attended_grad.reshape(tok_count, KV, group_size, HD), (1, 0, 2, 3))

    def backward_head(operands):
        query_blk, key_blk, value_blk, grad_blk, total_blk = operands
        scores = masked_scores(query_blk, key_blk)
        probs_f = jnp.exp(scores - total_blk[..., None])
        attn_probs = probs_f.astype(jnp.bfloat16)
        prob_grad = jnp.einsum(
            "tgh,kh->tgk", grad_blk, value_blk, preferred_element_type=jnp.float32
        )
        inner = jnp.sum(probs_f * prob_grad, axis=-1, keepdims=True)
        score_grad = (probs_f * (prob_grad - inner)).astype(jnp.bfloat16)
        query_grad = (
            jnp.einsum("tgk,kh->tgh", score_grad, key_blk, preferred_element_type=jnp.float32)
            * score_scale
        )
        key_grad = (
            jnp.einsum("tgk,tgh->kh", score_grad, query_blk, preferred_element_type=jnp.float32)
            * score_scale
        )
        value_grad = jnp.einsum(
            "tgk,tgh->kh", attn_probs, grad_blk, preferred_element_type=jnp.float32
        )
        return (query_grad, key_grad, value_grad)

    query_grad, key_grad_all, value_grad_all = lax.map(
        backward_head, (query_heads, key_all, value_all, grad_heads, log_total)
    )
    key_grad, value_grad = (
        lax.psum_scatter(
            key_grad_all.astype(jnp.bfloat16), "ea", scatter_dimension=1, tiled=True
        ).astype(jnp.float32),
        lax.psum_scatter(
            value_grad_all.astype(jnp.bfloat16), "ea", scatter_dimension=1, tiled=True
        ).astype(jnp.float32),
    )
    query_grad = query_grad.astype(jnp.bfloat16).astype(jnp.float32)
    query_grad = jnp.transpose(query_grad, (1, 0, 2, 3)).reshape(tok_count, HEADS, HD)
    key_grad = jnp.transpose(key_grad.astype(jnp.bfloat16).astype(jnp.float32), (1, 0, 2))
    value_grad = jnp.transpose(value_grad.astype(jnp.bfloat16), (1, 0, 2)).reshape(
        tok_count, KV * HD
    )
    unused, query_back = jax.vjp(prep_heads, q_raw, query_gain_f)
    q_raw_grad, query_gain_grad = query_back(query_grad)
    unused, key_back = jax.vjp(prep_heads, k_raw, key_gain_f)
    k_raw_grad, key_gain_grad = key_back(key_grad)
    q_raw_grad = q_raw_grad.reshape(tok_count, HEADS * HD).astype(jnp.bfloat16)
    k_raw_grad = k_raw_grad.reshape(tok_count, KV * HD).astype(jnp.bfloat16)
    query_weight_grad = contract_rows(normed, q_raw_grad)
    key_weight_grad = contract_rows(normed, k_raw_grad)
    value_weight_grad = contract_rows(normed, value_grad)
    normed_grad = (
        contract_cols(q_raw_grad, query_full)
        + contract_cols(k_raw_grad, key_full)
        + contract_cols(value_grad, value_full)
    )
    unused, attn_back = jax.vjp(rms_norm, input_f, attn_gain_f)
    input_part, attn_gain_grad = attn_back(normed_grad)
    input_grad = (hidden_grad + input_part).astype(jnp.bfloat16)
    dense_terms = (
        attn_gain_grad,
        query_weight_grad,
        key_weight_grad,
        value_weight_grad,
        out_grad,
        query_gain_grad,
        key_gain_grad,
        ffn_gain_grad,
        router_grad,
    )
    shares = (
        lax.psum_scatter(
            dense_terms[0].astype(jnp.bfloat16), "ga", scatter_dimension=0, tiled=True
        ).astype(jnp.float32),
        lax.psum_scatter(
            dense_terms[1].astype(jnp.bfloat16), "ga", scatter_dimension=0, tiled=True
        ).astype(jnp.float32),
        lax.psum_scatter(
            dense_terms[2].astype(jnp.bfloat16), "ga", scatter_dimension=0, tiled=True
        ).astype(jnp.float32),
        lax.psum_scatter(
            dense_terms[3].astype(jnp.bfloat16), "ga", scatter_dimension=0, tiled=True
        ).astype(jnp.float32),
        lax.psum_scatter(
            dense_terms[4].astype(jnp.bfloat16), "ga", scatter_dimension=0, tiled=True
        ).astype(jnp.float32),
        lax.psum_scatter(
            dense_terms[5].astype(jnp.bfloat16), "ga", scatter_dimension=0, tiled=True
        ).astype(jnp.float32),
        lax.psum_scatter(
            dense_terms[6].astype(jnp.bfloat16), "ga", scatter_dimension=0, tiled=True
        ).astype(jnp.float32),
        lax.psum_scatter(
            dense_terms[7].astype(jnp.bfloat16), "ga", scatter_dimension=0, tiled=True
        ).astype(jnp.float32),
        lax.psum_scatter(
            dense_terms[8].astype(jnp.bfloat16), "ga", scatter_dimension=0, tiled=True
        ).astype(jnp.float32),
    )
    dense_grads = (
        lax.psum(shares[0].astype(jnp.bfloat16), "ea").astype(jnp.float32),
        lax.psum(shares[1].astype(jnp.bfloat16), "ea").astype(jnp.float32),
        lax.psum(shares[2].astype(jnp.bfloat16), "ea").astype(jnp.float32),
        lax.psum(shares[3].astype(jnp.bfloat16), "ea").astype(jnp.float32),
        lax.psum(shares[4].astype(jnp.bfloat16), "ea").astype(jnp.float32),
        lax.psum(shares[5].astype(jnp.bfloat16), "ea").astype(jnp.float32),
        lax.psum(shares[6].astype(jnp.bfloat16), "ea").astype(jnp.float32),
        lax.psum(shares[7].astype(jnp.bfloat16), "ea").astype(jnp.float32),
        lax.psum(shares[8].astype(jnp.bfloat16), "ea").astype(jnp.float32),
    )
    attn_sum, query_sum, key_sum, value_sum, out_sum, qgain_sum, kgain_sum, ffn_sum, router_sum = (
        dense_grads
    )
    return (
        layer_output,
        input_grad,
        query_sum,
        key_sum,
        value_sum,
        out_sum,
        attn_sum,
        qgain_sum,
        kgain_sum,
        ffn_sum,
        router_sum,
        gate_sum,
        upw_sum,
        down_sum,
    )


def solution(mesh):
    in_specs = (
        P(("ga", "ea"), None),
        P("ga", None),
        P("ga", None),
        P("ga", None),
        P("ga", None),
        P("ga"),
        P("ga"),
        P("ga"),
        P("ga"),
        P("ga", None),
        P("ea", "ga", None),
        P("ea", "ga", None),
        P("ea", None, "ga"),
        P(("ga", "ea"), None),
        P("ga", None),
        P(("ga", "ea"), None),
    )
    out_specs = (
        P(("ga", "ea"), None),
        P(("ga", "ea"), None),
        P("ga", None),
        P("ga", None),
        P("ga", None),
        P("ga", None),
        P("ga"),
        P("ga"),
        P("ga"),
        P("ga"),
        P("ga", None),
        P("ea", "ga", None),
        P("ea", "ga", None),
        P("ea", None, "ga"),
    )
    return jax.shard_map(body, mesh=mesh, in_specs=in_specs, out_specs=out_specs, check_vma=False)
```

profile of v0, /device:TPU:1, one launch (start us, length us, event | category | flops | bytes accessed | tf_op | source)
XLA Modules:
  0.0 2618.3 jit_solution(2072668982798821161)
XLA Ops:
  29.5 17.8 all-gather.14.cloned.1.call-done
  53.0 31.6 %all-gather.18.cloned.1.call-done = bf16[2048,512]{1,0:T(8,128)(2,1)} async-done(((bf16[512,512]{1,0:T(8,128)(2,1)}), bf16[2048,512]{1,0:T(8,128)(2,1)}) %all-gather.18.cloned.1.call-update) | async-done | bytes 2097168 | tf_op jit(solution)/shard_map/all_gather | solution.py:130
  124.9 150.9 %all-gather.12.cloned.1.call-done = bf16[2048,4096]{1,0:T(8,128)(2,1)} async-done(((bf16[512,4096]{1,0:T(8,128)(2,1)}), bf16[2048,4096]{1,0:T(8,128)(2,1)}) %all-gather.12.cloned.1.call-update) | async-done | bytes 16777232 | tf_op jit(solution)/shard_map/all_gather | solution.py:128
  307.4 70.1 %while.28 = (s32[]{:T(128)}, bf16[4,256,8,128]{1,3,2,0:T(8,128)(2,1)}, f32[4,256,8]{1,2,0:T(8,128)}, bf16[4,256,8,128]{3,1,2,0:T(8,128)(2,1)}, bf16[4,2048,128]{...) while((s32[]{:T(128)}, ...), condition=%wide.region_8.9_spmd.clone, body=%wide.region_5.8_spmd.clone.sunk | while | flops 2200172544 | bytes 56700288 | solution.py:195
  377.5 88.1 %all-gather.22.cloned.1.call-done = bf16[4096,2048]{1,0:T(8,128)(2,1)} async-done(((bf16[1024,2048]{1,0:T(8,128)(2,1)}), bf16[4096,2048]{1,0:T(8,128)(2,1)}) %all-gather.22.cloned.1.call-update) | async-done | bytes 16777232 | tf_op jit(solution)/shard_map/all_gather | solution.py:131
  476.6 16.8 gather_fusion.4
  509.5 22.8 gather_fusion.2
  552.6 204.9 %all-to-all-done.2 = bf16[2,8,144,2048]{3,2,0,1:T(8,128)(2,1)} async-done(((bf16[2,8,144,2048]{3,2,0,1:T(8,128)(2,1)}), bf16[2,8,144,2048]{3,2,0,1:T(8,128)(2,1)}, u32[]{:S(2)}, u32[]{:S(2)}) %all-to-all-start.2) | async-done | bytes 9437216 | tf_op jit(solution)/shard_map/all_to_all | solution.py:245
  774.4 194.5 %all-to-all-done = bf16[2,8,144,2048]{3,2,0,1:T(8,128)(2,1)} async-done(((bf16[2,8,144,2048]{3,2,0,1:T(8,128)(2,1)}), bf16[2,8,144,2048]{3,2,0,1:T(8,128)(2,1)}, u32[]{:S(2)}, u32[]{:S(2)}) %all-to-all-start) | async-done | bytes 9437216 | tf_op jit(solution)/shard_map/all_to_all | solution.py:209
  1005.8 19.1 multiply_convert_fusion.1
  1093.5 165.7 %all-to-all-done.1 = bf16[2,8,144,2048]{3,2,0,1:T(8,128)(2,1)} async-done(((bf16[2,8,144,2048]{3,2,0,1:T(8,128)(2,1)}), bf16[2,8,144,2048]{3,2,0,1:T(8,128)(2,1)}, u32[]{:S(2)}, u32[]{:S(2)}) %all-to-all-start.1) | async-done | bytes 9437216 | tf_op jit(solution)/shard_map/all_to_all | solution.py:223
  1274.3 21.7 gather_fusion.1
  1318.2 152.5 %all-to-all-done.3 = bf16[2,8,144,2048]{3,2,0,1:T(8,128)(2,1)} async-done(((bf16[2,8,144,2048]{3,2,0,1:T(8,128)(2,1)}), bf16[2,8,144,2048]{3,2,0,1:T(8,128)(2,1)}, u32[]{:S(2)}, u32[]{:S(2)}) %all-to-all-start.3) | async-done | bytes 9437216 | tf_op jit(solution)/shard_map/all_to_all | solution.py:264
  1480.1 21.2 gather_fusion.3
  1532.7 155.3 %while.29 = (s32[]{:T(128)}, bf16[4,256,8,128]{3,1,2,0:T(8,128)(2,1)}, bf16[4,2048,128]{1,2,0:T(8,128)(2,1)}, bf16[4,2048,128]{1,2,0:T(8,128)(2,1)}, bf16[4,256,...) while((s32[]{:T(128)}, ...), condition=%wide.region_24.25_spmd.clone, body=%wide.region_22.24_spmd.clone.sunk | while | flops 5434505216 | bytes 153164240 | solution.py:329
  1688.9 30.5 %reduce-scatter.11.cloned.1.call-done = bf16[4,256,128]{1,2,0:T(8,128)(2,1)} async-done(((bf16[4,2048,128]{1,2,0:T(8,128)(2,1)}), bf16[4,256,128]{1,2,0:T(8,128)(2,1)}) %reduce-scatter.11.cloned.1.call-update) | async-done | bytes 262160 | tf_op jit(solution)/shard_map/reduce_scatter | solution.py:333
  1723.2 33.1 %reduce-scatter.13.cloned.1.call-done = bf16[4,256,128]{1,2,0:T(8,128)(2,1)} async-done(((bf16[4,2048,128]{1,2,0:T(8,128)(2,1)}), bf16[4,256,128]{1,2,0:T(8,128)(2,1)}) %reduce-scatter.13.cloned.1.call-update) | async-done | bytes 262160 | tf_op jit(solution)/shard_map/reduce_scatter | solution.py:336
  1856.6 135.4 %reduce-scatter.21.cloned.1.call-done = bf16[1024,2048]{1,0:T(8,128)(2,1)} async-done(((bf16[4096,2048]{1,0:T(8,128)(2,1)}), bf16[1024,2048]{1,0:T(8,128)(2,1)}) %reduce-scatter.21.cloned.1.call-update) | async-done | bytes 4194320 | tf_op jit(solution)/shard_map/reduce_scatter | solution.py:387
  1992.0 156.8 %reduce-scatter.15.cloned.1.call-done = bf16[512,4096]{1,0:T(8,128)(2,1)} async-done(((bf16[2048,4096]{1,0:T(8,128)(2,1)}), bf16[512,4096]{1,0:T(8,128)(2,1)}) %reduce-scatter.15.cloned.1.call-update) | async-done | bytes 4194320 | tf_op jit(solution)/shard_map/reduce_scatter | solution.py:378
  2150.1 71.8 %reduce-scatter.29.cloned.1.call-done = bf16[2,768,512]{2,1,0:T(8,128)(2,1)} async-done(((bf16[2,768,2048]{2,1,0:T(8,128)(2,1)}), bf16[2,768,512]{2,1,0:T(8,128)(2,1)}) %reduce-scatter.29.cloned.1.call-update) | async-done | bytes 1572880 | tf_op jit(solution)/shard_map/reduce_scatter | solution.py:279
  2225.4 70.1 %reduce-scatter.27.cloned.1.call-done = bf16[2,512,768]{2,1,0:T(8,128)(2,1)} async-done(((bf16[2,2048,768]{2,1,0:T(8,128)(2,1)}), bf16[2,512,768]{2,1,0:T(8,128)(2,1)}) %reduce-scatter.27.cloned.1.call-update) | async-done | bytes 1572880 | tf_op jit(solution)/shard_map/reduce_scatter | solution.py:276
  2298.9 70.4 %reduce-scatter.25.cloned.1.call-done = bf16[2,512,768]{2,1,0:T(8,128)(2,1)} async-done(((bf16[2,2048,768]{2,1,0:T(8,128)(2,1)}), bf16[2,512,768]{2,1,0:T(8,128)(2,1)}) %reduce-scatter.25.cloned.1.call-update) | async-done | bytes 1572880 | tf_op jit(solution)/shard_map/reduce_scatter | solution.py:273
  2398.2 25.8 all-reduce.10
  2430.8 165.0 %all-reduce.16.cloned.1.call-done = (bf16[512,4096]{1,0:T(8,128)(2,1)}, bf16[512,512]{1,0:T(8,128)(2,1)}, bf16[512,512]{1,0:T(8,128)(2,1)}, bf16[1024,2048]{1,0:T(8,128)(2,1)}) async-done(((bf16[512,4096]{1,0:T(8,128)(2,1)}, bf16[512,512]{1,0:T(8,128)(2,1)}, bf16[512,512]{1,0:T(8,128)(2,1)}, bf16[1024,2048]{1,0:T(8,128)(2,1)}), (bf16[512,4096]{1,0:T(8,128)(2,1)}, bf16[512,512]{1,0:T(8,128)(2,1)}, ...) | async-done | bytes 9437200 | tf_op jit(solution)/shard_map/psum | solution.py:405
  (477 shorter events, 733.0 us)
Async XLA Ops:
  7.2 40.1 %all-gather.14.cloned.1.call-start = ((), (), s32[]{:S(2)}) async-start(), calls=%async_computation.15 | async-start | bytes 2621440 | tf_op jit(solution)/shard_map/all_gather | solution.py:129
  7.9 76.6 %all-gather.18.cloned.1.call-start = ((), (), s32[]{:S(2)}) async-start(), calls=%async_computation.17 | async-start | bytes 2621440 | tf_op jit(solution)/shard_map/all_gather | solution.py:130
  8.7 112.3 %all-gather.16.cloned.1.call-start = ((), (), s32[]{:S(2)}) async-start(), calls=%async_computation.16 | async-start | bytes 2359296 | tf_op jit(solution)/shard_map/all_gather | solution.py:171
  52.3 223.5 %all-gather.12.cloned.1.call-start = ((), (), s32[]{:S(2)}) async-start(), calls=%async_computation.14 | async-start | bytes 20971520 | tf_op jit(solution)/shard_map/all_gather | solution.py:128
  52.9 254.4 %all-gather.20.cloned.1.call-start = ((), (), s32[]{:S(2)}) async-start(), calls=%async_computation.18 | async-start | bytes 2359296 | tf_op jit(solution)/shard_map/all_gather | solution.py:172
  87.7 377.9 %all-gather.22.cloned.1.call-start = ((), (), s32[]{:S(2)}) async-start(), calls=%async_computation.19 | async-start | bytes 20971520 | tf_op jit(solution)/shard_map/all_gather | solution.py:131
  546.3 211.2 %all-to-all-start.2 = ((bf16[2,8,144,2048]{3,2,0,1:T(8,128)(2,1)}), bf16[2,8,144,2048]{3,2,0,1:T(8,128)(2,1)}, u32[]{:S(2)}, u32[]{:S(2)}) async-start(bf16[2,8,144,2048]{3,2,0,1:T(8,128)(2,1)} %get-tuple-element.425), calls=%async_computation.2 | async-start | bytes 18874368 | tf_op jit(solution)/shard_map/all_to_all | solution.py:245
  551.9 426.2 %all-gather.26.cloned.1.call-start = ((), (), s32[]{:S(2)}) async-start(), calls=%async_computation.21 | async-start | bytes 7864320 | tf_op jit(solution)/shard_map/all_gather | solution.py:214
  757.5 211.5 %all-to-all-start = ((bf16[2,8,144,2048]{3,2,0,1:T(8,128)(2,1)}), bf16[2,8,144,2048]{3,2,0,1:T(8,128)(2,1)}, u32[]{:S(2)}, u32[]{:S(2)}) async-start(bf16[2,8,144,2048]{3,2,0,1:T(8,128)(2,1)} %get-tuple-element.426), calls=%async_computation | async-start | bytes 18874368 | tf_op jit(solution)/shard_map/all_to_all | solution.py:209
  763.3 228.8 %all-gather.24.cloned.1.call-start = ((), (), s32[]{:S(2)}) async-start(), calls=%async_computation.20 | async-start | bytes 7864320 | tf_op jit(solution)/shard_map/all_gather | solution.py:213
  764.0 241.8 %all-gather.28.cloned.1.call-start = ((), (), s32[]{:S(2)}) async-start(), calls=%async_computation.22 | async-start | bytes 7864320 | tf_op jit(solution)/shard_map/all_gather | solution.py:215
  1047.8 211.5 %all-to-all-start.1 = ((bf16[2,8,144,2048]{3,2,0,1:T(8,128)(2,1)}), bf16[2,8,144,2048]{3,2,0,1:T(8,128)(2,1)}, u32[]{:S(2)}, u32[]{:S(2)}) async-start(bf16[2,8,144,2048]{3,2,0,1:T(8,128)(2,1)} %copy.306), calls=%async_computation.1 | async-start | bytes 18874368 | tf_op jit(solution)/shard_map/all_to_all | solution.py:223
  1259.2 211.4 %all-to-all-start.3 = ((bf16[2,8,144,2048]{3,2,0,1:T(8,128)(2,1)}), bf16[2,8,144,2048]{3,2,0,1:T(8,128)(2,1)}, u32[]{:S(2)}, u32[]{:S(2)}) async-start(bf16[2,8,144,2048]{3,2,0,1:T(8,128)(2,1)} %copy.311), calls=%async_computation.3 | async-start | bytes 18874368 | tf_op jit(solution)/shard_map/all_to_all | solution.py:264
  1265.0 454.4 %reduce-scatter.11.cloned.1.call-start = ((), (), s32[]{:S(2)}) async-start(), calls=%async_computation.23 | async-start | bytes 2359296 | tf_op jit(solution)/shard_map/reduce_scatter | solution.py:333
  1688.2 68.1 %reduce-scatter.13.cloned.1.call-start = ((), (), s32[]{:S(2)}) async-start(), calls=%async_computation.24 | async-start | bytes 2359296 | tf_op jit(solution)/shard_map/reduce_scatter | solution.py:336
  1688.9 167.7 %reduce-scatter.17.cloned.1.call-start = ((), (), s32[]{:S(2)}) async-start(), calls=%async_computation.26 | async-start | bytes 2621440 | tf_op jit(solution)/shard_map/reduce_scatter | solution.py:381
  1723.1 133.5 %reduce-scatter.19.cloned.1.call-start = ((), (), s32[]{:S(2)}) async-start(), calls=%async_computation.27 | async-start | bytes 2621440 | tf_op jit(solution)/shard_map/reduce_scatter | solution.py:384
  1759.4 232.6 %reduce-scatter.21.cloned.1.call-start = ((), (), s32[]{:S(2)}) async-start(), calls=%async_computation.28 | async-start | bytes 20971520 | tf_op jit(solution)/shard_map/reduce_scatter | solution.py:387
  1772.3 376.5 %reduce-scatter.15.cloned.1.call-start = ((), (), s32[]{:S(2)}) async-start(), calls=%async_computation.25 | async-start | bytes 20971520 | tf_op jit(solution)/shard_map/reduce_scatter | solution.py:378
  1810.7 411.2 %reduce-scatter.29.cloned.1.call-start = ((), (), s32[]{:S(2)}) async-start(), calls=%async_computation.32 | async-start | bytes 7864320 | tf_op jit(solution)/shard_map/reduce_scatter | solution.py:279
  1825.5 470.0 %reduce-scatter.27.cloned.1.call-start = ((), (), s32[]{:S(2)}) async-start(), calls=%async_computation.31 | async-start | bytes 7864320 | tf_op jit(solution)/shard_map/reduce_scatter | solution.py:276
  1840.1 529.2 %reduce-scatter.25.cloned.1.call-start = ((), (), s32[]{:S(2)}) async-start(), calls=%async_computation.30 | async-start | bytes 7864320 | tf_op jit(solution)/shard_map/reduce_scatter | solution.py:273
  1853.9 544.3 %reduce-scatter.23.cloned.1.call-start = ((), (), s32[]{:S(2)}) async-start(), calls=%async_computation.29 | async-start | bytes 81920 | tf_op jit(solution)/shard_map/reduce_scatter | solution.py:399
  1856.3 739.4 %all-reduce.16.cloned.1.call-start = ((), (), s32[]{:S(2)}) async-start(), calls=%async_computation.33 | async-start | bytes 18874368 | tf_op jit(solution)/shard_map/psum | solution.py:405
  (96 other events, 3319.7 us)
Sparse Core Ops, SparseCore 0:
  9.9 37.4 all-gather.13
  49.2 35.3 all-gather.17
  86.7 31.2 all-gather.15
  119.7 156.0 all-gather.11
  277.8 29.4 all-gather.19
  309.0 156.5 all-gather.21
  554.5 69.9 all-gather.25
  766.0 69.9 all-gather.23
  837.9 70.0 all-gather.27
  1688.3 31.0 reduce-scatter.10
  1721.7 34.5 reduce-scatter.12
  1759.7 36.5 reduce-scatter.16
  1800.1 35.1 reduce-scatter.18
  1838.2 153.7 reduce-scatter.20
  1994.9 153.8 reduce-scatter.14
  2151.7 70.2 reduce-scatter.28
  2225.3 70.2 reduce-scatter.26
  2299.0 70.2 reduce-scatter.24
  2372.5 23.1 reduce-scatter.22
  2398.4 197.2 all-reduce.15
where the time goes:
time: 2630 us; the launch traced here: 2620 us
  waiting for transfers between devices  1750 us (67%)
  matrix products  380 us (14%)
  local copies, waits for them, and re-layouts  198 us (8%)
  other arithmetic  182 us (7%)
  blocking collectives  61.2 us (2%)
    all_to_all x1, waiting for transfers between devices, body(): lax.all_to_all(send_grads, 'ea', split_axis=1, concat_axis=1, tiled=True)  205 us
    all_to_all x1, waiting for transfers between devices, body(): lax.all_to_all(send_rows, 'ea', split_axis=1, concat_axis=1, tiled=True)  195 us
    all_to_all x1, waiting for transfers between devices, body(): lax.all_to_all(expert_out.reshape(local_experts, owner_count, capacity, m...  166 us
    psum x1, waiting for transfers between devices, body(): lax.psum(shares[1].astype(jnp.bfloat16), 'ea').astype(jnp.float32)  165 us
    reduce_scatter x1, waiting for transfers between devices, body(): lax.psum_scatter(dense_terms[1].astype(jnp.bfloat16), 'ga', scatter_dimen...  157 us
    all_to_all x1, waiting for transfers between devices, body(): lax.all_to_all(row_grad.reshape(local_experts, owner_count, capacity, mod...  152 us
    all_gather x1, waiting for transfers between devices, body(): lax.all_gather(w_query, 'ga', axis=0, tiled=True)  151 us
    reduce_scatter x1, waiting for transfers between devices, body(): lax.psum_scatter(dense_terms[4].astype(jnp.bfloat16), 'ga', scatter_dimen...  135 us
  transfers between devices with their start and end apart: 24, of which 17 were waited for; matrix products, arithmetic and copies ran while one was open for 15% of the time, Pallas kernels for 0%

commit v1 on v0

v1 whole, which is shorter than its diff:
```python
import functools

import jax
import jax.numpy as jnp
from jax import lax
from jax.experimental import pallas as pl
from jax.experimental.pallas import tpu as pltpu
from jax.sharding import Mesh
from jax.sharding import PartitionSpec as P

HEADS = 32
KV = 4
HD = 128
PIC = 256


NORM_EPS = 1e-06
ROPE_THETA = 1000000.0
MASKED_SCORE = -1e30
PRECISE = lax.Precision.HIGHEST
F32 = jnp.float32
BF16 = jnp.bfloat16
EXTRA = 128
LOG2E = 1.4426950408889634
VMEM = 56 << 20


def rms_norm(values, norm_gain):
    inverse = lax.rsqrt(jnp.mean(values * values, axis=-1, keepdims=True) + NORM_EPS)
    return values * inverse * norm_gain


def piece_ids(starts, positions):
    inside = (
        (starts[:, None] >= 0)
        & (positions[None, :] >= starts[:, None])
        & (positions[None, :] < starts[:, None] + PIC)
    )
    labels = jnp.arange(1, starts.shape[0] + 1, dtype=jnp.int32)[:, None]
    return jnp.sum(jnp.where(inside, labels, 0), axis=0)


def allowed_mask(starts, query_pos, key_pos):
    query_piece = piece_ids(starts, query_pos)
    key_piece = piece_ids(starts, key_pos)
    causal = key_pos[None, :] <= query_pos[:, None]
    shared = (query_piece[:, None] == key_piece[None, :]) & (query_piece[:, None] > 0)
    return causal | shared


def dot_nn(left, right):
    return lax.dot_general(left, right, (((1,), (0,)), ((), ())), preferred_element_type=F32)


def dot_tn(left, right):
    return lax.dot_general(left, right, (((0,), (0,)), ((), ())), preferred_element_type=F32)


def dot_nt(left, right):
    return lax.dot_general(left, right, (((1,), (1,)), ((), ())), preferred_element_type=F32)


def after(value, *others):
    return lax.optimization_barrier((value,) + others)[0]


def swap_core(value):
    return lax.ppermute(value, "core", [(0, 1), (1, 0)])


def swap_axis(value, axis, bit):
    return lax.ppermute(value, axis, [(i, i ^ bit) for i in range(lax.axis_size(axis))])


def plus(*terms):
    total = terms[0].astype(F32)
    for term in terms[1:]:
        total = total + term.astype(F32)
    return total.astype(BF16)


def line_gather(value, before=None, steps=None):
    count = lax.axis_size("z")
    place = lax.axis_index("z")
    below, above = {}, {}
    up = down = value
    for step in range(1, count):
        if before and step in before:
            up, down = lax.optimization_barrier((up, down) + tuple(before[step]))[:2]
        up = lax.ppermute(up, "z", [(p, p + 1) for p in range(step - 1, count - 1)])
        down = lax.ppermute(down, "z", [(p, p - 1) for p in range(1, count - step + 1)])
        up, down = lax.optimization_barrier((up, down))
        below[step], above[step] = up, down
        if steps is not None:
            steps.append((up, down))
    return [value] + [
        jnp.where(place >= step, below[step], above[count - step]) for step in range(1, count)
    ]


class LineSum:
    def __init__(self, slots):
        self.slots, self.done = slots, 0

    def step(self, *before):
        count = lax.axis_size("z")
        self.done += 1
        up, down = self.slots[self.done], self.slots[count - self.done]
        if self.done > 1:
            up, down = plus(up, self.held[0]), plus(down, self.held[1])
        if before:
            up, down = lax.optimization_barrier((up, down) + before)[:2]
        up = lax.ppermute(up, "z", [(p, p + 1) for p in range(self.done)])
        down = lax.ppermute(
            down, "z", [(p, p - 1) for p in range(count - 1, count - 1 - self.done, -1)]
        )
        self.held = lax.optimization_barrier((up, down))
        return self.held

    def result(self):
        while self.done < lax.axis_size("z") - 1:
            self.step()
        return plus(self.slots[0], *self.held)


def ea_gather(value, before=None):
    mine = jnp.concatenate(line_gather(value, before))
    return mine, swap_core(mine)


def core_slots(mine, other):
    got = swap_core(other)
    return [plus(mine[s], got[s]) for s in range(lax.axis_size("z"))]


def z_all_sum(value):
    return lax.psum(value, "z")


def z_all_sum_small(value):
    count = lax.axis_size("z")
    place = lax.axis_index("z")
    bits, bit = [], 1
    while bit < count:
        rows = value.shape[0] // 2
        upper = (place // bit) % 2
        keep = lax.dynamic_slice_in_dim(value, upper * rows, rows, 0)
        send = lax.dynamic_slice_in_dim(value, (1 - upper) * rows, rows, 0)
        value = plus(keep, swap_axis(send, "z", bit))
        bits.append(bit)
        bit *= 2
    for bit in reversed(bits):
        got = swap_axis(value, "z", bit)
        upper = (place // bit) % 2
        low, high = jnp.where(upper == 0, value, got), jnp.where(upper == 0, got, value)
        value = jnp.concatenate([low, high])
    return value


def ga_order():
    return lax.axis_index("ga") ^ jnp.arange(lax.axis_size("ga"))


def ga_first_hop(value):
    if lax.axis_size("ga") != 4:
        whole = lax.all_gather(value, "ga", axis=0)
        return [jnp.take(whole, ga_order(), axis=0).reshape((-1,) + value.shape[1:])]
    return [value, swap_axis(value, "ga", 1), swap_axis(value, "ga", 2)]


def ga_second_hop(first, part, parts, before):
    if len(first) == 1:
        return []
    half = first[0].shape[0] // 2
    rows = half // parts
    to_y = first[1][part * rows : (part + 1) * rows]
    to_x = first[2][half + part * rows : half + (part + 1) * rows]
    to_y, to_x = lax.optimization_barrier((to_y, to_x) + tuple(before))[:2]
    return [swap_axis(to_y, "ga", 2), swap_axis(to_x, "ga", 1)]


def shard_list(first, seconds, shape):
    if len(first) == 1:
        blocks = jnp.take(first[0].reshape((-1,) + shape), ga_order(), axis=0)
        blocks = blocks.reshape((4, -1) + shape).swapaxes(1, 2)
        blocks = blocks.reshape(4, shape[0], -1, shape[2])
        return [blocks[q] for q in range(4)], jnp.arange(4, dtype=jnp.int32)
    across = [hop[0] for hop in seconds] + [hop[1] for hop in seconds]
    blocks = first + [jnp.concatenate(across)]
    return [block.reshape(shape) for block in blocks], ga_order().astype(jnp.int32)


def ga_sum_first(value):
    if lax.axis_size("ga") != 4:
        return (value,)
    rows = value.shape[0] // 4
    half = rows // 2
    own, for_x, for_y = [value[r * rows : (r + 1) * rows] for r in range(3)]
    low = swap_axis(value[3 * rows : 3 * rows + half], "ga", 1)
    high = swap_axis(value[3 * rows + half :], "ga", 2)
    to_x = jnp.concatenate([for_x[:half], plus(for_x[half:], high)])
    to_y = jnp.concatenate([plus(for_y[:half], low), for_y[half:]])
    return own, to_x, to_y


def ga_sum_second(parts):
    if len(parts) == 1:
        return ga_sum_whole(parts[0])
    own, to_x, to_y = parts
    return plus(own, swap_axis(to_x, "ga", 1), swap_axis(to_y, "ga", 2))


def ga_sum_whole(value):
    blocks = value.reshape((lax.axis_size("ga"), -1) + value.shape[1:])
    blocks = jnp.take(blocks, ga_order(), axis=0).reshape(value.shape)
    return lax.psum_scatter(blocks, "ga", scatter_dimension=0, tiled=True)


def ga_gather_small(value):
    count = lax.axis_size("ga")
    held, bit = value[None], 1
    while bit < count:
        held = jnp.concatenate([held, swap_axis(held, "ga", bit)])
        bit *= 2
    return jnp.take(held, ga_order(), axis=0)


def sum_small(rows):
    total = rows + swap_core(rows)
    count, bit = lax.axis_size("z"), 1
    while bit < count:
        total = total + swap_axis(total, "z", bit)
        bit *= 2
    count = lax.axis_size("ga")
    total = jnp.take(total, ga_order(), axis=0)
    while count > 1:
        count //= 2
        total = total[:count] + swap_axis(total[count:], "ga", count)
    return total[0]


def core_halves(value):
    core = lax.axis_index("core")
    rows = value.shape[0] // 2
    return (
        lax.dynamic_slice_in_dim(value, core * rows, rows, 0),
        lax.dynamic_slice_in_dim(value, (1 - core) * rows, rows, 0),
    )


def dense_other(mine, other_half):
    if len(mine) == 1:
        return [swap_core(mine[0])]
    return [other_half] + [swap_core(piece) for piece in mine[1:]]


def split_cols(value, half):
    groups = lax.axis_size("ga")
    width = value.shape[1] // groups // 2
    order = ga_order()
    return jnp.concatenate(
        [
            lax.dynamic_slice_in_dim(value, (order[r] * 2 + half) * width, width, 1)
            for r in range(groups)
        ],
        axis=1,
    )


def join_cols(mine, other):
    groups = lax.axis_size("ga")
    core = lax.axis_index("core")
    width = mine.shape[1] // groups
    order = ga_order()
    parts = []
    for g in range(groups):
        a = lax.dynamic_slice_in_dim(mine, order[g] * width, width, 1)
        b = lax.dynamic_slice_in_dim(other, order[g] * width, width, 1)
        parts += [jnp.where(core == 0, a, b), jnp.where(core == 0, b, a)]
    return jnp.concatenate(parts, axis=1)


def core_sum(mine, other):
    return plus(mine, swap_core(other))


def whole_shard(share):
    core = lax.axis_index("core")
    other_share = swap_core(share)
    low = jnp.where(core == 0, share, other_share)
    high = jnp.where(core == 0, other_share, share)
    return jnp.concatenate([low, high], axis=0).astype(F32)


def cost(micros):
    return pl.CostEstimate(flops=micros * 10**9, bytes_accessed=1024, transcendentals=0)


def pieces_kernel(plan, *refs):
    acc = None
    lefts, out_ref = refs[: 1 + max(which for which, _, _ in plan)], refs[-1]
    for (which, at, size), ref in zip(plan, refs[len(lefts) : -1]):
        term = dot_nn(lefts[which][:, at : at + size], ref[...])
        acc = term if acc is None else acc + term
    out_ref[...] = acc


def pieces_matmul(lefts, piece_lists):
    plan, pieces = [], []
    for which, some in enumerate(piece_lists):
        at = 0
        for piece in some:
            plan.append((which, at, piece.shape[0]))
            pieces.append(piece)
            at += piece.shape[0]
    rows, width = lefts[0].shape[0], pieces[0].shape[1]
    tile = min(1024 if width > 4096 else 512, width)
    return pl.pallas_call(
        functools.partial(pieces_kernel, plan),
        grid=(width // tile,),
        in_specs=[pl.BlockSpec(left.shape, lambda n: (0, 0)) for left in lefts]
        + [pl.BlockSpec((piece.shape[0], tile), lambda n: (0, n)) for piece in pieces],
        out_specs=pl.BlockSpec((rows, tile), lambda n: (0, n)),
        out_shape=jax.ShapeDtypeStruct((rows, width), F32),
        compiler_params=pltpu.CompilerParams(vmem_limit_bytes=VMEM),
        cost_estimate=cost(6),
        name="dense_matmul",
    )(*lefts, *pieces)


def pieces_back_kernel(sizes, left_ref, *refs):
    n = pl.program_id(0)
    out_ref, acc = refs[-2:]

    @pl.when(n == 0)
    def _():
        acc[...] = jnp.zeros_like(acc)

    at = 0
    for ref, size in zip(refs[:-2], sizes):
        acc[:, at : at + size] += dot_nt(left_ref[...], ref[...])
        at += size

    @pl.when(n == pl.num_programs(0) - 1)
    def _():
        out_ref[...] = acc[...].astype(out_ref.dtype)


def pieces_back(left, pieces, dtype):
    rows, width = left.shape
    tile = min(512, width)
    sizes = [piece.shape[0] for piece in pieces]
    return pl.pallas_call(
        functools.partial(pieces_back_kernel, sizes),
        grid=(width // tile,),
        in_specs=[pl.BlockSpec((rows, tile), lambda n: (0, n))]
        + [pl.BlockSpec((size, tile), lambda n: (0, n)) for size in sizes],
        out_specs=pl.BlockSpec((rows, sum(sizes)), lambda n: (0, 0)),
        out_shape=jax.ShapeDtypeStruct((rows, sum(sizes)), dtype),
        scratch_shapes=[pltpu.VMEM((rows, sum(sizes)), F32)],
        compiler_params=pltpu.CompilerParams(vmem_limit_bytes=VMEM),
        cost_estimate=cost(6),
        name="dense_back",
    )(left, *pieces)


def prep_head(raw, gain, cosine, sine):
    inverse = lax.rsqrt(jnp.mean(raw * raw, axis=-1, keepdims=True) + NORM_EPS)
    scaled = raw * inverse * gain
    turned = scaled * cosine + pltpu.roll(scaled, HD // 2, 1) * sine
    return turned.astype(BF16), inverse


def head_cols(index):
    return pl.ds(pl.multiple_of(index * HD, HD), HD)


def prep_kv_kernel(raw_ref, cos_ref, sin_ref, gain_ref, out_ref):
    for h in range(KV):
        span = slice(h * HD, (h + 1) * HD)
        keys, _ = prep_head(raw_ref[:, span], gain_ref[...], cos_ref[...], sin_ref[...])
        out_ref[:, span] = keys
    out_ref[:, KV * HD :] = raw_ref[:, KV * HD :].astype(BF16)


def prep_kv(raw, cosine, sine, gain):
    rows, width = raw.shape[0], 2 * KV * HD
    whole = lambda a: pl.BlockSpec(a.shape, lambda i: (0, 0))
    return pl.pallas_call(
        prep_kv_kernel,
        grid=(1,),
        in_specs=[
            pl.BlockSpec((rows, width), lambda i: (0, raw.shape[1] // width - 1)),
            whole(cosine),
            whole(sine),
            whole(gain),
        ],
        out_specs=pl.BlockSpec((rows, width), lambda i: (0, 0)),
        out_shape=jax.ShapeDtypeStruct((rows, width), BF16),
        compiler_params=pltpu.CompilerParams(vmem_limit_bytes=VMEM),
        cost_estimate=cost(1),
        name="prep_kv",
    )(raw, cosine, sine, gain)


def head_back(raw, inverse, grad, gain, cosine, sine):
    scaled_grad = grad * cosine + pltpu.roll(grad * sine, HD // 2, 1)
    unit = raw * inverse
    gain_grad = jnp.sum(scaled_grad * unit, axis=0, keepdims=True)
    unit_grad = scaled_grad * gain
    mean = jnp.mean(unit_grad * unit, axis=-1, keepdims=True)
    return inverse * (unit_grad - unit * mean), gain_grad


def kv_back_kernel(raw_ref, grad_ref, cos_ref, sin_ref, gain_ref, out_ref, gain_grad_ref):
    total = jnp.zeros((1, HD), F32)
    for h in range(KV):
        span = slice(h * HD, (h + 1) * HD)
        raw = raw_ref[:, span]
        cosine, sine, gain = cos_ref[...], sin_ref[...], gain_ref[...]
        _, inverse = prep_head(raw, gain, cosine, sine)
        grad = grad_ref[:, 2 * h * HD : (2 * h + 1) * HD].astype(F32)
        raw_grad, gain_grad = head_back(raw, inverse, grad, gain, cosine, sine)
        out_ref[:, span] = raw_grad.astype(BF16)
        out_ref[:, (KV + h) * HD : (KV + h + 1) * HD] = grad_ref[
            :, (2 * h + 1) * HD : (2 * h + 2) * HD
        ]
        total = total + gain_grad
    gain_grad_ref[...] = jnp.broadcast_to(total, gain_grad_ref.shape)


def kv_back(raw, grad, cosine, sine, gain):
    rows, width = raw.shape[0], 2 * KV * HD
    whole = lambda a: pl.BlockSpec(a.shape, lambda i: (0, 0))
    return pl.pallas_call(
        kv_back_kernel,
        grid=(1,),
        in_specs=[
            pl.BlockSpec((rows, width), lambda i: (0, raw.shape[1] // width - 1)),
            whole(grad),
            whole(cosine),
            whole(sine),
            whole(gain),
        ],
        out_specs=[
            pl.BlockSpec((rows, width), lambda i: (0, 0)),
            pl.BlockSpec((8, HD), lambda i: (0, 0)),
        ],
        out_shape=[
            jax.ShapeDtypeStruct((rows, width), BF16),
            jax.ShapeDtypeStruct((8, HD), F32),
        ],
        compiler_params=pltpu.CompilerParams(vmem_limit_bytes=VMEM),
        cost_estimate=cost(1),
        name="kv_back",
    )(raw, grad, cosine, sine, gain)


def attend_kernel(
    place,
    raw_ref,
    key_a,
    key_b,
    value_a,
    value_b,
    bias_ref,
    cos_ref,
    sin_ref,
    gain_ref,
    mine_ref,
    other_ref,
    log_ref,
):
    half = key_a.shape[0]
    chunk = min(512, half)
    to_log2 = LOG2E * HD**-0.5
    count = raw_ref.shape[1] // HD

    def one_head(at_head, out_ref, column):
        head = place[KV + at_head]
        query, _ = prep_head(
            raw_ref[:, head_cols(head)], gain_ref[...], cos_ref[...], sin_ref[...]
        )
        total = jnp.zeros((query.shape[0], 1), F32)
        acc = jnp.zeros(query.shape, F32)
        for side, (key_ref, value_ref) in enumerate(((key_a, value_a), (key_b, value_b))):
            for at in range(0, half, chunk):
                scores = dot_nt(query, key_ref[at : at + chunk, :])
                first = side * half + at
                weights = jnp.exp2(scores * to_log2 + bias_ref[:, first : first + chunk])
                total = total + jnp.sum(weights, axis=1, keepdims=True)
                acc = acc + dot_nn(weights.astype(BF16), value_ref[at : at + chunk, :])
        out_ref[:, head_cols(column)] = (acc / total).astype(BF16)
        logs = jnp.transpose(jnp.broadcast_to(jnp.log2(total), query.shape))
        log_ref[0, pl.ds(at_head, 1), :] = logs[0:1, :]

    @pl.loop(0, count // 2)
    def _(i):
        one_head(i, mine_ref, i)
        one_head(count // 2 + i, other_ref, i)


def attend_specs(rows, group, half, tables):
    whole = lambda h, place: (0, 0)
    side = lambda first: pl.BlockSpec((half, HD), lambda h, place: (0, first + h))
    return [
        pl.BlockSpec((rows, group), lambda h, place: (0, h)),
        side(0),
        side(0),
        side(KV),
        side(KV),
    ] + [pl.BlockSpec(t.shape, whole) for t in tables]


def attend(place, raw, kv_mine, kv_other, bias, cosine, sine, gain):
    rows = raw.shape[0]
    group = HEADS * HD // KV
    half = kv_mine.shape[0]
    tables = (bias, cosine, sine, gain)
    half_spec = pl.BlockSpec((rows, group // 2), lambda h, place: (0, place[h]))
    return pl.pallas_call(
        attend_kernel,
        grid_spec=pltpu.PrefetchScalarGridSpec(
            num_scalar_prefetch=1,
            grid=(KV,),
            in_specs=attend_specs(rows, group, half, tables),
            out_specs=[
                half_spec,
                half_spec,
                pl.BlockSpec((1, HEADS // KV, rows), lambda h, place: (h, 0, 0)),
            ],
        ),
        out_shape=[
            jax.ShapeDtypeStruct((rows, HEADS * HD // 2), BF16),
            jax.ShapeDtypeStruct((rows, HEADS * HD // 2), BF16),
            jax.ShapeDtypeStruct((KV, HEADS // KV, rows), F32),
        ],
        compiler_params=pltpu.CompilerParams(vmem_limit_bytes=VMEM),
        cost_estimate=cost(18),
        name="attend",
    )(place, raw, kv_mine, kv_other, kv_mine, kv_other, *tables)


def attend_back_kernel(
    place,
    raw_ref,
    key_a,
    key_b,
    value_a,
    value_b,
    bias_ref,
    cos_ref,
    sin_ref,
    gain_ref,
    grad_mine,
    grad_other,
    out_mine,
    out_other,
    log_ref,
    raw_grad_ref,
    kv_grad_ref,
    gain_grad_ref,
    key_acc,
    value_acc,
):
    h = pl.program_id(0)
    half = key_a.shape[0]
    chunk = min(512, half)
    scale = HD**-0.5
    to_log2 = LOG2E * scale
    count = raw_ref.shape[1] // HD
    key_acc[...] = jnp.zeros_like(key_acc)
    value_acc[...] = jnp.zeros_like(value_acc)

    @pl.when(h == 0)
    def _():
        gain_grad_ref[...] = jnp.zeros_like(gain_grad_ref)

    def one_head(at_head, grad_ref, out_ref, column):
        head = place[KV + at_head]
        raw = raw_ref[:, head_cols(head)]
        cosine, sine, gain = cos_ref[...], sin_ref[...], gain_ref[...]
        query, inverse = prep_head(raw, gain, cosine, sine)
        grad = grad_ref[:, head_cols(column)]
        product = grad.astype(F32) * out_ref[:, head_cols(column)].astype(F32)
        inner = jnp.sum(jnp.transpose(product), axis=0, keepdims=True)
        logs = log_ref[0, pl.ds(at_head, 1), :]
        query_grad = jnp.zeros(query.shape, F32)
        for side, (key_ref, value_ref) in enumerate(((key_a, value_a), (key_b, value_b))):
            for at in range(0, half, chunk):
                keys = key_ref[at : at + chunk, :]
                first = side * half + at
                span = slice(first, first + chunk)
                scores = dot_nt(keys, query)
                probs = jnp.exp2(scores * to_log2 + bias_ref[span, :] - logs)
                prob_grad = dot_nt(value_ref[at : at + chunk, :], grad)
                score_grad = (probs * (prob_grad - inner)).astype(BF16)
                value_acc[span, :] += dot_nn(probs.astype(BF16), grad)
                key_acc[span, :] += dot_nn(score_grad, query)
                query_grad = query_grad + dot_tn(score_grad, keys)
        query_grad = (query_grad * scale).astype(BF16).astype(F32)
        raw_grad, gain_grad = head_back(raw, inverse, query_grad, gain, cosine, sine)
        gain_grad_ref[0:1, :] += gain_grad
        raw_grad_ref[:, head_cols(head)] = raw_grad.astype(BF16)

    @pl.loop(0, count // 2)
    def _(i):
        one_head(i, grad_mine, out_mine, i)
        one_head(count // 2 + i, grad_other, out_other, i)

    heads = kv_grad_ref.shape[1] // HD // 2
    kv_grad_ref[:, head_cols(h)] = (key_acc[...] * scale).astype(BF16)
    kv_grad_ref[:, head_cols(heads + h)] = value_acc[...].astype(BF16)


def attend_back(
    first, count, place, raw, kv_mine, kv_other, bias, cosine, sine, gain, grad, outs, logs
):
    rows = raw.shape[0]
    group = HEADS * HD // KV
    half = kv_mine.shape[0]
    tables = (bias, cosine, sine, gain)
    half_spec = pl.BlockSpec((rows, group // 2), lambda h, place: (0, place[first + h]))
    other_spec = pl.BlockSpec((rows, group // 2), lambda h, place: (0, KV + place[first + h]))
    whole = lambda h, place: (0, 0)
    side = lambda at: pl.BlockSpec((half, HD), lambda h, place: (0, at + first + h))
    return pl.pallas_call(
        attend_back_kernel,
        grid_spec=pltpu.PrefetchScalarGridSpec(
            num_scalar_prefetch=1,
            grid=(count,),
            in_specs=[
                pl.BlockSpec((rows, group), lambda h, place: (0, first + h)),
                side(0),
                side(0),
                side(KV),
                side(KV),
            ]
            + [pl.BlockSpec(t.shape, whole) for t in tables]
            + [half_spec, other_spec, half_spec, half_spec]
            + [pl.BlockSpec((1,) + logs.shape[1:], lambda h, place: (first + h, 0, 0))],
            out_specs=[
                pl.BlockSpec((rows, group), lambda h, place: (0, h)),
                pl.BlockSpec((2 * half, 2 * count * HD), whole),
                pl.BlockSpec((8, HD), whole),
            ],
            scratch_shapes=[pltpu.VMEM((2 * half, HD), F32), pltpu.VMEM((2 * half, HD), F32)],
        ),
        out_shape=[
            jax.ShapeDtypeStruct((rows, count * group), BF16),
            jax.ShapeDtypeStruct((2 * half, 2 * count * HD), BF16),
            jax.ShapeDtypeStruct((8, HD), F32),
        ],
        compiler_params=pltpu.CompilerParams(vmem_limit_bytes=VMEM),
        cost_estimate=cost(9),
        name="attend_back",
    )(place, raw, kv_mine, kv_other, kv_mine, kv_other, *tables, grad, grad, *outs, logs)


def pick_rows(spot_row, cap):
    places = lax.broadcasted_iota(jnp.int32, (cap, spot_row.shape[1]), 0)
    return jnp.where(places == spot_row, 1.0, 0.0).astype(BF16)


def put_rows(spot_col, cap):
    places = lax.broadcasted_iota(jnp.int32, (spot_col.shape[0], cap), 1)
    return jnp.where(places == spot_col, 1.0, 0.0).astype(BF16)


def pick_kernel(cap, rows_ref, spot_ref, out_ref):
    block = spot_ref.shape[2]
    for e in range(spot_ref.shape[0]):
        for b in range(spot_ref.shape[1]):
            pick = pick_rows(spot_ref[e, b : b + 1, :], cap)
            rows = rows_ref[b * block : (b + 1) * block, :]
            out_ref[e, b * cap : (b + 1) * cap, :] = dot_nn(pick, rows).astype(BF16)


def pick(rows, spots, cap, width):
    experts, blocks, block = spots.shape
    tile = min(512, width)
    return pl.pallas_call(
        functools.partial(pick_kernel, cap),
        grid=(width // tile,),
        in_specs=[
            pl.BlockSpec((blocks * block, tile), lambda n: (0, n)),
            pl.BlockSpec(spots.shape, lambda n: (0, 0, 0)),
        ],
        out_specs=pl.BlockSpec((experts, blocks * cap, tile), lambda n: (0, 0, n)),
        out_shape=jax.ShapeDtypeStruct((experts, blocks * cap, width), BF16),
        compiler_params=pltpu.CompilerParams(vmem_limit_bytes=VMEM),
        cost_estimate=cost(3),
        name="pick",
    )(rows, spots)


def expert_kernel(
    cap,
    first_ref,
    rows_ref,
    spot_ref,
    mark_ref,
    cot_ref,
    router_ref,
    *refs,
):
    weight_refs = refs[:-5]
    row_out, act_out, pre_out, extra_out, acc = refs[-5:]
    _, depth, all_ff = weight_refs[0].shape
    ff = all_ff // 3
    experts = first_ref[1]
    block = spot_ref.shape[2]
    blocks = spot_ref.shape[1]
    marks = []
    for b in range(blocks):
        pick = pick_rows(spot_ref[0, b : b + 1, :], cap)
        span = slice(b * block, (b + 1) * block)
        row_out[0, b * cap : (b + 1) * cap, :] = dot_nn(pick, rows_ref[span, :]).astype(BF16)
        marks.append(dot_nn(pick, mark_ref[span, :]))
    marked = jnp.concatenate(marks, axis=0) > 0.5
    rows = row_out[0]
    logits = dot_nn(rows, router_ref[...])
    peak = jnp.max(jnp.where(marked, logits, MASKED_SCORE), axis=1, keepdims=True)
    weights = jnp.where(marked, jnp.exp(jnp.where(marked, logits - peak, 0.0)), 0.0)
    lanes = lax.broadcasted_iota(jnp.int32, weights.shape, 1)
    own = first_ref[0] + pl.program_id(0)
    total = jnp.sum(weights, axis=1, keepdims=True)
    gate = jnp.sum(jnp.where(lanes == own, weights, 0.0), axis=1, keepdims=True)
    gate = gate / jnp.where(total > 0.0, total, 1.0)
    for r, ref in enumerate(weight_refs):
        cols = pl.ds(pl.multiple_of(first_ref[2 + r] * depth, depth), depth)
        for left, span in ((row_out, slice(2 * ff)), (cot_ref, slice(2 * ff, all_ff))):
            term = dot_nn(left[0, :, cols], ref[0, :, span])
            if r == 0:
                acc[:, span] = term
            else:
                acc[:, span] += term
    act_grad = acc[:, 2 * ff :]
    gate_pre, up_pre = acc[:, :ff], acc[:, ff : 2 * ff]
    sig = 1.0 / (1.0 + jnp.exp(-gate_pre))
    silu = gate_pre * sig
    act = silu * up_pre
    gate_grad = jnp.sum(act * act_grad, axis=1, keepdims=True)
    act_grad = act_grad * gate
    act_out[0] = (act * gate).astype(BF16)
    slope = sig * (1.0 + gate_pre * (1.0 - sig))
    pre_out[0, :, :ff] = (act_grad * up_pre * slope).astype(BF16)
    pre_out[0, :, ff:] = (act_grad * silu).astype(BF16)
    high = gate_grad.astype(BF16).astype(F32)
    low = gate_grad - high
    extra = jnp.where(lanes == own, high, jnp.where(lanes == own + experts, low, 0.0))
    extra_out[0] = extra.astype(BF16)


def expert_rows(first, rows, spots, marks, cot_rows, router, weights, cap):
    experts, blocks, block = spots.shape
    depth, all_ff = weights[0].shape[1:]
    both = all_ff // 3 * 2
    width = rows.shape[1]
    count = blocks * cap
    one = lambda *shape: pl.BlockSpec((1,) + shape, lambda e, first: (e,) + (0,) * len(shape))
    whole = lambda a: pl.BlockSpec(a.shape, lambda e, first: (0, 0))
    return pl.pallas_call(
        functools.partial(expert_kernel, cap),
        grid_spec=pltpu.PrefetchScalarGridSpec(
            num_scalar_prefetch=1,
            grid=(experts,),
            in_specs=[
                whole(rows),
                one(blocks, block),
                whole(marks),
                one(count, width),
                whole(router),
            ]
            + [one(depth, all_ff)] * len(weights),
            out_specs=[
                one(count, width),
                one(count, both // 2),
                one(count, both),
                one(count, EXTRA),
            ],
            scratch_shapes=[pltpu.VMEM((count, all_ff), F32)],
        ),
        out_shape=[
            jax.ShapeDtypeStruct((experts, count, width), BF16),
            jax.ShapeDtypeStruct((experts, count, both // 2), BF16),
            jax.ShapeDtypeStruct((experts, count, both), BF16),
            jax.ShapeDtypeStruct((experts, count, EXTRA), BF16),
        ],
        compiler_params=pltpu.CompilerParams(vmem_limit_bytes=VMEM),
        cost_estimate=cost(11),
        name="expert_rows",
    )(first, rows, spots, marks, cot_rows, router, *weights)


def rows_back_kernel(cap, order, left_ref, spot_ref, *refs):
    out_ref, acc = refs[-2:]
    e = pl.program_id(0)
    blocks, block, wide = out_ref.shape
    weight_refs = refs[: order.shape[0]]
    depth = weight_refs[0].shape[1]

    @pl.when(e == 0)
    def _():
        acc[...] = jnp.zeros_like(acc)

    lane = lax.broadcasted_iota(jnp.int32, spot_ref.shape, 1)
    spot = jnp.sum(jnp.where(lane == e, spot_ref[...], 0), axis=1, keepdims=True)
    puts = [put_rows(spot[b * block : (b + 1) * block], cap) for b in range(blocks)]
    for r, ref in enumerate(weight_refs):
        cols = pl.ds(pl.multiple_of(order[r] * depth, depth), depth)
        rows = dot_nt(left_ref[0], ref[0]).astype(BF16)
        for b in range(blocks):
            acc[b * block : (b + 1) * block, cols] += dot_nn(
                puts[b], rows[b * cap : (b + 1) * cap, :]
            )
    if len(refs) > order.shape[0] + 2:
        extra_ref = refs[order.shape[0]]
        for b in range(blocks):
            acc[b * block : (b + 1) * block, wide - EXTRA :] += dot_nn(
                puts[b], extra_ref[0, b * cap : (b + 1) * cap, :]
            )

    @pl.when(e == pl.num_programs(0) - 1)
    def _():
        out_ref[...] = acc[...].astype(BF16).reshape(out_ref.shape)


def rows_back(order, left, weights, at, spot_cols, cap, extra=None):
    experts, count, size = left.shape
    depth = weights[0].shape[1]
    blocks = count // cap
    block = spot_cols.shape[0] // blocks
    width = depth * len(weights) + (0 if extra is None else EXTRA)
    shape = (blocks, block, width)
    one = lambda *shape: pl.BlockSpec((1,) + shape, lambda e, order: (e,) + (0,) * len(shape))
    extras = [] if extra is None else [extra]
    return pl.pallas_call(
        functools.partial(rows_back_kernel, cap),
        grid_spec=pltpu.PrefetchScalarGridSpec(
            num_scalar_prefetch=1,
            grid=(experts,),
            in_specs=[one(count, size), pl.BlockSpec(spot_cols.shape, lambda e, order: (0, 0))]
            + [pl.BlockSpec((1, depth, size), lambda e, order: (e, 0, at))] * len(weights)
            + [one(count, EXTRA)] * len(extras),
            out_specs=pl.BlockSpec(shape, lambda e, order: (0, 0, 0)),
            scratch_shapes=[pltpu.VMEM((blocks * block, width), F32)],
        ),
        out_shape=jax.ShapeDtypeStruct(shape, BF16),
        compiler_params=pltpu.CompilerParams(vmem_limit_bytes=VMEM),
        cost_estimate=cost(5 if extra is None else 10),
        name="mixtures" if extra is None else "row_grads",
    )(order, left, spot_cols, *weights, *extras)


def expert_grad_kernel(row_a, row_b, cot_a, cot_b, pre_a, pre_b, act_a, act_b, out_ref):
    both = pre_a.shape[2]
    total = dot_tn(row_a[0], pre_a[0]) + dot_tn(row_b[0], pre_b[0])
    out_ref[0, 0, :, :both] = total.astype(BF16)
    total = dot_tn(cot_a[0], act_a[0]) + dot_tn(cot_b[0], act_b[0])
    out_ref[0, 0, :, both:] = total.astype(BF16)


def expert_grads(rows, cots, pres, acts, shards):
    experts, count, width = rows[0].shape
    both, ff = pres[0].shape[2], acts[0].shape[2]
    depth = width // shards
    part = pl.BlockSpec((1, count, depth), lambda e, n: (e, 0, n))
    full = lambda size: pl.BlockSpec((1, count, size), lambda e, n: (e, 0, 0))
    return pl.pallas_call(
        expert_grad_kernel,
        grid=(experts, shards),
        in_specs=[part] * 4 + [full(both)] * 2 + [full(ff)] * 2,
        out_specs=pl.BlockSpec((1, 1, depth, both + ff), lambda e, n: (n, e, 0, 0)),
        out_shape=jax.ShapeDtypeStruct((shards, experts, depth, both + ff), BF16),
        compiler_params=pltpu.CompilerParams(vmem_limit_bytes=VMEM),
        cost_estimate=cost(18),
        name="expert_grads",
    )(rows[0], rows[1], cots[0], cots[1], pres[0], pres[1], acts[0], acts[1])


def body(
    layer_input,
    w_query,
    w_key,
    w_value,
    w_out,
    attn_gain,
    query_gain,
    key_gain,
    ffn_gain,
    w_router,
    w_gate,
    w_up,
    w_down,
    routes,
    pic_starts,
    cotangent,
):
    tok_count, model_width = layer_input.shape
    top_count = routes.shape[1]
    ga_count = lax.axis_size("ga")
    z_count = lax.axis_size("z")
    ea_count = 2 * z_count
    core = lax.axis_index("core")
    chip = lax.axis_index("z")
    local_experts, _, ff = w_gate.shape
    expert_total = local_experts * ea_count
    cap = max(2, 9 * tok_count * top_count // (8 * expert_total))
    group_size = HEADS // KV
    kv_width = KV * HD
    q_width = HEADS * HD

    small = [attn_gain, query_gain, key_gain, ffn_gain, w_router.reshape(-1)]
    small_all = ga_gather_small(jnp.concatenate(small))
    at, smalls = 0, []
    for piece in small:
        smalls.append(small_all[:, at : at + piece.shape[0]].reshape(-1))
        at += piece.shape[0]
    attn_gain_f, query_gain_f, key_gain_f, ffn_gain_f = [s.astype(F32) for s in smalls[:4]]
    router_full = smalls[4].reshape(model_width, expert_total)
    router_wide = jnp.pad(router_full, ((0, 0), (0, EXTRA - expert_total)))

    qkv_weights = (w_query, w_key, w_value)
    qkv_own = jnp.concatenate([core_halves(w)[0] for w in qkv_weights], axis=1)

    marks = jnp.sum(
        (routes[:, :, None] == jnp.arange(EXTRA, dtype=jnp.int32)[None, None, :]).astype(F32), axis=1
    )
    cot_steps = []
    qkv_first = ga_first_hop(after(qkv_own, small_all))
    cot_mine = line_gather(
        after(jnp.concatenate([cotangent, marks.astype(BF16)], axis=1), small_all), steps=cot_steps
    )
    qkv_twin = jnp.concatenate(
        [core_halves(after(w, *cot_steps[0]))[1] for w in qkv_weights], axis=1
    )
    qkv_second = ga_second_hop(qkv_first, 0, 1, cot_steps[1])
    qkv_mine = qkv_first + qkv_second
    qkv_other = dense_other(qkv_mine, qkv_twin)
    cot_mine = after(jnp.concatenate(cot_mine), *qkv_second)
    cot_sides = [cot_mine, swap_core(cot_mine)]
    first_expert = (chip * 2 + core) * local_experts
    mark_sides, spot_rows, spot_cols, cot_rows = [], [], [], []
    before = jnp.tril(jnp.ones((tok_count, tok_count), BF16))
    for side in cot_sides:
        side_marks = side[:, model_width:]
        chosen = lax.dynamic_slice_in_dim(side_marks, first_expert, local_experts, 1)
        chosen = chosen.reshape(z_count, tok_count, local_experts)
        rank = jnp.einsum("ts,bse->bte", before, chosen, preferred_element_type=F32)
        spots = jnp.where(chosen > 0, rank - 1.0, -1.0).astype(jnp.int32)
        mark_sides.append(side_marks)
        spot_rows.append(jnp.transpose(spots, (2, 0, 1)))
        spot_cols.append(spots.reshape(z_count * tok_count, local_experts))
        cot_rows.append(pick(side, spot_rows[-1], cap, model_width))

    ea_index = chip * 2 + core
    positions = ea_index * tok_count + jnp.arange(tok_count, dtype=jnp.int32)
    holder = ((chip - jnp.arange(z_count)) % z_count * 2)[None, :] + jnp.stack([core, 1 - core])[
        :, None
    ]
    key_pos = (holder.reshape(-1, 1) * tok_count + jnp.arange(tok_count)[None, :]).reshape(-1)
    key_pos = key_pos.astype(jnp.int32)
    allowed = allowed_mask(pic_starts[0], positions, key_pos)
    bias = jnp.where(allowed, 0.0, MASKED_SCORE).astype(F32)
    bias_turned = jnp.where(jnp.transpose(allowed), 0.0, MASKED_SCORE).astype(F32)
    frequency = ROPE_THETA ** (-jnp.arange(HD // 2, dtype=F32) * 2.0 / HD)
    angles = positions.astype(F32)[:, None] * frequency[None, :]
    cosine = jnp.concatenate([jnp.cos(angles), jnp.cos(angles)], axis=1)
    sine = jnp.concatenate([-jnp.sin(angles), jnp.sin(angles)], axis=1)
    per_key = max(1, ga_count // KV)
    ga_index = lax.axis_index("ga")
    run = group_size // 2 // per_key
    step = jnp.arange(per_key) ^ (ga_index % per_key)
    own_heads = (step[:, None] * 2 * run + jnp.arange(run)[None, :]).reshape(-1)
    key_place = jnp.arange(KV) ^ (ga_index // per_key)
    place = jnp.concatenate(
        [key_place, own_heads + core * run, own_heads + (1 - core) * run]
    ).astype(jnp.int32)

    input_f = layer_input.astype(F32)
    normed = rms_norm(input_f, attn_gain_f).astype(BF16)
    normed_mine = split_cols(normed, core)
    normed_other = split_cols(normed, 1 - core)
    normed_used = after(normed_mine, bias, bias_turned, cosine, sine)
    qkv = pieces_matmul((normed_used, normed_other), (qkv_mine, qkv_other))
    query_gain_row, key_gain_row = query_gain_f.reshape(1, HD), key_gain_f.reshape(1, HD)
    kv_own = prep_kv(qkv, cosine, sine, key_gain_row)

    out_own, out_twin = core_halves(w_out)
    out_first = ga_first_hop(after(out_own, *qkv_second))
    kv_mine, kv_other = ea_gather(kv_own, {2: cot_rows[:1], 3: cot_rows[1:] + out_first[1:]})
    out_mine = out_first + ga_second_hop(out_first, 0, 1, ())
    expert_own = jnp.concatenate([w_gate, w_up, jnp.swapaxes(w_down, 1, 2)], axis=2)
    expert_flat = expert_own.reshape(-1, 3 * ff)
    expert_gather = ga_first_hop(after(expert_flat, *out_first[1:]))

    att_mine, att_other, log_rows = attend(
        place,
        qkv,
        kv_mine,
        kv_other,
        bias,
        cosine,
        sine,
        query_gain_row,
    )
    out_other = dense_other(out_first + [after(p, att_mine) for p in out_mine[3:]], out_twin)
    hidden = input_f + pieces_matmul((att_mine, att_other), (out_mine, out_other))
    ffn_in = rms_norm(hidden, ffn_gain_f).astype(BF16)

    row_slots = line_gather(ffn_in, {3: expert_gather[1:]})
    hops = [ga_second_hop(expert_gather, 0, 2, ())]
    row_mine = after(jnp.concatenate(row_slots), *hops[0])
    row_sides = [row_mine, swap_core(row_mine)]
    hops.append(ga_second_hop(expert_gather, 1, 2, hops[0]))
    expert_all, order = shard_list(expert_gather, hops, expert_own.shape)
    logits = dot_nn(ffn_in, router_full)
    own_marks = marks[:, :expert_total] > 0
    peak = jnp.max(jnp.where(own_marks, logits, MASKED_SCORE), axis=1, keepdims=True)
    weights = jnp.exp(jnp.where(own_marks, logits - peak, MASKED_SCORE))
    gates = weights / jnp.sum(weights, axis=1, keepdims=True)

    first = jnp.concatenate([jnp.stack([first_expert, expert_total]).astype(jnp.int32), order])
    picked, acts, pres, extras = [], [], [], []
    for side in range(2):
        rows, act, pre, extra = expert_rows(
            first,
            row_sides[side],
            spot_rows[side],
            mark_sides[side],
            cot_rows[side],
            router_wide,
            expert_all,
            cap,
        )
        picked.append(rows)
        acts.append(act)
        pres.append(pre)
        extras.append(extra)
    expert_grad = expert_grads(picked, cot_rows, pres, acts, ga_count)
    expert_sum = lax.psum_scatter(expert_grad, "ga", scatter_dimension=0)
    row_other = rows_back(
        order, after(pres[1], expert_grad), expert_all, 0, spot_cols[1], cap, extras[1]
    )
    row_mine = rows_back(
        order, after(pres[0], row_other), expert_all, 0, spot_cols[0], cap, extras[0]
    )
    rows = LineSum(core_slots(row_mine, row_other))
    rows.step()
    mix_other = rows_back(order, after(acts[1], rows.slots[1]), expert_all, 2, spot_cols[1], cap)
    rows.step(mix_other)
    mix_mine = rows_back(order, after(acts[0], *rows.held), expert_all, 2, spot_cols[0], cap)
    rows.step(mix_mine)
    row_sum = rows.result()

    grad_out = cotangent.astype(F32)
    gate_grad = (
        row_sum[:, model_width : model_width + expert_total].astype(F32)
        + row_sum[:, model_width + expert_total : model_width + 2 * expert_total].astype(F32)
    )
    inner = jnp.sum(gates * gate_grad, axis=1, keepdims=True)
    logit_grad = gates * (gate_grad - inner)
    router_grad = lax.dot_general(
        ffn_in.astype(F32), logit_grad, (((0,), (0,)), ((), ())), precision=PRECISE
    )
    ffn_in_grad = row_sum[:, :model_width].astype(F32) + jnp.dot(
        logit_grad, router_full.astype(F32).T, precision=PRECISE
    )
    unused, ffn_back = jax.vjp(rms_norm, hidden, ffn_gain_f)
    hidden_part, ffn_gain_grad = ffn_back(ffn_in_grad)
    hidden_grad = grad_out + hidden_part
    branch_grad = hidden_grad.astype(BF16)
    out_terms = [dot_tn(a, branch_grad) for a in (att_mine, att_other)]
    out_terms[1] = out_terms[1].astype(BF16)
    att_grads = pieces_back(after(branch_grad, out_terms[1]), out_mine + out_other, BF16)
    raw_grads, kv_grads, gain_grads = [], [], []

    def back(head, *before):
        raw_grad, kv_grad, gain_grad = attend_back(
            head,
            1,
            place,
            qkv,
            kv_mine,
            kv_other,
            bias_turned,
            cosine,
            sine,
            query_gain_row,
            after(att_grads, *before),
            (att_mine, att_other),
            log_rows,
        )
        raw_grads.append(raw_grad)
        kv_grads.append(kv_grad)
        gain_grads.append(gain_grad[0])

    def weight_terms(grad):
        return dot_tn(normed_mine, grad), dot_tn(normed_other, grad).astype(BF16)

    mix = LineSum(core_slots(mix_mine, after(mix_other, out_terms[1])))
    held = [mix.step()]
    back(0, mix.slots[1], expert_sum)
    held.append(mix.step(raw_grads[0]))
    out_total = core_sum(*out_terms)
    out_share = ga_sum_whole(out_total)
    back(1, raw_grads[0], out_total, *held[0])
    held.append(mix.step(raw_grads[1]))
    back(2, raw_grads[1], *held[1])
    back(3, raw_grads[2], *held[2])
    mix_sum = mix.result()
    layer_output = (hidden + mix_sum.astype(F32)).astype(BF16)
    query_raw_grad = jnp.concatenate(raw_grads, axis=1)
    query_terms = weight_terms(query_raw_grad)
    query_gain_grad = sum(gain_grads)
    kv_grad = after(jnp.concatenate(kv_grads, axis=1), mix_sum)
    kv_grad = kv_grad.reshape(2, z_count, tok_count, 2 * kv_width)
    keys_values = LineSum(core_slots(kv_grad[0], kv_grad[1]))
    keys_values.step(query_terms[1])
    query_total = core_sum(*query_terms)
    keys_values.step(query_total)
    query_first = ga_sum_first(query_total)
    keys_values.step(out_share)
    kv_raw_grad, key_gain_grad = kv_back(
        qkv, after(keys_values.result(), *query_first), cosine, sine, key_gain_row
    )
    key_gain_grad = key_gain_grad[0]
    out_all = z_all_sum(out_share)
    query_share = ga_sum_second(query_first)
    kv_total = core_sum(*weight_terms(kv_raw_grad))
    kv_share = ga_sum_second(ga_sum_first(after(kv_total, query_share)))
    query_all = z_all_sum(after(query_share, out_all))
    out_sum, query_sum = whole_shard(out_all), whole_shard(query_all)
    kv_sum = whole_shard(z_all_sum_small(kv_share))
    key_sum, value_sum = kv_sum[:, :kv_width], kv_sum[:, kv_width:]
    chunks = [query_raw_grad, kv_raw_grad]
    qkv_grad = jnp.concatenate(chunks, axis=1)
    both_grads = pieces_back(qkv_grad, qkv_mine + qkv_other, F32)
    half_width = model_width // 2
    normed_grad = join_cols(both_grads[:, :half_width], both_grads[:, half_width:])
    unused, attn_back = jax.vjp(rms_norm, input_f, attn_gain_f)
    input_part, attn_gain_grad = attn_back(normed_grad)
    input_grad = (hidden_grad + input_part).astype(BF16)

    tiny = [attn_gain_grad, query_gain_grad, key_gain_grad, ffn_gain_grad, router_grad.reshape(-1)]
    tiny_own = sum_small(jnp.concatenate([t.reshape(ga_count, -1) for t in tiny], axis=1))
    at, tiny_sums = 0, []
    for piece in tiny:
        width = piece.shape[0] // ga_count
        tiny_sums.append(tiny_own[at : at + width])
        at += width
    attn_sum, qgain_sum, kgain_sum, ffn_sum, router_sum = tiny_sums
    return (
        layer_output,
        input_grad,
        query_sum,
        key_sum,
        value_sum,
        out_sum,
        attn_sum,
        qgain_sum,
        kgain_sum,
        ffn_sum,
        router_sum.reshape(-1, expert_total),
        expert_sum[:, :, :ff].astype(F32),
        expert_sum[:, :, ff : 2 * ff].astype(F32),
        jnp.swapaxes(expert_sum[:, :, 2 * ff :], 1, 2).astype(F32),
    )


def solution(mesh):
    ga_count, ea_count = mesh.shape["ga"], mesh.shape["ea"]
    inner = Mesh(mesh.devices.reshape(ga_count, ea_count // 2, 2), ("ga", "z", "core"))
    everyone = ("ga", "z", "core")
    owners = ("z", "core")
    in_specs = (
        P(everyone, None),
        P("ga", None),
        P("ga", None),
        P("ga", None),
        P("ga", None),
        P("ga"),
        P("ga"),
        P("ga"),
        P("ga"),
        P("ga", None),
        P(owners, "ga", None),
        P(owners, "ga", None),
        P(owners, None, "ga"),
        P(everyone, None),
        P("ga", None),
        P(everyone, None),
    )
    out_specs = (
        P(everyone, None),
        P(everyone, None),
        P("ga", None),
        P("ga", None),
        P("ga", None),
        P("ga", None),
        P("ga"),
        P("ga"),
        P("ga"),
        P("ga"),
        P("ga", None),
        P(owners, "ga", None),
        P(owners, "ga", None),
        P(owners, None, "ga"),
    )
    return jax.shard_map(body, mesh=inner, in_specs=in_specs, out_specs=out_specs, check_vma=False)
```

time: 2630 us -> 1230 us (0.47)
  waiting for transfers between devices: 1750 us -> 481 us
  matrix products: 380 us -> 34.6 us
  Pallas kernels: 0 us -> 329 us
  starting transfers between devices: 23.9 us -> 134 us
  local copies, waits for them, and re-layouts: 198 us -> 89.4 us
  blocking collectives: 61.2 us -> 0 us
  other arithmetic: 182 us -> 133 us
    all_to_all x4 -> x0, waiting for transfers between devices: 718 us -> none  [the longest x1 205 us: body(): lax.all_to_all(send_grads, 'ea', split_axis=1, concat_axis=1, tiled=True)]
    reduce_scatter x10 -> x1, waiting for transfers between devices: 568 us -> 0.01 us  [ga_sum_whole(): return lax.psum_scatter(blocks, 'ga', scatter_dimension=0, tiled=True)]
    ppermute x0 -> x89, waiting for transfers between devices: none -> 363 us  [the longest x32 117 us: swap_axis(): lax.ppermute(value, axis, [(i, i ^ bit) for i in range(lax.axis_size(axis...]
    dot_general x54 -> x11, matrix products: 380 us -> 34.6 us  [the longest x6 26.9 us: dot_tn(): lax.dot_general(left, right, (((0,), (0,)), ((), ())), preferred_element_...]
    pallas_call x0 -> x20, Pallas kernels: none -> 329 us  [the longest x4 73.1 us: attend_back(): pl.pallas_call(attend_back_kernel, grid_spec=pltpu.PrefetchScalarGridSpec...]
    all_gather x9 -> x0, waiting for transfers between devices: 298 us -> none  [the longest x1 151 us: body(): lax.all_gather(w_query, 'ga', axis=0, tiled=True)]
    ppermute x0 -> x89, starting transfers between devices: none -> 133 us  [the longest x9 42.3 us: step(): up = lax.ppermute(up, 'z', [(p, p + 1) for p in range(self.done)])]
    gather x9 -> x5, local copies, waits for them, and re-layouts: 93.2 us -> 15.5 us  [the longest x3 14.1 us: ga_sum_whole(): blocks = jnp.take(blocks, ga_order(), axis=0).reshape(value.shape)]
  transfers between devices with their start and end apart: 24 -> 93, of which waited for: 17 -> 41; matrix products, arithmetic and copies ran while one was open for 15% -> 19% of each run, Pallas kernels for 0% -> 22%
where the time goes in v1:
time: 1230 us; the launch traced here: 1220 us
  waiting for transfers between devices  481 us (39%)
  Pallas kernels  329 us (27%)
  starting transfers between devices  134 us (11%)
  other arithmetic  133 us (11%)
  local copies, waits for them, and re-layouts  89.4 us (7%)
  matrix products  34.6 us (3%)
  between operations  21.1 us (2%)
    psum x2, waiting for transfers between devices, z_all_sum(): return lax.psum(value, 'z')  117 us
    ppermute x32, waiting for transfers between devices, swap_axis(): lax.ppermute(value, axis, [(i, i ^ bit) for i in range(lax.axis_size(axis...  117 us
    ppermute x9, waiting for transfers between devices, line_gather(): lax.ppermute(down, 'z', [(p, p - 1) for p in range(1, count - step + 1)])  89 us
    ppermute x9, waiting for transfers between devices, step(): up = lax.ppermute(up, 'z', [(p, p + 1) for p in range(self.done)])  76.9 us
    pallas_call x4, Pallas kernels, attend_back(): pl.pallas_call(attend_back_kernel, grid_spec=pltpu.PrefetchScalarGridSpec...  73.1 us
    pallas_call x4, Pallas kernels, rows_back(): pl.pallas_call(functools.partial(rows_back_kernel, cap), grid_spec=pltpu....  64.3 us
    pallas_call x2, Pallas kernels, expert_rows(): pl.pallas_call(functools.partial(expert_kernel, cap), grid_spec=pltpu.Pre...  50.4 us
    ppermute x9, starting transfers between devices, step(): up = lax.ppermute(up, 'z', [(p, p + 1) for p in range(self.done)])  42.3 us
  transfers between devices with their start and end apart: 93, of which 41 were waited for; matrix products, arithmetic and copies ran while one was open for 19% of the time, Pallas kernels for 22%

profile of v1, /device:TPU:1, one launch (start us, length us, event | category | flops | bytes accessed | tf_op | source)
XLA Modules:
  0.0 1221.4 jit_solution(11365479748776844837)
XLA Ops:
  34.4 17.4 %collective-permute-done.4 = bf16[256,2176]{1,0:T(8,128)(2,1)S(1)} collective-permute-done((bf16[256,2176]{1,0:T(8,128)(2,1)}, bf16[256,2176]{1,0:T(8,128)(2,1)S(1)}, u32[]{:S(2)}, u32[]{:S(2)}) %collective-permute-start.4) | collective-permute-done | bytes 1114144 | tf_op jit(solution)/shard_map/ppermute | solution.py:90
  62.4 21.2 %collective-permute-done.7 = bf16[256,2176]{1,0:T(8,128)(2,1)S(1)} collective-permute-done((bf16[256,2176]{1,0:T(8,128)(2,1)S(1)}, bf16[256,2176]{1,0:T(8,128)(2,1)S(1)}, u32[]{:S(2)}, u32[]{:S(2)}) %collective-permute-start.7) | collective-permute-done | bytes 1114144 | tf_op jit(solution)/shard_map/ppermute | solution.py:91
  230.2 36.6 %attend.1 = (bf16[256,2048]{1,0:T(8,128)(2,1)}, bf16[256,2048]{1,0:T(8,128)(2,1)}, f32[4,8,256]{2,1,0:T(8,128)}) custom-call(s32[12]{0:T(128)} %pad_add_fusion.place, f32[256,5120]{1,0:T(8,128)} %dense_matmul.2.raw_ref, bf16[1024,1024]{1,0:T(8,128)(2,1)} %pad_maximum_fusion.8.key_a.value_a, bf16[1024,1024]{1,0:T(8,128)(2,1)} %collective-permute-done.25.key_b.value_b, ...), custom_call_target="tpu_custom_call" | custom-call | flops 17999998976 | bytes 1024 | tf_op jit(solution)/shard_map/attend/pallas_call | solution.py:521
  287.9 21.1 %collective-permute-done.32 = bf16[256,2048]{1,0:T(8,128)(2,1)S(1)} collective-permute-done((bf16[256,2048]{1,0:T(8,128)(2,1)S(1)}, bf16[256,2048]{1,0:T(8,128)(2,1)S(1)}, u32[]{:S(2)}, u32[]{:S(2)}) %collective-permute-start.32) | collective-permute-done | bytes 1048608 | tf_op jit(solution)/shard_map/ppermute | solution.py:90
  315.0 37.4 %collective-permute-done.36 = bf16[1024,2304]{1,0:T(8,128)(2,1)} collective-permute-done((bf16[1024,2304]{1,0:T(8,128)(2,1)}, bf16[1024,2304]{1,0:T(8,128)(2,1)}, u32[]{:S(2)}, u32[]{:S(2)}) %collective-permute-start.36) | collective-permute-done | bytes 4718624 | tf_op jit(solution)/shard_map/ppermute | solution.py:72
  355.3 15.5 %collective-permute-done.37 = bf16[1024,2304]{1,0:T(8,128)(2,1)} collective-permute-done((bf16[1024,2304]{1,0:T(8,128)(2,1)S(1)}, bf16[1024,2304]{1,0:T(8,128)(2,1)}, u32[]{:S(2)}, u32[]{:S(2)}) %collective-permute-start.37) | collective-permute-done | bytes 4718624 | tf_op jit(solution)/shard_map/ppermute | solution.py:72
  377.5 19.7 %collective-permute-done.39 = bf16[256,2048]{1,0:T(8,128)(2,1)S(1)} collective-permute-done((bf16[256,2048]{1,0:T(8,128)(2,1)S(1)}, bf16[256,2048]{1,0:T(8,128)(2,1)S(1)}, u32[]{:S(2)}, u32[]{:S(2)}) %collective-permute-start.39) | collective-permute-done | bytes 1048608 | tf_op jit(solution)/shard_map/ppermute | solution.py:91
  410.8 21.5 %collective-permute-done.43 = bf16[256,2304]{1,0:T(8,128)(2,1)} collective-permute-done((bf16[256,2304]{1,0:T(8,128)(2,1)}, bf16[256,2304]{1,0:T(8,128)(2,1)}, u32[]{:S(2)}, u32[]{:S(2)}) %collective-permute-start.43) | collective-permute-done | bytes 1179680 | tf_op jit(solution)/shard_map/ppermute | solution.py:72
  438.7 25.1 %expert_rows.2 = (bf16[2,576,2048]{2,1,0:T(8,128)(2,1)}, bf16[2,576,768]{2,1,0:T(8,128)(2,1)}, bf16[2,576,1536]{2,1,0:T(8,128)(2,1)}, bf16[2,576,128]{2,1,0:T(8,128)(2,1)}) custom-call(s32[6]{0:T(128)} %pad_add_fusion.2.first_ref, bf16[1024,2048]{1,0:T(8,128)(2,1)} %pad_maximum_fusion.4.rows_ref, s32[2,4,256]{2,1,0:T(4,128)} %bitcast.172, ...), custom_call_target="tpu_custom_call" | custom-call | flops 11000000512 | bytes 1024 | tf_op jit(solution)/shard_map/expert_rows/pallas_call | solution.py:763
  463.8 25.3 %expert_rows.3 = (bf16[2,576,2048]{2,1,0:T(8,128)(2,1)}, bf16[2,576,768]{2,1,0:T(8,128)(2,1)}, bf16[2,576,1536]{2,1,0:T(8,128)(2,1)}, bf16[2,576,128]{2,1,0:T(8,128)(2,1)}) custom-call(s32[6]{0:T(128)} %pad_add_fusion.2.first_ref, bf16[1024,2048]{1,0:T(8,128)(2,1)} %collective-permute-done.44.rows_ref, s32[2,4,256]{2,1,0:T(4,128)} %bitcast.174, ...), custom_call_target="tpu_custom_call" | custom-call | flops 11000000512 | bytes 1024 | tf_op jit(solution)/shard_map/expert_rows/pallas_call | solution.py:763
  489.1 36.1 %expert_grads.1 = bf16[4,2,512,2304]{3,2,1,0:T(8,128)(2,1)} custom-call(bf16[2,576,2048]{2,1,0:T(8,128)(2,1)} %get-tuple-element.178.row_a, bf16[2,576,2048]{2,1,0:T(8,128)(2,1)} %get-tuple-element.179.row_b, bf16[2,576,2048]{2,1,0:T(8,128)(2,1)} %pick.2.cot_ref.cot_a, bf16[2,576,2048]{2,1,0:T(8,128)(2,1)} %pick.3.cot_ref.cot_b, ...), custom_call_target="tpu_custom_call" | custom-call | flops 17999998976 | bytes 1024 | tf_op jit(solution)/shard_map/expert_grads/pallas_call | solution.py:870
  526.9 19.6 %row_grads.2 = bf16[4,256,2176]{2,1,0:T(8,128)(2,1)} custom-call(s32[4]{0:T(128)} %copy-done.70, bf16[2,576,1536]{2,1,0:T(8,128)(2,1)} %get-tuple-element.181.pre_b.left_ref, s32[1024,2]{1,0:T(8,128)} %bitcast.156, bf16[2,512,2304]{2,1,0:T(8,128)(2,1)} %pad_maximum_fusion.1, bf16[2,512,2304]{2,1,0:T(8,128)(2,1)} %bitcast.19.refs_1_, ...), custom_call_target="tpu_custom_call" | custom-call | flops 10000000000 | bytes 1024 | tf_op jit(solution)/shard_map/row_grads/pallas_call | solution.py:838
  548.7 18.6 %row_grads.3 = bf16[4,256,2176]{2,1,0:T(8,128)(2,1)} custom-call(s32[4]{0:T(128)} %copy-done.70, bf16[2,576,1536]{2,1,0:T(8,128)(2,1)} %get-tuple-element.183.pre_a.left_ref, s32[1024,2]{1,0:T(8,128)} %bitcast.154, bf16[2,512,2304]{2,1,0:T(8,128)(2,1)} %pad_maximum_fusion.1, bf16[2,512,2304]{2,1,0:T(8,128)(2,1)} %bitcast.19.refs_1_, ...), custom_call_target="tpu_custom_call" | custom-call | flops 10000000000 | bytes 1024 | tf_op jit(solution)/shard_map/row_grads/pallas_call | solution.py:838
  607.7 22.1 %collective-permute-done.48 = bf16[256,2176]{1,0:T(8,128)(2,1)S(1)} collective-permute-done((bf16[256,2176]{1,0:T(8,128)(2,1)S(1)}, bf16[256,2176]{1,0:T(8,128)(2,1)S(1)}, u32[]{:S(2)}, u32[]{:S(2)}) %collective-permute-start.48) | collective-permute-done | bytes 1114144 | tf_op jit(solution)/shard_map/ppermute | solution.py:113
  652.6 20.9 %collective-permute-done.50 = bf16[256,2176]{1,0:T(8,128)(2,1)S(1)} collective-permute-done((bf16[256,2176]{1,0:T(8,128)(2,1)S(1)}, bf16[256,2176]{1,0:T(8,128)(2,1)S(1)}, u32[]{:S(2)}, u32[]{:S(2)}) %collective-permute-start.50) | collective-permute-done | bytes 1114144 | tf_op jit(solution)/shard_map/ppermute | solution.py:113
  692.3 17.7 %collective-permute-done.52 = bf16[4,256,2048]{2,1,0:T(8,128)(2,1)S(1)} collective-permute-done((bf16[4,256,2048]{2,1,0:T(8,128)(2,1)S(1)}, bf16[4,256,2048]{2,1,0:T(8,128)(2,1)S(1)}, u32[]{:S(2)}, u32[]{:S(2)}) %collective-permute-start.52) | collective-permute-done | bytes 4194336 | tf_op jit(solution)/shard_map/ppermute | solution.py:68
  776.8 18.4 %attend_back.4 = (bf16[256,1024]{1,0:T(8,128)(2,1)}, bf16[2048,256]{1,0:T(8,128)(2,1)}, f32[8,128]{1,0:T(8,128)}) custom-call(s32[12]{0:T(128)} %pad_add_fusion.place, f32[256,5120]{1,0:T(8,128)} %dense_matmul.2.raw_ref, bf16[1024,1024]{1,0:T(8,128)(2,1)} %pad_maximum_fusion.8.key_a.value_a, bf16[1024,1024]{1,0:T(8,128)(2,1)} %collective-permute-done.25.key_b.value_b, ...), custom_call_target="tpu_custom_call" | custom-call | flops 8999999488 | bytes 1024 | tf_op jit(solution)/shard_map/attend_back/pallas_call | solution.py:627
  804.7 18.3 %attend_back.5 = (bf16[256,1024]{1,0:T(8,128)(2,1)}, bf16[2048,256]{1,0:T(8,128)(2,1)}, f32[8,128]{1,0:T(8,128)}) custom-call(s32[12]{0:T(128)} %pad_add_fusion.place, f32[256,5120]{1,0:T(8,128)} %dense_matmul.2.raw_ref, bf16[1024,1024]{1,0:T(8,128)(2,1)} %pad_maximum_fusion.8.key_a.value_a, bf16[1024,1024]{1,0:T(8,128)(2,1)} %collective-permute-done.25.key_b.value_b, ...), custom_call_target="tpu_custom_call" | custom-call | flops 8999999488 | bytes 1024 | tf_op jit(solution)/shard_map/attend_back/pallas_call | solution.py:627
  835.8 18.2 %attend_back.6 = (bf16[256,1024]{1,0:T(8,128)(2,1)}, bf16[2048,256]{1,0:T(8,128)(2,1)}, f32[8,128]{1,0:T(8,128)}) custom-call(s32[12]{0:T(128)} %pad_add_fusion.place, f32[256,5120]{1,0:T(8,128)} %dense_matmul.2.raw_ref, bf16[1024,1024]{1,0:T(8,128)(2,1)} %pad_maximum_fusion.8.key_a.value_a, bf16[1024,1024]{1,0:T(8,128)(2,1)} %collective-permute-done.25.key_b.value_b, ...), custom_call_target="tpu_custom_call" | custom-call | flops 8999999488 | bytes 1024 | tf_op jit(solution)/shard_map/attend_back/pallas_call | solution.py:627
  858.0 18.2 %attend_back.7 = (bf16[256,1024]{1,0:T(8,128)(2,1)}, bf16[2048,256]{1,0:T(8,128)(2,1)}, f32[8,128]{1,0:T(8,128)}) custom-call(s32[12]{0:T(128)} %pad_add_fusion.place, f32[256,5120]{1,0:T(8,128)} %dense_matmul.2.raw_ref, bf16[1024,1024]{1,0:T(8,128)(2,1)} %pad_maximum_fusion.8.key_a.value_a, bf16[1024,1024]{1,0:T(8,128)(2,1)} %collective-permute-done.25.key_b.value_b, ...), custom_call_target="tpu_custom_call" | custom-call | flops 8999999488 | bytes 1024 | tf_op jit(solution)/shard_map/attend_back/pallas_call | solution.py:627
  976.7 15.4 %dense_back.3 = f32[256,2048]{1,0:T(8,128)} custom-call(bf16[256,5120]{1,0:T(8,128)(2,1)} %constant_dynamic-update-slice_fusion.4.left_ref, bf16[256,5120]{1,0:T(8,128)(2,1)} %copy-done.3, bf16[256,5120]{1,0:T(8,128)(2,1)} %collective-permute-done.2.refs_3_.refs_1_, bf16[256,5120]{1,0:T(8,128)(2,1)} %collective-permute-done.3.refs_4_.refs_2_, ...), custom_call_target="tpu_custom_call" | custom-call | flops 6000000000 | bytes 1024 | tf_op jit(solution)/shard_map/dense_back/pallas_call | solution.py:353
  1054.6 48.3 %all-reduce.5.cloned.1.call-done = bf16[512,2048]{1,0:T(8,128)(2,1)} async-done(((bf16[512,2048]{1,0:T(8,128)(2,1)}), bf16[512,2048]{1,0:T(8,128)(2,1)}) %all-reduce.5.cloned.1.call-update) | async-done | bytes 2097168 | tf_op jit(solution)/shard_map/psum | solution.py:137
  1113.2 15.6 %collective-permute-done.80 = bf16[64,1024]{1,0:T(8,128)(2,1)S(1)} collective-permute-done((bf16[64,1024]{1,0:T(8,128)(2,1)S(1)}, bf16[64,1024]{1,0:T(8,128)(2,1)S(1)}, u32[]{:S(2)}, u32[]{:S(2)}) %collective-permute-start.80) | collective-permute-done | bytes 131104 | tf_op jit(solution)/shard_map/ppermute | solution.py:72
  1130.6 69.1 %all-reduce.7.cloned.1.call-done = bf16[256,4096]{1,0:T(8,128)(2,1)} async-done(((bf16[256,4096]{1,0:T(8,128)(2,1)}), bf16[256,4096]{1,0:T(8,128)(2,1)}) %all-reduce.7.cloned.1.call-update) | async-done | bytes 2097168 | tf_op jit(solution)/shard_map/psum | solution.py:137
  (571 shorter events, 602.9 us)
Async XLA Ops:
  7.2 769.6 %reduce-scatter.7.cloned.1.call-start = ((), (), s32[]{:S(2)}) async-start(), calls=%async_computation.5 | async-start | bytes 23592960
  32.5 56.1 %collective-permute-start.2 = (bf16[256,5120]{1,0:T(8,128)(2,1)S(1)}, bf16[256,5120]{1,0:T(8,128)(2,1)}, u32[]{:S(2)}, u32[]{:S(2)}) collective-permute-start(bf16[256,5120]{1,0:T(8,128)(2,1)S(1)} %pad_maximum_fusion.6.refs_2_.refs_0_), channel_id=1, source_target_pairs={{0,8},{8,0},{16,24},{24,16},{1,9},{9,1},{17,25},{25,17},{2,10},{10... | collective-permute-start | bytes 7864328 | tf_op jit(solution)/shard_map/ppermute | solution.py:72
  32.9 57.2 %collective-permute-start.3 = (bf16[256,5120]{1,0:T(8,128)(2,1)S(1)}, bf16[256,5120]{1,0:T(8,128)(2,1)}, u32[]{:S(2)}, u32[]{:S(2)}) collective-permute-start(bf16[256,5120]{1,0:T(8,128)(2,1)S(1)} %pad_maximum_fusion.6.refs_2_.refs_0_), channel_id=1, source_target_pairs={{0,16},{8,24},{16,0},{24,8},{1,17},{9,25},{17,1},{25,9},{2,18},{10... | collective-permute-start | bytes 7864328 | tf_op jit(solution)/shard_map/ppermute | solution.py:72
  93.1 43.7 %collective-permute-start.10 = (bf16[256,5120]{1,0:T(8,128)(2,1)}, bf16[256,5120]{1,0:T(8,128)(2,1)}, u32[]{:S(2)}, u32[]{:S(2)}) collective-permute-start(bf16[256,5120]{1,0:T(8,128)(2,1)} %collective-permute-done.2.refs_3_.refs_1_), channel_id=1, source_target_pairs={{0,1},{1,0},{2,3},{3,2},{4,5},{5,4},{6,7},{7,6},{8,9},{9,8},{10,11... | collective-permute-start | bytes 7864328 | tf_op jit(solution)/shard_map/ppermute | solution.py:68
  119.2 70.9 %collective-permute-start.20 = (bf16[1024,2176]{1,0:T(8,128)(2,1)}, bf16[1024,2176]{1,0:T(8,128)(2,1)}, u32[]{:S(2)}, u32[]{:S(2)}) collective-permute-start(bf16[1024,2176]{1,0:T(8,128)(2,1)} %pad_maximum_fusion.3.rows_ref), channel_id=1, source_target_pairs={{0,1},{1,0},{2,3},{3,2},{4,5},{5,4},{6,7},{7,6},{8,9},{9,8},{10,11... | collective-permute-start | bytes 13369352 | tf_op jit(solution)/shard_map/ppermute | solution.py:68
  136.7 61.2 %collective-permute-start.21 = (bf16[512,2048]{1,0:T(8,128)(2,1)}, bf16[512,2048]{1,0:T(8,128)(2,1)}, u32[]{:S(2)}, u32[]{:S(2)}) collective-permute-start(bf16[512,2048]{1,0:T(8,128)(2,1)} %get-tuple-element.150.refs_2_.refs_0_), channel_id=1, source_target_pairs={{0,8},{8,0},{16,24},{24,16},{1,9},{9,1},{17,25},{25,17},{2,10},{10... | collective-permute-start | bytes 6291464 | tf_op jit(solution)/shard_map/ppermute | solution.py:72
  137.0 60.9 %collective-permute-start.22 = (bf16[512,2048]{1,0:T(8,128)(2,1)}, bf16[512,2048]{1,0:T(8,128)(2,1)}, u32[]{:S(2)}, u32[]{:S(2)}) collective-permute-start(bf16[512,2048]{1,0:T(8,128)(2,1)} %get-tuple-element.150.refs_2_.refs_0_), channel_id=1, source_target_pairs={{0,16},{8,24},{16,0},{24,8},{1,17},{9,25},{17,1},{25,9},{2,18},{10... | collective-permute-start | bytes 6291464 | tf_op jit(solution)/shard_map/ppermute | solution.py:72
  219.0 48.3 %collective-permute-start.28 = (bf16[512,2048]{1,0:T(8,128)(2,1)}, bf16[512,2048]{1,0:T(8,128)(2,1)}, u32[]{:S(2)}, u32[]{:S(2)}) collective-permute-start(bf16[512,2048]{1,0:T(8,128)(2,1)} %collective-permute-done.21.refs_3_.refs_1_), channel_id=1, source_target_pairs={{0,1},{1,0},{2,3},{3,2},{4,5},{5,4},{6,7},{7,6},{8,9},{9,8},{10,11... | collective-permute-start | bytes 6291464 | tf_op jit(solution)/shard_map/ppermute | solution.py:68
  228.6 123.9 %collective-permute-start.36 = (bf16[1024,2304]{1,0:T(8,128)(2,1)}, bf16[1024,2304]{1,0:T(8,128)(2,1)}, u32[]{:S(2)}, u32[]{:S(2)}) collective-permute-start(bf16[1024,2304]{1,0:T(8,128)(2,1)} %bitcast.142), channel_id=1, source_target_pairs={{0,8},{8,0},{16,24},{24,16},{1,9},{9,1},{17,25},{25,17},{2,10},{10... | collective-permute-start | bytes 14155784 | tf_op jit(solution)/shard_map/ppermute | solution.py:72
  267.3 103.4 %collective-permute-start.37 = (bf16[1024,2304]{1,0:T(8,128)(2,1)S(1)}, bf16[1024,2304]{1,0:T(8,128)(2,1)}, u32[]{:S(2)}, u32[]{:S(2)}) collective-permute-start(bf16[1024,2304]{1,0:T(8,128)(2,1)S(1)} %bitcast.145), channel_id=1, source_target_pairs={{0,16},{8,24},{16,0},{24,8},{1,17},{9,25},{17,1},{25,9},{2,18},{10... | collective-permute-start | bytes 14155784 | tf_op jit(solution)/shard_map/ppermute | solution.py:72
  313.0 42.3 %collective-permute-start.34 = (bf16[256,2048]{1,0:T(8,128)(2,1)S(1)}, bf16[256,2048]{1,0:T(8,128)(2,1)S(1)}, u32[]{:S(2)}, u32[]{:S(2)}) collective-permute-start(bf16[256,2048]{1,0:T(8,128)(2,1)S(1)} %collective-permute-done.32), channel_id=1, source_target_pairs={{2,4},{4,6},{3,5},{5,7},{10,12},{12,14},{11,13},{13,15},{18,20},{2... | collective-permute-start | bytes 3145736 | tf_op jit(solution)/shard_map/ppermute | solution.py:90
  313.7 41.6 %collective-permute-start.35 = (bf16[256,2048]{1,0:T(8,128)(2,1)S(1)}, bf16[256,2048]{1,0:T(8,128)(2,1)S(1)}, u32[]{:S(2)}, u32[]{:S(2)}) collective-permute-start(bf16[256,2048]{1,0:T(8,128)(2,1)S(1)} %collective-permute-done.33), channel_id=1, source_target_pairs={{2,0},{4,2},{3,1},{5,3},{10,8},{12,10},{11,9},{13,11},{18,16},{20,... | collective-permute-start | bytes 3145736 | tf_op jit(solution)/shard_map/ppermute | solution.py:91
  402.4 61.4 %collective-permute-start.44 = (bf16[1024,2048]{1,0:T(8,128)(2,1)}, bf16[1024,2048]{1,0:T(8,128)(2,1)}, u32[]{:S(2)}, u32[]{:S(2)}) collective-permute-start(bf16[1024,2048]{1,0:T(8,128)(2,1)} %pad_maximum_fusion.4.rows_ref), channel_id=1, source_target_pairs={{0,1},{1,0},{2,3},{3,2},{4,5},{5,4},{6,7},{7,6},{8,9},{9,8},{10,11... | collective-permute-start | bytes 12582920 | tf_op jit(solution)/shard_map/ppermute | solution.py:68
  525.2 410.2 %reduce-scatter.5.cloned.1.call-start = ((), (), s32[]{:S(2)}) async-start(), calls=%async_computation.2 | async-start | bytes 10485760 | tf_op jit(solution)/shard_map/reduce_scatter | solution.py:216
  690.3 46.2 %collective-permute-start.57 = (bf16[2048,2048]{1,0:T(8,128)(2,1)}, bf16[2048,2048]{1,0:T(8,128)(2,1)}, u32[]{:S(2)}, u32[]{:S(2)}) collective-permute-start(bf16[2048,2048]{1,0:T(8,128)(2,1)} %convolution_convert_fusion.1), channel_id=1, source_target_pairs={{0,1},{1,0},{2,3},{3,2},{4,5},{5,4},{6,7},{7,6},{8,9},{9,8},{10,11... | collective-permute-start | bytes 25165832 | tf_op jit(solution)/shard_map/ppermute | solution.py:68
  772.3 330.7 %all-reduce.5.cloned.1.call-start = ((), (), s32[]{:S(2)}) async-start(), calls=%async_computation.3 | async-start | bytes 4194304 | tf_op jit(solution)/shard_map/psum | solution.py:137
  960.4 65.1 %collective-permute-start.71 = (bf16[256,4096]{1,0:T(8,128)(2,1)}, bf16[256,4096]{1,0:T(8,128)(2,1)}, u32[]{:S(2)}, u32[]{:S(2)}) collective-permute-start(bf16[256,4096]{1,0:T(8,128)(2,1)} %pad_maximum_fusion.10), channel_id=1, source_target_pairs={{0,16},{8,24},{16,0},{24,8},{1,17},{9,25},{17,1},{25,9},{2,18},{10... | collective-permute-start | bytes 6291464 | tf_op jit(solution)/shard_map/ppermute | solution.py:72
  962.6 62.9 %collective-permute-start.70 = (bf16[256,4096]{1,0:T(8,128)(2,1)}, bf16[256,4096]{1,0:T(8,128)(2,1)}, u32[]{:S(2)}, u32[]{:S(2)}) collective-permute-start(bf16[256,4096]{1,0:T(8,128)(2,1)} %pad_maximum_fusion.9), channel_id=1, source_target_pairs={{0,8},{8,0},{16,24},{24,16},{1,9},{9,1},{17,25},{25,17},{2,10},{10... | collective-permute-start | bytes 6291464 | tf_op jit(solution)/shard_map/ppermute | solution.py:72
  972.7 48.9 %collective-permute-start.73 = (bf16[1024,1024]{1,0:T(8,128)(2,1)}, bf16[1024,1024]{1,0:T(8,128)(2,1)}, u32[]{:S(2)}, u32[]{:S(2)}) collective-permute-start(bf16[1024,1024]{1,0:T(8,128)(2,1)} %convolution_convert_fusion.2), channel_id=1, source_target_pairs={{0,1},{1,0},{2,3},{3,2},{4,5},{5,4},{6,7},{7,6},{8,9},{9,8},{10,11... | collective-permute-start | bytes 6291464 | tf_op jit(solution)/shard_map/ppermute | solution.py:68
  1012.5 187.2 %all-reduce.7.cloned.1.call-start = ((), (), s32[]{:S(2)}) async-start(), calls=%async_computation.4 | async-start | bytes 4194304 | tf_op jit(solution)/shard_map/psum | solution.py:137
  1053.0 50.6 %collective-permute-start.78 = (bf16[128,1024]{1,0:T(8,128)(2,1)S(1)}, bf16[128,1024]{1,0:T(8,128)(2,1)S(1)}, u32[]{:S(2)}, u32[]{:S(2)}) collective-permute-start(bf16[128,1024]{1,0:T(8,128)(2,1)S(1)} %constant_dynamic-slice_fusion.1), channel_id=1, source_target_pairs={{0,2},{2,0},{4,6},{6,4},{1,3},{3,1},{5,7},{7,5},{8,10},{10,8},{12,... | collective-permute-start | bytes 786440 | tf_op jit(solution)/shard_map/ppermute | solution.py:72
  1053.2 51.6 %collective-permute-start.88 = (f32[1,9280]{1,0:T(1,128)S(1)}, f32[1,9280]{1,0:T(1,128)S(1)}, u32[]{:S(2)}, u32[]{:S(2)}) collective-permute-start(f32[1,9280]{1,0:T(1,128)S(1)} %slice.444), channel_id=1, source_target_pairs={{0,8},{8,0},{16,24},{24,16},{1,9},{9,1},{17,25},{25,17},{2,10},{10... | collective-permute-start | bytes 111368 | tf_op jit(solution)/shard_map/ppermute | solution.py:72
  1103.0 97.7 %collective-permute-start.83 = (bf16[512,2048]{1,0:T(8,128)(2,1)}, bf16[512,2048]{1,0:T(8,128)(2,1)}, u32[]{:S(2)}, u32[]{:S(2)}) collective-permute-start(bf16[512,2048]{1,0:T(8,128)(2,1)} %all-reduce.5.cloned.1.call-done), channel_id=1, source_target_pairs={{0,1},{1,0},{2,3},{3,2},{4,5},{5,4},{6,7},{7,6},{8,9},{9,8},{10,11... | collective-permute-start | bytes 6291464 | tf_op jit(solution)/shard_map/ppermute | solution.py:68
  1128.9 71.6 %collective-permute-start.81 = (bf16[128,1024]{1,0:T(8,128)(2,1)S(1)}, bf16[128,1024]{1,0:T(8,128)(2,1)S(1)}, u32[]{:S(2)}, u32[]{:S(2)}) collective-permute-start(bf16[128,1024]{1,0:T(8,128)(2,1)S(1)} %pad_maximum_fusion.17), channel_id=1, source_target_pairs={{0,2},{2,0},{4,6},{6,4},{1,3},{3,1},{5,7},{7,5},{8,10},{10,8},{12,... | collective-permute-start | bytes 786440 | tf_op jit(solution)/shard_map/ppermute | solution.py:72
  (163 other events, 3095.2 us)
Sparse Core Ops, SparseCore 0:
  525.3 170.4 reduce-scatter.6
  772.4 86.7 reduce-scatter.4
  1012.6 90.2 all-reduce.4
  1105.9 93.8 all-reduce.6

commit v2 on v1

--- a/solution.py
+++ b/solution.py
@@ -106,10 +106,11 @@
         count = lax.axis_size("z")
         self.done += 1
         up, down = self.slots[self.done], self.slots[count - self.done]
+        if before:
+            up, down = lax.optimization_barrier((up, down) + before)[:2]
         if self.done > 1:
             up, down = plus(up, self.held[0]), plus(down, self.held[1])
-        if before:
-            up, down = lax.optimization_barrier((up, down) + before)[:2]
+        self.sent = (up, down)
         up = lax.ppermute(up, "z", [(p, p + 1) for p in range(self.done)])
         down = lax.ppermute(
             down, "z", [(p, p - 1) for p in range(count - 1, count - 1 - self.done, -1)]
@@ -123,8 +124,8 @@
         return plus(self.slots[0], *self.held)
 
 
-def ea_gather(value, before=None):
-    mine = jnp.concatenate(line_gather(value, before))
+def ea_gather(value, before=None, steps=None):
+    mine = jnp.concatenate(line_gather(value, before, steps))
     return mine, swap_core(mine)
 
 
@@ -179,17 +180,6 @@
     return [swap_axis(to_y, "ga", 2), swap_axis(to_x, "ga", 1)]
 
 
-def shard_list(first, seconds, shape):
-    if len(first) == 1:
-        blocks = jnp.take(first[0].reshape((-1,) + shape), ga_order(), axis=0)
-        blocks = blocks.reshape((4, -1) + shape).swapaxes(1, 2)
-        blocks = blocks.reshape(4, shape[0], -1, shape[2])
-        return [blocks[q] for q in range(4)], jnp.arange(4, dtype=jnp.int32)
-    across = [hop[0] for hop in seconds] + [hop[1] for hop in seconds]
-    blocks = first + [jnp.concatenate(across)]
-    return [block.reshape(shape) for block in blocks], ga_order().astype(jnp.int32)
-
-
 def ga_sum_first(value):
     if lax.axis_size("ga") != 4:
         return (value,)
@@ -203,11 +193,12 @@
     return own, to_x, to_y
 
 
-def ga_sum_second(parts):
+def ga_sum_second(parts, before=()):
     if len(parts) == 1:
         return ga_sum_whole(parts[0])
     own, to_x, to_y = parts
-    return plus(own, swap_axis(to_x, "ga", 1), swap_axis(to_y, "ga", 2))
+    terms = (own, swap_axis(to_x, "ga", 1), swap_axis(to_y, "ga", 2))
+    return plus(*lax.optimization_barrier(terms + tuple(before))[:3])
 
 
 def ga_sum_whole(value):
@@ -248,10 +239,8 @@
     )
 
 
-def dense_other(mine, other_half):
-    if len(mine) == 1:
-        return [swap_core(mine[0])]
-    return [other_half] + [swap_core(piece) for piece in mine[1:]]
+def swap_pieces(pieces):
+    return [swap_core(piece) for piece in pieces]
 
 
 def split_cols(value, half):
@@ -264,6 +253,15 @@
             for r in range(groups)
         ],
         axis=1,
+    )
+
+
+def device_cols(value):
+    groups = lax.axis_size("ga")
+    width = value.shape[1] // groups
+    order = ga_order()
+    return jnp.concatenate(
+        [lax.dynamic_slice_in_dim(value, order[g] * width, width, 1) for g in range(groups)], axis=1
     )
 
 
@@ -284,12 +282,16 @@
     return plus(mine, swap_core(other))
 
 
-def whole_shard(share):
+def whole_shard(shares):
     core = lax.axis_index("core")
-    other_share = swap_core(share)
-    low = jnp.where(core == 0, share, other_share)
-    high = jnp.where(core == 0, other_share, share)
-    return jnp.concatenate([low, high], axis=0).astype(F32)
+    rows = shares[0].shape[0]
+    out = jnp.zeros((2 * rows, sum(share.shape[1] for share in shares)), F32)
+    at = 0
+    for share in shares:
+        for half, part in ((core, share), (1 - core, swap_core(share))):
+            out = lax.dynamic_update_slice(out, part.astype(F32), (half * rows, at))
+        at += share.shape[1]
+    return out
 
 
 def cost(micros):
@@ -536,7 +538,7 @@
             jax.ShapeDtypeStruct((KV, HEADS // KV, rows), F32),
         ],
         compiler_params=pltpu.CompilerParams(vmem_limit_bytes=VMEM),
-        cost_estimate=cost(18),
+        cost_estimate=cost(2),
         name="attend",
     )(place, raw, kv_mine, kv_other, kv_mine, kv_other, *tables)
 
@@ -702,11 +704,13 @@
     mark_ref,
     cot_ref,
     router_ref,
-    *refs,
+    weight_ref,
+    row_out,
+    act_out,
+    pre_out,
+    extra_out,
 ):
-    weight_refs = refs[:-5]
-    row_out, act_out, pre_out, extra_out, acc = refs[-5:]
-    _, depth, all_ff = weight_refs[0].shape
+    shards, _, depth, all_ff = weight_ref.shape
     ff = all_ff // 3
     experts = first_ref[1]
     block = spot_ref.shape[2]
@@ -727,16 +731,9 @@
     total = jnp.sum(weights, axis=1, keepdims=True)
     gate = jnp.sum(jnp.where(lanes == own, weights, 0.0), axis=1, keepdims=True)
     gate = gate / jnp.where(total > 0.0, total, 1.0)
-    for r, ref in enumerate(weight_refs):
-        cols = pl.ds(pl.multiple_of(first_ref[2 + r] * depth, depth), depth)
-        for left, span in ((row_out, slice(2 * ff)), (cot_ref, slice(2 * ff, all_ff))):
-            term = dot_nn(left[0, :, cols], ref[0, :, span])
-            if r == 0:
-                acc[:, span] = term
-            else:
-                acc[:, span] += term
-    act_grad = acc[:, 2 * ff :]
-    gate_pre, up_pre = acc[:, :ff], acc[:, ff : 2 * ff]
+    pre = dot_nn(rows, weight_ref[:, :, :, : 2 * ff].reshape(shards * depth, 2 * ff))
+    act_grad = dot_nn(cot_ref[0], weight_ref[:, :, :, 2 * ff :].reshape(shards * depth, ff))
+    gate_pre, up_pre = pre[:, :ff], pre[:, ff:]
     sig = 1.0 / (1.0 + jnp.exp(-gate_pre))
     silu = gate_pre * sig
     act = silu * up_pre
@@ -754,7 +751,7 @@
 
 def expert_rows(first, rows, spots, marks, cot_rows, router, weights, cap):
     experts, blocks, block = spots.shape
-    depth, all_ff = weights[0].shape[1:]
+    shards, _, depth, all_ff = weights.shape
     both = all_ff // 3 * 2
     width = rows.shape[1]
     count = blocks * cap
@@ -771,15 +768,14 @@
                 whole(marks),
                 one(count, width),
                 whole(router),
-            ]
-            + [one(depth, all_ff)] * len(weights),
+                pl.BlockSpec((shards, 1, depth, all_ff), lambda e, first: (0, e, 0, 0)),
+            ],
             out_specs=[
                 one(count, width),
                 one(count, both // 2),
                 one(count, both),
                 one(count, EXTRA),
             ],
-            scratch_shapes=[pltpu.VMEM((count, all_ff), F32)],
         ),
         out_shape=[
             jax.ShapeDtypeStruct((experts, count, width), BF16),
@@ -790,15 +786,14 @@
         compiler_params=pltpu.CompilerParams(vmem_limit_bytes=VMEM),
         cost_estimate=cost(11),
         name="expert_rows",
-    )(first, rows, spots, marks, cot_rows, router, *weights)
-
-
-def rows_back_kernel(cap, order, left_ref, spot_ref, *refs):
+    )(first, rows, spots, marks, cot_rows, router, weights)
+
+
+def rows_back_kernel(cap, shards, left_ref, spot_ref, *refs):
     out_ref, acc = refs[-2:]
     e = pl.program_id(0)
     blocks, block, wide = out_ref.shape
-    weight_refs = refs[: order.shape[0]]
-    depth = weight_refs[0].shape[1]
+    depth = refs[0].shape[2]
 
     @pl.when(e == 0)
     def _():
@@ -807,18 +802,16 @@
     lane = lax.broadcasted_iota(jnp.int32, spot_ref.shape, 1)
     spot = jnp.sum(jnp.where(lane == e, spot_ref[...], 0), axis=1, keepdims=True)
     puts = [put_rows(spot[b * block : (b + 1) * block], cap) for b in range(blocks)]
-    for r, ref in enumerate(weight_refs):
-        cols = pl.ds(pl.multiple_of(order[r] * depth, depth), depth)
-        rows = dot_nt(left_ref[0], ref[0]).astype(BF16)
+    for r in range(shards):
+        rows = dot_nt(left_ref[0], refs[r][0, 0]).astype(BF16)
         for b in range(blocks):
-            acc[b * block : (b + 1) * block, cols] += dot_nn(
+            acc[b * block : (b + 1) * block, r * depth : (r + 1) * depth] += dot_nn(
                 puts[b], rows[b * cap : (b + 1) * cap, :]
             )
-    if len(refs) > order.shape[0] + 2:
-        extra_ref = refs[order.shape[0]]
+    if len(refs) > shards + 2:
         for b in range(blocks):
             acc[b * block : (b + 1) * block, wide - EXTRA :] += dot_nn(
-                puts[b], extra_ref[0, b * cap : (b + 1) * cap, :]
+                puts[b], refs[shards][0, b * cap : (b + 1) * cap, :]
             )
 
     @pl.when(e == pl.num_programs(0) - 1)
@@ -826,31 +819,29 @@
         out_ref[...] = acc[...].astype(BF16).reshape(out_ref.shape)
 
 
-def rows_back(order, left, weights, at, spot_cols, cap, extra=None):
+def rows_back(left, weights, at, spot_cols, cap, extra=None):
     experts, count, size = left.shape
-    depth = weights[0].shape[1]
+    shards, _, depth, _ = weights.shape
     blocks = count // cap
     block = spot_cols.shape[0] // blocks
-    width = depth * len(weights) + (0 if extra is None else EXTRA)
+    width = depth * shards + (0 if extra is None else EXTRA)
     shape = (blocks, block, width)
-    one = lambda *shape: pl.BlockSpec((1,) + shape, lambda e, order: (e,) + (0,) * len(shape))
+    one = lambda *shape: pl.BlockSpec((1,) + shape, lambda e: (e,) + (0,) * len(shape))
+    shard = lambda r: pl.BlockSpec((1, 1, depth, size), lambda e: (r, e, 0, at))
     extras = [] if extra is None else [extra]
     return pl.pallas_call(
-        functools.partial(rows_back_kernel, cap),
-        grid_spec=pltpu.PrefetchScalarGridSpec(
-            num_scalar_prefetch=1,
-            grid=(experts,),
-            in_specs=[one(count, size), pl.BlockSpec(spot_cols.shape, lambda e, order: (0, 0))]
-            + [pl.BlockSpec((1, depth, size), lambda e, order: (e, 0, at))] * len(weights)
-            + [one(count, EXTRA)] * len(extras),
-            out_specs=pl.BlockSpec(shape, lambda e, order: (0, 0, 0)),
-            scratch_shapes=[pltpu.VMEM((blocks * block, width), F32)],
-        ),
+        functools.partial(rows_back_kernel, cap, shards),
+        grid=(experts,),
+        in_specs=[one(count, size), pl.BlockSpec(spot_cols.shape, lambda e: (0, 0))]
+        + [shard(r) for r in range(shards)]
+        + [one(count, EXTRA)] * len(extras),
+        out_specs=pl.BlockSpec(shape, lambda e: (0, 0, 0)),
         out_shape=jax.ShapeDtypeStruct(shape, BF16),
+        scratch_shapes=[pltpu.VMEM((blocks * block, width), F32)],
         compiler_params=pltpu.CompilerParams(vmem_limit_bytes=VMEM),
         cost_estimate=cost(5 if extra is None else 10),
         name="mixtures" if extra is None else "row_grads",
-    )(order, left, spot_cols, *weights, *extras)
+    )(left, spot_cols, *[weights] * shards, *extras)
 
 
 def expert_grad_kernel(row_a, row_b, cot_a, cot_b, pre_a, pre_b, act_a, act_b, out_ref):
@@ -937,7 +928,8 @@
     )
     qkv_second = ga_second_hop(qkv_first, 0, 1, cot_steps[1])
     qkv_mine = qkv_first + qkv_second
-    qkv_other = dense_other(qkv_mine, qkv_twin)
+    qkv_swapped = swap_pieces(qkv_mine[1:] if ga_count == 4 else qkv_mine)
+    qkv_other = ([qkv_twin] if ga_count == 4 else []) + qkv_swapped
     cot_mine = after(jnp.concatenate(cot_mine), *qkv_second)
     cot_sides = [cot_mine, swap_core(cot_mine)]
     first_expert = (chip * 2 + core) * local_experts
@@ -989,15 +981,20 @@
 
     out_own, out_twin = core_halves(w_out)
     out_first = ga_first_hop(after(out_own, *qkv_second))
-    kv_mine, kv_other = ea_gather(kv_own, {2: cot_rows[:1], 3: cot_rows[1:] + out_first[1:]})
-    out_mine = out_first + ga_second_hop(out_first, 0, 1, ())
+    kv_steps = []
+    kv_mine, kv_other = ea_gather(
+        kv_own, {2: cot_rows[:1], 3: cot_rows[1:] + out_first[1:]}, kv_steps
+    )
+    out_second = ga_second_hop(out_first, 0, 1, ())
+    out_mine = out_first + out_second
+    out_swapped = swap_pieces(out_mine[1:] if ga_count == 4 else out_mine)
+    out_other = ([out_twin] if ga_count == 4 else []) + out_swapped
     expert_own = jnp.concatenate([w_gate, w_up, jnp.swapaxes(w_down, 1, 2)], axis=2)
-    expert_flat = expert_own.reshape(-1, 3 * ff)
-    expert_gather = ga_first_hop(after(expert_flat, *out_first[1:]))
+    expert_all = lax.all_gather(after(expert_own, *out_first[1:], *kv_steps[1]), "ga", axis=0)
 
     att_mine, att_other, log_rows = attend(
         place,
-        qkv,
+        after(qkv, *out_second),
         kv_mine,
         kv_other,
         bias,
@@ -1005,23 +1002,18 @@
         sine,
         query_gain_row,
     )
-    out_other = dense_other(out_first + [after(p, att_mine) for p in out_mine[3:]], out_twin)
     hidden = input_f + pieces_matmul((att_mine, att_other), (out_mine, out_other))
     ffn_in = rms_norm(hidden, ffn_gain_f).astype(BF16)
 
-    row_slots = line_gather(ffn_in, {3: expert_gather[1:]})
-    hops = [ga_second_hop(expert_gather, 0, 2, ())]
-    row_mine = after(jnp.concatenate(row_slots), *hops[0])
+    row_mine = after(jnp.concatenate(line_gather(ffn_in)), expert_all)
     row_sides = [row_mine, swap_core(row_mine)]
-    hops.append(ga_second_hop(expert_gather, 1, 2, hops[0]))
-    expert_all, order = shard_list(expert_gather, hops, expert_own.shape)
     logits = dot_nn(ffn_in, router_full)
     own_marks = marks[:, :expert_total] > 0
     peak = jnp.max(jnp.where(own_marks, logits, MASKED_SCORE), axis=1, keepdims=True)
     weights = jnp.exp(jnp.where(own_marks, logits - peak, MASKED_SCORE))
     gates = weights / jnp.sum(weights, axis=1, keepdims=True)
 
-    first = jnp.concatenate([jnp.stack([first_expert, expert_total]).astype(jnp.int32), order])
+    first = jnp.stack([first_expert, expert_total]).astype(jnp.int32)
     picked, acts, pres, extras = [], [], [], []
     for side in range(2):
         rows, act, pre, extra = expert_rows(
@@ -1041,18 +1033,19 @@
     expert_grad = expert_grads(picked, cot_rows, pres, acts, ga_count)
     expert_sum = lax.psum_scatter(expert_grad, "ga", scatter_dimension=0)
     row_other = rows_back(
-        order, after(pres[1], expert_grad), expert_all, 0, spot_cols[1], cap, extras[1]
+        after(pres[1], expert_grad), expert_all, 0, spot_cols[1], cap, extras[1]
     )
     row_mine = rows_back(
-        order, after(pres[0], row_other), expert_all, 0, spot_cols[0], cap, extras[0]
+        after(pres[0], row_other), expert_all, 0, spot_cols[0], cap, extras[0]
     )
     rows = LineSum(core_slots(row_mine, row_other))
-    rows.step()
-    mix_other = rows_back(order, after(acts[1], rows.slots[1]), expert_all, 2, spot_cols[1], cap)
+    held = rows.step()
+    mix_other = rows_back(after(acts[1], rows.slots[1]), expert_all, 2, spot_cols[1], cap)
     rows.step(mix_other)
-    mix_mine = rows_back(order, after(acts[0], *rows.held), expert_all, 2, spot_cols[0], cap)
+    mix_mine = rows_back(after(acts[0], *held), expert_all, 2, spot_cols[0], cap)
+    mix = LineSum(core_slots(mix_mine, mix_other))
     rows.step(mix_mine)
-    row_sum = rows.result()
+    row_sum = after(rows.result(), *mix.slots)
 
     grad_out = cotangent.astype(F32)
     gate_grad = (
@@ -1071,7 +1064,7 @@
     hidden_part, ffn_gain_grad = ffn_back(ffn_in_grad)
     hidden_grad = grad_out + hidden_part
     branch_grad = hidden_grad.astype(BF16)
-    out_terms = [dot_tn(a, branch_grad) for a in (att_mine, att_other)]
+    out_terms = [dot_tn(device_cols(a), branch_grad) for a in (att_mine, att_other)]
     out_terms[1] = out_terms[1].astype(BF16)
     att_grads = pieces_back(after(branch_grad, out_terms[1]), out_mine + out_other, BF16)
     raw_grads, kv_grads, gain_grads = [], [], []
@@ -1099,44 +1092,51 @@
     def weight_terms(grad):
         return dot_tn(normed_mine, grad), dot_tn(normed_other, grad).astype(BF16)
 
-    mix = LineSum(core_slots(mix_mine, after(mix_other, out_terms[1])))
-    held = [mix.step()]
-    back(0, mix.slots[1], expert_sum)
+    held = [mix.step(*rows.held)]
+    back(0, out_terms[1], expert_sum, *mix.sent)
     held.append(mix.step(raw_grads[0]))
     out_total = core_sum(*out_terms)
-    out_share = ga_sum_whole(out_total)
+    out_share = lax.psum_scatter(out_total, "ga", scatter_dimension=0, tiled=True)
     back(1, raw_grads[0], out_total, *held[0])
     held.append(mix.step(raw_grads[1]))
+    query_parts = [jnp.concatenate(raw_grads[:2], axis=1)]
+    query_terms = [weight_terms(query_parts[0])]
     back(2, raw_grads[1], *held[1])
-    back(3, raw_grads[2], *held[2])
+    query_totals = [core_sum(*query_terms[0])]
+    back(3, raw_grads[2], query_terms[0][1], out_share, *held[2])
+    query_firsts = [ga_sum_first(query_totals[0])]
     mix_sum = mix.result()
     layer_output = (hidden + mix_sum.astype(F32)).astype(BF16)
-    query_raw_grad = jnp.concatenate(raw_grads, axis=1)
-    query_terms = weight_terms(query_raw_grad)
+    query_parts.append(jnp.concatenate(raw_grads[2:], axis=1))
+    query_terms.append(weight_terms(query_parts[1]))
     query_gain_grad = sum(gain_grads)
-    kv_grad = after(jnp.concatenate(kv_grads, axis=1), mix_sum)
+    kv_grad = after(jnp.concatenate(kv_grads, axis=1), *held[2])
     kv_grad = kv_grad.reshape(2, z_count, tok_count, 2 * kv_width)
     keys_values = LineSum(core_slots(kv_grad[0], kv_grad[1]))
-    keys_values.step(query_terms[1])
-    query_total = core_sum(*query_terms)
-    keys_values.step(query_total)
-    query_first = ga_sum_first(query_total)
-    keys_values.step(out_share)
+    keys_values.step(query_terms[1][1], *query_firsts[0])
+    query_shares = [ga_sum_second(query_firsts[0])]
+    query_totals.append(core_sum(*query_terms[1]))
+    out_all = z_all_sum(out_share)
+    keys_values.step(query_totals[1], out_all)
+    query_firsts.append(ga_sum_first(after(query_totals[1], query_shares[0])))
+    keys_values.step(query_shares[0])
     kv_raw_grad, key_gain_grad = kv_back(
-        qkv, after(keys_values.result(), *query_first), cosine, sine, key_gain_row
+        qkv, after(keys_values.result(), *query_firsts[1]), cosine, sine, key_gain_row
     )
     key_gain_grad = key_gain_grad[0]
-    out_all = z_all_sum(out_share)
-    query_share = ga_sum_second(query_first)
-    kv_total = core_sum(*weight_terms(kv_raw_grad))
-    kv_share = ga_sum_second(ga_sum_first(after(kv_total, query_share)))
-    query_all = z_all_sum(after(query_share, out_all))
-    out_sum, query_sum = whole_shard(out_all), whole_shard(query_all)
-    kv_sum = whole_shard(z_all_sum_small(kv_share))
-    key_sum, value_sum = kv_sum[:, :kv_width], kv_sum[:, kv_width:]
-    chunks = [query_raw_grad, kv_raw_grad]
+    chunks = query_parts + [kv_raw_grad]
     qkv_grad = jnp.concatenate(chunks, axis=1)
     both_grads = pieces_back(qkv_grad, qkv_mine + qkv_other, F32)
+    query_shares.append(ga_sum_second(query_firsts[1], [both_grads]))
+    kv_total = core_sum(*weight_terms(kv_raw_grad))
+    kv_first = ga_sum_first(after(kv_total, query_shares[1]))
+    query_alls = [z_all_sum(after(share, out_all)) for share in query_shares]
+    kv_share = ga_sum_second((kv_first[0],) + tuple(after(p, *query_alls) for p in kv_first[1:]))
+    kv_sum = whole_shard([z_all_sum_small(kv_share)])
+    out_sum = whole_shard([out_all])
+    query_sum = whole_shard(query_alls)
+    key_sum, value_sum = kv_sum[:, :kv_width], kv_sum[:, kv_width:]
+    both_grads = after(both_grads, *query_alls)
     half_width = model_width // 2
     normed_grad = join_cols(both_grads[:, :half_width], both_grads[:, half_width:])
     unused, attn_back = jax.vjp(rms_norm, input_f, attn_gain_f)

time: 1230 us -> 1200 us (0.976)
  waiting for transfers between devices: 481 us -> 458 us
  other arithmetic: 133 us -> 119 us
    ppermute x9, waiting for transfers between devices: 89 us -> 114 us  [line_gather(): lax.ppermute(down, 'z', [(p, p - 1) for p in range(1, count - step + 1)])]
    psum x2, waiting for transfers between devices: 117 us -> 95.9 us  [z_all_sum(): return lax.psum(value, 'z')]
    dynamic_update_slice x0 -> x8, other arithmetic: none -> 15.6 us  [whole_shard(): out = lax.dynamic_update_slice(out, part.astype(F32), (half * rows, at))]
    gather x3 -> x0, local copies, waits for them, and re-layouts: 14.1 us -> none  [ga_sum_whole(): blocks = jnp.take(blocks, ga_order(), axis=0).reshape(value.shape)]
    convert_element_type x4 -> x0, other arithmetic: 13.9 us -> none  [the longest x3 9 us: whole_shard(): return jnp.concatenate([low, high], axis=0).astype(F32)]
    unnamed x201 -> x252, local copies, waits for them, and re-layouts: 21 us -> 34.4 us
    ppermute x32 -> x30, waiting for transfers between devices: 117 us -> 105 us  [swap_axis(): lax.ppermute(value, axis, [(i, i ^ bit) for i in range(lax.axis_size(axis...]
    ppermute x21 -> x23, waiting for transfers between devices: 31.2 us -> 20.1 us  [swap_core(): return lax.ppermute(value, 'core', [(0, 1), (1, 0)])]
  transfers between devices with their start and end apart: 93 -> 94, of which waited for: 41 -> 41; matrix products, arithmetic and copies ran while one was open for 19% -> 17% of each run, Pallas kernels for 22% -> 22%
where the time goes in v2:
time: 1200 us; the launch traced here: 1190 us
  waiting for transfers between devices  458 us (38%)
  Pallas kernels  322 us (27%)
  starting transfers between devices  138 us (12%)
  other arithmetic  119 us (10%)
  local copies, waits for them, and re-layouts  90.9 us (8%)
  matrix products  39 us (3%)
  between operations  24 us (2%)
    ppermute x9, waiting for transfers between devices, line_gather(): lax.ppermute(down, 'z', [(p, p - 1) for p in range(1, count - step + 1)])  114 us
    ppermute x30, waiting for transfers between devices, swap_axis(): lax.ppermute(value, axis, [(i, i ^ bit) for i in range(lax.axis_size(axis...  105 us
    psum x2, waiting for transfers between devices, z_all_sum(): return lax.psum(value, 'z')  95.9 us
    pallas_call x4, Pallas kernels, attend_back(): pl.pallas_call(attend_back_kernel, grid_spec=pltpu.PrefetchScalarGridSpec...  73.3 us
    ppermute x9, waiting for transfers between devices, step(): up = lax.ppermute(up, 'z', [(p, p + 1) for p in range(self.done)])  71.8 us
    pallas_call x4, Pallas kernels, rows_back(): pl.pallas_call(functools.partial(rows_back_kernel, cap, shards), grid=(ex...  61.7 us
    pallas_call x2, Pallas kernels, expert_rows(): pl.pallas_call(functools.partial(expert_kernel, cap), grid_spec=pltpu.Pre...  44.8 us
    convert_element_type x25, other arithmetic, plus(): return total.astype(BF16)  40.7 us
  transfers between devices with their start and end apart: 94, of which 41 were waited for; matrix products, arithmetic and copies ran while one was open for 17% of the time, Pallas kernels for 22%

profile of v2, /device:TPU:1, one launch (start us, length us, event | category | flops | bytes accessed | tf_op | source)
XLA Modules:
  0.0 1190.9 jit_solution(1239993191288288681)
XLA Ops:
  39.5 14.1 %collective-permute-done.4 = bf16[256,2176]{1,0:T(8,128)(2,1)} collective-permute-done((bf16[256,2176]{1,0:T(8,128)(2,1)S(1)}, bf16[256,2176]{1,0:T(8,128)(2,1)}, u32[]{:S(2)}, u32[]{:S(2)}) %collective-permute-start.4) | collective-permute-done | bytes 1114144 | tf_op jit(solution)/shard_map/ppermute | solution.py:90
  70.4 16.1 %collective-permute-done.7 = bf16[256,2176]{1,0:T(8,128)(2,1)} collective-permute-done((bf16[256,2176]{1,0:T(8,128)(2,1)}, bf16[256,2176]{1,0:T(8,128)(2,1)}, u32[]{:S(2)}, u32[]{:S(2)}) %collective-permute-start.7) | collective-permute-done | bytes 1114144 | tf_op jit(solution)/shard_map/ppermute | solution.py:91
  109.6 18.5 %collective-permute-done.21 = bf16[256,2176]{1,0:T(8,128)(2,1)S(1)} collective-permute-done((bf16[256,2176]{1,0:T(8,128)(2,1)}, bf16[256,2176]{1,0:T(8,128)(2,1)S(1)}, u32[]{:S(2)}, u32[]{:S(2)}) %collective-permute-start.21) | collective-permute-done | bytes 1114144 | tf_op jit(solution)/shard_map/ppermute | solution.py:91
  150.2 14.1 %dense_matmul.2.raw_ref = f32[256,5120]{1,0:T(8,128)} custom-call(bf16[256,1024]{1,0:T(8,128)(2,1)} %pad_maximum_fusion.12.refs_0_, bf16[256,1024]{1,0:T(8,128)(2,1)} %pad_maximum_fusion.13.refs_1_, bf16[256,5120]{1,0:T(8,128)(2,1)} %pad_maximum_fusion.4.refs_2_.refs_0_, bf16[256,5120]{1,0:T(8,128)(2,1)} %collective-permute-done.2.refs_3_.refs_1_, ...), custom_call_target="tpu_custom_call" | custom-call | flops 6000000000 | bytes 1024 | tf_op jit(solution)/shard_map/dense_matmul/pallas_call | solution.py:320
  246.0 43.7 %collective-permute-done.16.refs_5_.refs_3_ = bf16[256,2048]{1,0:T(8,128)(2,1)} collective-permute-done((bf16[256,2048]{1,0:T(8,128)(2,1)S(1)}, bf16[256,2048]{1,0:T(8,128)(2,1)}, u32[]{:S(2)}, u32[]{:S(2)}) %collective-permute-start.16) | collective-permute-done | bytes 1048608 | tf_op jit(solution)/shard_map/ppermute | solution.py:72
  292.9 36.6 %attend.1 = (bf16[256,2048]{1,0:T(8,128)(2,1)}, bf16[256,2048]{1,0:T(8,128)(2,1)}, f32[4,8,256]{2,1,0:T(8,128)}) custom-call(s32[12]{0:T(128)} %pad_add_fusion.place, f32[256,5120]{1,0:T(8,128)} %dense_matmul.2.raw_ref, bf16[1024,1024]{1,0:T(8,128)(2,1)} %copy-done.4, bf16[1024,1024]{1,0:T(8,128)(2,1)} %collective-permute-done.27.key_b.value_b, ...), custom_call_target="tpu_custom_call" | custom-call | flops 2000000000 | bytes 1024 | tf_op jit(solution)/shard_map/attend/pallas_call | solution.py:523
  346.3 21.2 %collective-permute-done.32 = bf16[256,2048]{1,0:T(8,128)(2,1)S(1)} collective-permute-done((bf16[256,2048]{1,0:T(8,128)(2,1)S(1)}, bf16[256,2048]{1,0:T(8,128)(2,1)S(1)}, u32[]{:S(2)}, u32[]{:S(2)}) %collective-permute-start.32) | collective-permute-done | bytes 1048608 | tf_op jit(solution)/shard_map/ppermute | solution.py:90
  373.5 24.3 %collective-permute-done.35 = bf16[256,2048]{1,0:T(8,128)(2,1)S(1)} collective-permute-done((bf16[256,2048]{1,0:T(8,128)(2,1)S(1)}, bf16[256,2048]{1,0:T(8,128)(2,1)S(1)}, u32[]{:S(2)}, u32[]{:S(2)}) %collective-permute-start.35) | collective-permute-done | bytes 1048608 | tf_op jit(solution)/shard_map/ppermute | solution.py:91
  400.2 23.1 %collective-permute-done.37 = bf16[256,2048]{1,0:T(8,128)(2,1)S(1)} collective-permute-done((bf16[256,2048]{1,0:T(8,128)(2,1)S(1)}, bf16[256,2048]{1,0:T(8,128)(2,1)S(1)}, u32[]{:S(2)}, u32[]{:S(2)}) %collective-permute-start.37) | collective-permute-done | bytes 1048608 | tf_op jit(solution)/shard_map/ppermute | solution.py:91
  430.6 22.3 %expert_rows.2 = (bf16[2,576,2048]{2,1,0:T(8,128)(2,1)}, bf16[2,576,768]{2,1,0:T(8,128)(2,1)}, bf16[2,576,1536]{2,1,0:T(8,128)(2,1)}, bf16[2,576,128]{2,1,0:T(8,128)(2,1)}) custom-call(s32[2]{0:T(128)} %pad_add_fusion.2.first_ref, bf16[1024,2048]{1,0:T(8,128)(2,1)} %pad_maximum_fusion.2.rows_ref, s32[2,4,256]{2,1,0:T(4,128)} %bitcast.154, ...), custom_call_target="tpu_custom_call" | custom-call | flops 11000000512 | bytes 1024 | tf_op jit(solution)/shard_map/expert_rows/pallas_call | solution.py:760
  452.9 22.5 %expert_rows.3 = (bf16[2,576,2048]{2,1,0:T(8,128)(2,1)}, bf16[2,576,768]{2,1,0:T(8,128)(2,1)}, bf16[2,576,1536]{2,1,0:T(8,128)(2,1)}, bf16[2,576,128]{2,1,0:T(8,128)(2,1)}) custom-call(s32[2]{0:T(128)} %pad_add_fusion.2.first_ref, bf16[1024,2048]{1,0:T(8,128)(2,1)} %collective-permute-done.38.rows_ref, s32[2,4,256]{2,1,0:T(4,128)} %bitcast.156, ...), custom_call_target="tpu_custom_call" | custom-call | flops 11000000512 | bytes 1024 | tf_op jit(solution)/shard_map/expert_rows/pallas_call | solution.py:760
  475.4 36.1 %expert_grads.1 = bf16[4,2,512,2304]{3,2,1,0:T(8,128)(2,1)} custom-call(bf16[2,576,2048]{2,1,0:T(8,128)(2,1)} %get-tuple-element.180.row_a, bf16[2,576,2048]{2,1,0:T(8,128)(2,1)} %get-tuple-element.181.row_b, bf16[2,576,2048]{2,1,0:T(8,128)(2,1)} %pick.2.cot_ref.cot_a, bf16[2,576,2048]{2,1,0:T(8,128)(2,1)} %pick.3.cot_ref.cot_b, ...), custom_call_target="tpu_custom_call" | custom-call | flops 17999998976 | bytes 1024 | tf_op jit(solution)/shard_map/expert_grads/pallas_call | solution.py:861
  513.2 18.9 %row_grads.2 = bf16[4,256,2176]{2,1,0:T(8,128)(2,1)} custom-call(bf16[2,576,1536]{2,1,0:T(8,128)(2,1)} %get-tuple-element.183.pre_b.left_ref, s32[1024,2]{1,0:T(8,128)} %bitcast.138, bf16[4,2,512,2304]{3,2,1,0:T(8,128)(2,1)} %bitcast.119, bf16[4,2,512,2304]{3,2,1,0:T(8,128)(2,1)} %bitcast.120, bf16[4,2,512,2304]{3,2,1,0:T(8,128)(2,1)} %bitcast.121, ...), custom_call_target="tpu_custom_call" | custom-call | flops 10000000000 | bytes 1024 | tf_op jit(solution)/shard_map/row_grads/pallas_call | solution.py:832
  533.1 18.1 %row_grads.3 = bf16[4,256,2176]{2,1,0:T(8,128)(2,1)} custom-call(bf16[2,576,1536]{2,1,0:T(8,128)(2,1)} %get-tuple-element.185.pre_a.left_ref, s32[1024,2]{1,0:T(8,128)} %bitcast.136, bf16[4,2,512,2304]{3,2,1,0:T(8,128)(2,1)} %bitcast.123, bf16[4,2,512,2304]{3,2,1,0:T(8,128)(2,1)} %bitcast.124, bf16[4,2,512,2304]{3,2,1,0:T(8,128)(2,1)} %bitcast.125, ...), custom_call_target="tpu_custom_call" | custom-call | flops 10000000000 | bytes 1024 | tf_op jit(solution)/shard_map/row_grads/pallas_call | solution.py:832
  627.9 16.2 %collective-permute-done.45 = bf16[256,2176]{1,0:T(8,128)(2,1)S(1)} collective-permute-done((bf16[256,2176]{1,0:T(8,128)(2,1)}, bf16[256,2176]{1,0:T(8,128)(2,1)S(1)}, u32[]{:S(2)}, u32[]{:S(2)}) %collective-permute-start.45) | collective-permute-done | bytes 1114144 | tf_op jit(solution)/shard_map/ppermute | solution.py:114
  665.4 12.7 %collective-permute-done.47 = bf16[2048,2048]{1,0:T(8,128)(2,1)S(1)} collective-permute-done((bf16[2048,2048]{1,0:T(8,128)(2,1)S(1)}, bf16[2048,2048]{1,0:T(8,128)(2,1)S(1)}, u32[]{:S(2)}, u32[]{:S(2)}) %collective-permute-start.47) | collective-permute-done | bytes 8388640 | tf_op jit(solution)/shard_map/ppermute | solution.py:68
  713.6 18.5 %attend_back.4 = (bf16[256,1024]{1,0:T(8,128)(2,1)}, bf16[2048,256]{1,0:T(8,128)(2,1)}, f32[8,128]{1,0:T(8,128)}) custom-call(s32[12]{0:T(128)} %pad_add_fusion.place, f32[256,5120]{1,0:T(8,128)} %dense_matmul.2.raw_ref, bf16[1024,1024]{1,0:T(8,128)(2,1)} %copy-done.4, bf16[1024,1024]{1,0:T(8,128)(2,1)} %collective-permute-done.27.key_b.value_b, ...), custom_call_target="tpu_custom_call" | custom-call | flops 8999999488 | bytes 1024 | tf_op jit(solution)/shard_map/attend_back/pallas_call | solution.py:629
  740.6 18.2 %attend_back.5 = (bf16[256,1024]{1,0:T(8,128)(2,1)}, bf16[2048,256]{1,0:T(8,128)(2,1)}, f32[8,128]{1,0:T(8,128)}) custom-call(s32[12]{0:T(128)} %pad_add_fusion.place, f32[256,5120]{1,0:T(8,128)} %dense_matmul.2.raw_ref, bf16[1024,1024]{1,0:T(8,128)(2,1)} %copy-done.4, bf16[1024,1024]{1,0:T(8,128)(2,1)} %collective-permute-done.27.key_b.value_b, ...), custom_call_target="tpu_custom_call" | custom-call | flops 8999999488 | bytes 1024 | tf_op jit(solution)/shard_map/attend_back/pallas_call | solution.py:629
  772.6 18.2 %attend_back.6 = (bf16[256,1024]{1,0:T(8,128)(2,1)}, bf16[2048,256]{1,0:T(8,128)(2,1)}, f32[8,128]{1,0:T(8,128)}) custom-call(s32[12]{0:T(128)} %pad_add_fusion.place, f32[256,5120]{1,0:T(8,128)} %dense_matmul.2.raw_ref, bf16[1024,1024]{1,0:T(8,128)(2,1)} %copy-done.4, bf16[1024,1024]{1,0:T(8,128)(2,1)} %collective-permute-done.27.key_b.value_b, ...), custom_call_target="tpu_custom_call" | custom-call | flops 8999999488 | bytes 1024 | tf_op jit(solution)/shard_map/attend_back/pallas_call | solution.py:629
  797.6 18.3 %attend_back.7 = (bf16[256,1024]{1,0:T(8,128)(2,1)}, bf16[2048,256]{1,0:T(8,128)(2,1)}, f32[8,128]{1,0:T(8,128)}) custom-call(s32[12]{0:T(128)} %pad_add_fusion.place, f32[256,5120]{1,0:T(8,128)} %dense_matmul.2.raw_ref, bf16[1024,1024]{1,0:T(8,128)(2,1)} %copy-done.4, bf16[1024,1024]{1,0:T(8,128)(2,1)} %collective-permute-done.27.key_b.value_b, ...), custom_call_target="tpu_custom_call" | custom-call | flops 8999999488 | bytes 1024 | tf_op jit(solution)/shard_map/attend_back/pallas_call | solution.py:629
  858.4 21.6 %collective-permute-done.61 = bf16[256,1024]{1,0:T(8,128)(2,1)S(1)} collective-permute-done((bf16[256,1024]{1,0:T(8,128)(2,1)S(1)}, bf16[256,1024]{1,0:T(8,128)(2,1)S(1)}, u32[]{:S(2)}, u32[]{:S(2)}) %collective-permute-start.61) | collective-permute-done | bytes 524320 | tf_op jit(solution)/shard_map/ppermute | solution.py:114
  887.8 42.5 %all-reduce.6.cloned.1.call-done = bf16[512,2048]{1,0:T(8,128)(2,1)} async-done(((bf16[512,2048]{1,0:T(8,128)(2,1)}), bf16[512,2048]{1,0:T(8,128)(2,1)}) %all-reduce.6.cloned.1.call-update) | async-done | bytes 2097168 | tf_op jit(solution)/shard_map/psum | solution.py:138
  991.1 15.7 %dense_back.3 = f32[256,2048]{1,0:T(8,128)} custom-call(bf16[256,5120]{1,0:T(8,128)(2,1)} %constant_dynamic-update-slice_fusion.4.left_ref, bf16[256,5120]{1,0:T(8,128)(2,1)} %pad_maximum_fusion.4.refs_2_.refs_0_, bf16[256,5120]{1,0:T(8,128)(2,1)} %collective-permute-done.2.refs_3_.refs_1_, bf16[256,5120]{1,0:T(8,128)(2,1)} %collective-permute-done.3.refs_4_.refs_2_, ...), custom_call_target="tpu_custom_call" | custom-call | flops 6000000000 | bytes 1024 | tf_op jit(solution)/shard_map/dense_back/pallas_call | solution.py:355
  1043.3 53.5 %all-reduce.8.cloned.1.call-done = (bf16[256,2048]{1,0:T(8,128)(2,1)}, bf16[256,2048]{1,0:T(8,128)(2,1)}) async-done(((bf16[256,2048]{1,0:T(8,128)(2,1)}, bf16[256,2048]{1,0:T(8,128)(2,1)}), (bf16[256,2048]{1,0:T(8,128)(2,1)}, bf16[256,2048]{1,0:T(8,128)(2,1)})) %all-reduce.8.cloned.1.call-update) | async-done | bytes 2097168 | tf_op jit(solution)/shard_map/psum | solution.py:138
  (639 shorter events, 602.0 us)
Async XLA Ops:
  7.2 418.7 %all-gather.3.cloned.1.call-start = ((), (), s32[]{:S(2)}) async-start(), calls=%async_computation.4 | async-start | bytes 23592960 | tf_op jit(solution)/shard_map/all_gather | solution.py:993
  35.3 58.5 %collective-permute-start.2 = (bf16[256,5120]{1,0:T(8,128)(2,1)}, bf16[256,5120]{1,0:T(8,128)(2,1)}, u32[]{:S(2)}, u32[]{:S(2)}) collective-permute-start(bf16[256,5120]{1,0:T(8,128)(2,1)} %pad_maximum_fusion.4.refs_2_.refs_0_), channel_id=1, source_target_pairs={{0,8},{8,0},{16,24},{24,16},{1,9},{9,1},{17,25},{25,17},{2,10},{10... | collective-permute-start | bytes 7864328 | tf_op jit(solution)/shard_map/ppermute | solution.py:72
  38.2 64.7 %collective-permute-start.3 = (bf16[256,5120]{1,0:T(8,128)(2,1)}, bf16[256,5120]{1,0:T(8,128)(2,1)}, u32[]{:S(2)}, u32[]{:S(2)}) collective-permute-start(bf16[256,5120]{1,0:T(8,128)(2,1)} %pad_maximum_fusion.4.refs_2_.refs_0_), channel_id=1, source_target_pairs={{0,16},{8,24},{16,0},{24,8},{1,17},{9,25},{17,1},{25,9},{2,18},{10... | collective-permute-start | bytes 7864328 | tf_op jit(solution)/shard_map/ppermute | solution.py:72
  93.8 45.0 %collective-permute-start.10 = (bf16[256,5120]{1,0:T(8,128)(2,1)}, bf16[256,5120]{1,0:T(8,128)(2,1)S(1)}, u32[]{:S(2)}, u32[]{:S(2)}) collective-permute-start(bf16[256,5120]{1,0:T(8,128)(2,1)} %collective-permute-done.2.refs_3_.refs_1_), channel_id=1, source_target_pairs={{0,1},{1,0},{2,3},{3,2},{4,5},{5,4},{6,7},{7,6},{8,9},{9,8},{10,11... | collective-permute-start | bytes 7864328 | tf_op jit(solution)/shard_map/ppermute | solution.py:68
  105.9 40.1 %collective-permute-start.11 = (bf16[256,5120]{1,0:T(8,128)(2,1)}, bf16[256,5120]{1,0:T(8,128)(2,1)}, u32[]{:S(2)}, u32[]{:S(2)}) collective-permute-start(bf16[256,5120]{1,0:T(8,128)(2,1)} %collective-permute-done.3.refs_4_.refs_2_), channel_id=1, source_target_pairs={{0,1},{1,0},{2,3},{3,2},{4,5},{5,4},{6,7},{7,6},{8,9},{9,8},{10,11... | collective-permute-start | bytes 7864328 | tf_op jit(solution)/shard_map/ppermute | solution.py:68
  138.4 62.2 %collective-permute-start.14 = (bf16[512,2048]{1,0:T(8,128)(2,1)}, bf16[512,2048]{1,0:T(8,128)(2,1)}, u32[]{:S(2)}, u32[]{:S(2)}) collective-permute-start(bf16[512,2048]{1,0:T(8,128)(2,1)} %get-tuple-element.150.refs_2_.refs_0_), channel_id=1, source_target_pairs={{0,8},{8,0},{16,24},{24,16},{1,9},{9,1},{17,25},{25,17},{2,10},{10... | collective-permute-start | bytes 6291464 | tf_op jit(solution)/shard_map/ppermute | solution.py:72
  138.8 61.9 %collective-permute-start.15 = (bf16[512,2048]{1,0:T(8,128)(2,1)}, bf16[512,2048]{1,0:T(8,128)(2,1)}, u32[]{:S(2)}, u32[]{:S(2)}) collective-permute-start(bf16[512,2048]{1,0:T(8,128)(2,1)} %get-tuple-element.150.refs_2_.refs_0_), channel_id=1, source_target_pairs={{0,16},{8,24},{16,0},{24,8},{1,17},{9,25},{17,1},{25,9},{2,18},{10... | collective-permute-start | bytes 6291464 | tf_op jit(solution)/shard_map/ppermute | solution.py:72
  200.7 513.0 %reduce-scatter.7.cloned.1.call-start = ((), (), s32[]{:S(2)}) async-start(), calls=%async_computation.5 | async-start | bytes 23592960
  238.6 54.2 %collective-permute-start.27 = (bf16[1024,1024]{1,0:T(8,128)(2,1)S(1)}, bf16[1024,1024]{1,0:T(8,128)(2,1)}, u32[]{:S(2)}, u32[]{:S(2)}) collective-permute-start(bf16[1024,1024]{1,0:T(8,128)(2,1)S(1)} %pad_maximum_fusion.6.key_a.value_a), channel_id=1, source_target_pairs={{0,1},{1,0},{2,3},{3,2},{4,5},{5,4},{6,7},{7,6},{8,9},{9,8},{10,11... | collective-permute-start | bytes 6291464 | tf_op jit(solution)/shard_map/ppermute | solution.py:68
  242.3 47.4 %collective-permute-start.16 = (bf16[256,2048]{1,0:T(8,128)(2,1)S(1)}, bf16[256,2048]{1,0:T(8,128)(2,1)}, u32[]{:S(2)}, u32[]{:S(2)}) collective-permute-start(bf16[256,2048]{1,0:T(8,128)(2,1)S(1)} %slice.417), channel_id=1, source_target_pairs={{0,16},{8,24},{16,0},{24,8},{1,17},{9,25},{17,1},{25,9},{2,18},{10... | collective-permute-start | bytes 3145736 | tf_op jit(solution)/shard_map/ppermute | solution.py:72
  243.5 47.8 %collective-permute-start.17 = (bf16[256,2048]{1,0:T(8,128)(2,1)S(1)}, bf16[256,2048]{1,0:T(8,128)(2,1)}, u32[]{:S(2)}, u32[]{:S(2)}) collective-permute-start(bf16[256,2048]{1,0:T(8,128)(2,1)S(1)} %slice.418), channel_id=1, source_target_pairs={{0,8},{8,0},{16,24},{24,16},{1,9},{9,1},{17,25},{25,17},{2,10},{10... | collective-permute-start | bytes 3145736 | tf_op jit(solution)/shard_map/ppermute | solution.py:72
  244.8 84.7 %collective-permute-start.28 = (bf16[512,2048]{1,0:T(8,128)(2,1)}, bf16[512,2048]{1,0:T(8,128)(2,1)}, u32[]{:S(2)}, u32[]{:S(2)}) collective-permute-start(bf16[512,2048]{1,0:T(8,128)(2,1)} %collective-permute-done.14.refs_3_.refs_1_), channel_id=1, source_target_pairs={{0,1},{1,0},{2,3},{3,2},{4,5},{5,4},{6,7},{7,6},{8,9},{9,8},{10,11... | collective-permute-start | bytes 6291464 | tf_op jit(solution)/shard_map/ppermute | solution.py:68
  246.0 83.5 %collective-permute-start.29 = (bf16[512,2048]{1,0:T(8,128)(2,1)}, bf16[512,2048]{1,0:T(8,128)(2,1)}, u32[]{:S(2)}, u32[]{:S(2)}) collective-permute-start(bf16[512,2048]{1,0:T(8,128)(2,1)} %collective-permute-done.15.refs_4_.refs_2_), channel_id=1, source_target_pairs={{0,1},{1,0},{2,3},{3,2},{4,5},{5,4},{6,7},{7,6},{8,9},{9,8},{10,11... | collective-permute-start | bytes 6291464 | tf_op jit(solution)/shard_map/ppermute | solution.py:68
  289.7 39.7 %collective-permute-start.30 = (bf16[256,2048]{1,0:T(8,128)(2,1)}, bf16[256,2048]{1,0:T(8,128)(2,1)}, u32[]{:S(2)}, u32[]{:S(2)}) collective-permute-start(bf16[256,2048]{1,0:T(8,128)(2,1)} %collective-permute-done.16.refs_5_.refs_3_), channel_id=1, source_target_pairs={{0,1},{1,0},{2,3},{3,2},{4,5},{5,4},{6,7},{7,6},{8,9},{9,8},{10,11... | collective-permute-start | bytes 3145736 | tf_op jit(solution)/shard_map/ppermute | solution.py:68
  291.3 38.2 %collective-permute-start.31 = (bf16[256,2048]{1,0:T(8,128)(2,1)}, bf16[256,2048]{1,0:T(8,128)(2,1)}, u32[]{:S(2)}, u32[]{:S(2)}) collective-permute-start(bf16[256,2048]{1,0:T(8,128)(2,1)} %collective-permute-done.17.refs_6_.refs_4_), channel_id=1, source_target_pairs={{0,1},{1,0},{2,3},{3,2},{4,5},{5,4},{6,7},{7,6},{8,9},{9,8},{10,11... | collective-permute-start | bytes 3145736 | tf_op jit(solution)/shard_map/ppermute | solution.py:68
  511.5 286.1 %reduce-scatter.5.cloned.1.call-start = ((), (), s32[]{:S(2)}) async-start(), calls=%async_computation.2 | async-start | bytes 10485760 | tf_op jit(solution)/shard_map/reduce_scatter | solution.py:1099
  591.4 60.5 %collective-permute-start.42 = (bf16[4,256,2048]{2,1,0:T(8,128)(2,1)}, bf16[4,256,2048]{2,1,0:T(8,128)(2,1)}, u32[]{:S(2)}, u32[]{:S(2)}) collective-permute-start(bf16[4,256,2048]{2,1,0:T(8,128)(2,1)} %mixtures.3), channel_id=1, source_target_pairs={{0,1},{1,0},{2,3},{3,2},{4,5},{5,4},{6,7},{7,6},{8,9},{9,8},{10,11... | collective-permute-start | bytes 12582920 | tf_op jit(solution)/shard_map/ppermute | solution.py:68
  688.7 241.6 %all-reduce.6.cloned.1.call-start = ((), (), s32[]{:S(2)}) async-start(), calls=%async_computation.3 | async-start | bytes 4194304 | tf_op jit(solution)/shard_map/psum | solution.py:138
  765.1 60.9 %collective-permute-start.55 = (bf16[1024,2048]{1,0:T(8,128)(2,1)}, bf16[1024,2048]{1,0:T(8,128)(2,1)}, u32[]{:S(2)}, u32[]{:S(2)}) collective-permute-start(bf16[1024,2048]{1,0:T(8,128)(2,1)} %convolution_convert_fusion.2), channel_id=1, source_target_pairs={{0,1},{1,0},{2,3},{3,2},{4,5},{5,4},{6,7},{7,6},{8,9},{9,8},{10,11... | collective-permute-start | bytes 12582920 | tf_op jit(solution)/shard_map/ppermute | solution.py:68
  821.3 61.1 %collective-permute-start.60 = (bf16[1024,2048]{1,0:T(8,128)(2,1)}, bf16[1024,2048]{1,0:T(8,128)(2,1)}, u32[]{:S(2)}, u32[]{:S(2)}) collective-permute-start(bf16[1024,2048]{1,0:T(8,128)(2,1)} %convolution_convert_fusion.1), channel_id=1, source_target_pairs={{0,1},{1,0},{2,3},{3,2},{4,5},{5,4},{6,7},{7,6},{8,9},{9,8},{10,11... | collective-permute-start | bytes 12582920 | tf_op jit(solution)/shard_map/ppermute | solution.py:68
  834.5 262.2 %all-reduce.8.cloned.1.call-start = ((), (), s32[]{:S(2)}) async-start(), calls=%async_computation.6 | async-start | bytes 4194304 | tf_op jit(solution)/shard_map/psum | solution.py:138
  988.5 44.9 %collective-permute-start.83 = (bf16[512,2048]{1,0:T(8,128)(2,1)}, bf16[512,2048]{1,0:T(8,128)(2,1)}, u32[]{:S(2)}, u32[]{:S(2)}) collective-permute-start(bf16[512,2048]{1,0:T(8,128)(2,1)} %all-reduce.6.cloned.1.call-done), channel_id=1, source_target_pairs={{0,1},{1,0},{2,3},{3,2},{4,5},{5,4},{6,7},{7,6},{8,9},{9,8},{10,11... | collective-permute-start | bytes 6291464 | tf_op jit(solution)/shard_map/ppermute | solution.py:68
  1109.0 57.2 %collective-permute-start.71 = (bf16[256,2048]{1,0:T(8,128)(2,1)}, bf16[256,2048]{1,0:T(8,128)(2,1)}, u32[]{:S(2)}, u32[]{:S(2)}) collective-permute-start(bf16[256,2048]{1,0:T(8,128)(2,1)} %get-tuple-element.322), channel_id=1, source_target_pairs={{0,1},{1,0},{2,3},{3,2},{4,5},{5,4},{6,7},{7,6},{8,9},{9,8},{10,11... | collective-permute-start | bytes 3145736 | tf_op jit(solution)/shard_map/ppermute | solution.py:68
  1109.2 69.9 %collective-permute-start.72 = (bf16[256,2048]{1,0:T(8,128)(2,1)}, bf16[256,2048]{1,0:T(8,128)(2,1)}, u32[]{:S(2)}, u32[]{:S(2)}) collective-permute-start(bf16[256,2048]{1,0:T(8,128)(2,1)} %get-tuple-element.323), channel_id=1, source_target_pairs={{0,1},{1,0},{2,3},{3,2},{4,5},{5,4},{6,7},{7,6},{8,9},{9,8},{10,11... | collective-permute-start | bytes 3145736 | tf_op jit(solution)/shard_map/ppermute | solution.py:68
  (194 other events, 2710.7 us)
Sparse Core Ops, SparseCore 0:
  200.8 199.3 all-gather.2
  511.6 167.7 reduce-scatter.6
  688.8 84.3 reduce-scatter.4
  834.7 95.5 all-reduce.5
  1013.9 82.8 all-reduce.7

commit v3 on v2

--- a/solution.py
+++ b/solution.py
@@ -278,8 +278,9 @@
     return jnp.concatenate(parts, axis=1)
 
 
-def core_sum(mine, other):
-    return plus(mine, swap_core(other))
+def core_sum(mine, other, before=()):
+    got = swap_core(other)
+    return plus(mine, after(got, *before) if before else got)
 
 
 def whole_shard(shares):
@@ -987,14 +988,12 @@
     )
     out_second = ga_second_hop(out_first, 0, 1, ())
     out_mine = out_first + out_second
-    out_swapped = swap_pieces(out_mine[1:] if ga_count == 4 else out_mine)
-    out_other = ([out_twin] if ga_count == 4 else []) + out_swapped
     expert_own = jnp.concatenate([w_gate, w_up, jnp.swapaxes(w_down, 1, 2)], axis=2)
     expert_all = lax.all_gather(after(expert_own, *out_first[1:], *kv_steps[1]), "ga", axis=0)
 
     att_mine, att_other, log_rows = attend(
         place,
-        after(qkv, *out_second),
+        qkv,
         kv_mine,
         kv_other,
         bias,
@@ -1002,6 +1001,9 @@
         sine,
         query_gain_row,
     )
+    out_swapped = swap_pieces(out_first[1:] if ga_count == 4 else out_first)
+    out_swapped += swap_pieces([after(piece, att_mine) for piece in out_second])
+    out_other = ([out_twin] if ga_count == 4 else []) + out_swapped
     hidden = input_f + pieces_matmul((att_mine, att_other), (out_mine, out_other))
     ffn_in = rms_norm(hidden, ffn_gain_f).astype(BF16)
 
@@ -1095,7 +1097,7 @@
     held = [mix.step(*rows.held)]
     back(0, out_terms[1], expert_sum, *mix.sent)
     held.append(mix.step(raw_grads[0]))
-    out_total = core_sum(*out_terms)
+    out_total = core_sum(*out_terms, before=[att_grads])
     out_share = lax.psum_scatter(out_total, "ga", scatter_dimension=0, tiled=True)
     back(1, raw_grads[0], out_total, *held[0])
     held.append(mix.step(raw_grads[1]))
@@ -1131,12 +1133,12 @@
     kv_total = core_sum(*weight_terms(kv_raw_grad))
     kv_first = ga_sum_first(after(kv_total, query_shares[1]))
     query_alls = [z_all_sum(after(share, out_all)) for share in query_shares]
-    kv_share = ga_sum_second((kv_first[0],) + tuple(after(p, *query_alls) for p in kv_first[1:]))
-    kv_sum = whole_shard([z_all_sum_small(kv_share)])
+    kv_share = ga_sum_second(kv_first)
+    kv_sum = whole_shard([z_all_sum_small(after(kv_share, *query_alls))])
     out_sum = whole_shard([out_all])
     query_sum = whole_shard(query_alls)
     key_sum, value_sum = kv_sum[:, :kv_width], kv_sum[:, kv_width:]
-    both_grads = after(both_grads, *query_alls)
+    both_grads = after(both_grads, query_shares[1])
     half_width = model_width // 2
     normed_grad = join_cols(both_grads[:, :half_width], both_grads[:, half_width:])
     unused, attn_back = jax.vjp(rms_norm, input_f, attn_gain_f)
@@ -1144,7 +1146,8 @@
     input_grad = (hidden_grad + input_part).astype(BF16)
 
     tiny = [attn_gain_grad, query_gain_grad, key_gain_grad, ffn_gain_grad, router_grad.reshape(-1)]
-    tiny_own = sum_small(jnp.concatenate([t.reshape(ga_count, -1) for t in tiny], axis=1))
+    tiny_rows = jnp.concatenate([t.reshape(ga_count, -1) for t in tiny], axis=1)
+    tiny_own = sum_small(after(tiny_rows, *query_alls))
     at, tiny_sums = 0, []
     for piece in tiny:
         width = piece.shape[0] // ga_count

time: 1200 us -> 1160 us (0.967)
  waiting for transfers between devices: 458 us -> 403 us
    ppermute x30, waiting for transfers between devices: 105 us -> 53.9 us  [swap_axis(): lax.ppermute(value, axis, [(i, i ^ bit) for i in range(lax.axis_size(axis...]
    unnamed x252 -> x218, local copies, waits for them, and re-layouts: 34.4 us -> 27.1 us
  transfers between devices with their start and end apart: 94 -> 94, of which waited for: 41 -> 43; matrix products, arithmetic and copies ran while one was open for 17% -> 20% of each run, Pallas kernels for 22% -> 23%
where the time goes in v3:
time: 1160 us; the launch traced here: 1150 us
  waiting for transfers between devices  403 us (35%)
  Pallas kernels  323 us (28%)
  starting transfers between devices  146 us (13%)
  other arithmetic  126 us (11%)
  local copies, waits for them, and re-layouts  85.8 us (7%)
  matrix products  43.4 us (4%)
  between operations  23.5 us (2%)
    ppermute x9, waiting for transfers between devices, line_gather(): lax.ppermute(down, 'z', [(p, p - 1) for p in range(1, count - step + 1)])  113 us
    psum x2, waiting for transfers between devices, z_all_sum(): return lax.psum(value, 'z')  103 us
    pallas_call x4, Pallas kernels, attend_back(): pl.pallas_call(attend_back_kernel, grid_spec=pltpu.PrefetchScalarGridSpec...  74.2 us
    pallas_call x4, Pallas kernels, rows_back(): pl.pallas_call(functools.partial(rows_back_kernel, cap, shards), grid=(ex...  60.7 us
    ppermute x9, waiting for transfers between devices, step(): up = lax.ppermute(up, 'z', [(p, p + 1) for p in range(self.done)])  60.4 us
    ppermute x30, waiting for transfers between devices, swap_axis(): lax.ppermute(value, axis, [(i, i ^ bit) for i in range(lax.axis_size(axis...  53.9 us
    ppermute x9, starting transfers between devices, step(): up = lax.ppermute(up, 'z', [(p, p + 1) for p in range(self.done)])  49.1 us
    pallas_call x2, Pallas kernels, expert_rows(): pl.pallas_call(functools.partial(expert_kernel, cap), grid_spec=pltpu.Pre...  44.7 us
  transfers between devices with their start and end apart: 94, of which 43 were waited for; matrix products, arithmetic and copies ran while one was open for 20% of the time, Pallas kernels for 23%

profile of v3, /device:TPU:1, one launch (start us, length us, event | category | flops | bytes accessed | tf_op | source)
XLA Modules:
  0.0 1150.8 jit_solution(13206135565745816145)
XLA Ops:
  39.5 14.1 %collective-permute-done.4 = bf16[256,2176]{1,0:T(8,128)(2,1)} collective-permute-done((bf16[256,2176]{1,0:T(8,128)(2,1)S(1)}, bf16[256,2176]{1,0:T(8,128)(2,1)}, u32[]{:S(2)}, u32[]{:S(2)}) %collective-permute-start.4) | collective-permute-done | bytes 1114144 | tf_op jit(solution)/shard_map/ppermute | solution.py:90
  70.5 16.1 %collective-permute-done.7 = bf16[256,2176]{1,0:T(8,128)(2,1)} collective-permute-done((bf16[256,2176]{1,0:T(8,128)(2,1)}, bf16[256,2176]{1,0:T(8,128)(2,1)}, u32[]{:S(2)}, u32[]{:S(2)}) %collective-permute-start.7) | collective-permute-done | bytes 1114144 | tf_op jit(solution)/shard_map/ppermute | solution.py:91
  109.6 18.5 %collective-permute-done.17 = bf16[256,2176]{1,0:T(8,128)(2,1)S(1)} collective-permute-done((bf16[256,2176]{1,0:T(8,128)(2,1)}, bf16[256,2176]{1,0:T(8,128)(2,1)S(1)}, u32[]{:S(2)}, u32[]{:S(2)}) %collective-permute-start.17) | collective-permute-done | bytes 1114144 | tf_op jit(solution)/shard_map/ppermute | solution.py:91
  150.2 14.1 %dense_matmul.2.raw_ref = f32[256,5120]{1,0:T(8,128)} custom-call(bf16[256,1024]{1,0:T(8,128)(2,1)} %pad_maximum_fusion.12.refs_0_, bf16[256,1024]{1,0:T(8,128)(2,1)} %pad_maximum_fusion.13.refs_1_, bf16[256,5120]{1,0:T(8,128)(2,1)} %pad_maximum_fusion.4.refs_2_.refs_0_, bf16[256,5120]{1,0:T(8,128)(2,1)} %collective-permute-done.2.refs_3_.refs_1_, ...), custom_call_target="tpu_custom_call" | custom-call | flops 6000000000 | bytes 1024 | tf_op jit(solution)/shard_map/dense_matmul/pallas_call | solution.py:321
  249.1 36.7 %attend.1 = (bf16[256,2048]{1,0:T(8,128)(2,1)}, bf16[256,2048]{1,0:T(8,128)(2,1)}, f32[4,8,256]{2,1,0:T(8,128)}) custom-call(s32[12]{0:T(128)} %pad_add_fusion.place, f32[256,5120]{1,0:T(8,128)} %dense_matmul.2.raw_ref, bf16[1024,1024]{1,0:T(8,128)(2,1)} %copy-done.4, bf16[1024,1024]{1,0:T(8,128)(2,1)} %collective-permute-done.25.key_b.value_b, ...), custom_call_target="tpu_custom_call" | custom-call | flops 2000000000 | bytes 1024 | tf_op jit(solution)/shard_map/attend/pallas_call | solution.py:524
  296.8 13.4 %dense_matmul.3 = f32[256,2048]{1,0:T(8,128)} custom-call(bf16[256,2048]{1,0:T(8,128)(2,1)} %get-tuple-element.166.refs_0_.out_mine, bf16[256,2048]{1,0:T(8,128)(2,1)} %get-tuple-element.167.refs_1_.out_other, bf16[512,2048]{1,0:T(8,128)(2,1)} %get-tuple-element.161.refs_2_.refs_0_, bf16[512,2048]{1,0:T(8,128)(2,1)} %collective-permute-done.21.refs_3_.refs_1_, ...), custom_call_target="tpu_custom_call" | custom-call | flops 6000000000 | bytes 1024 | tf_op jit(solution)/shard_map/dense_matmul/pallas_call | solution.py:321
  316.6 20.7 %collective-permute-done.32 = bf16[256,2048]{1,0:T(8,128)(2,1)S(1)} collective-permute-done((bf16[256,2048]{1,0:T(8,128)(2,1)S(1)}, bf16[256,2048]{1,0:T(8,128)(2,1)S(1)}, u32[]{:S(2)}, u32[]{:S(2)}) %collective-permute-start.32) | collective-permute-done | bytes 1048608 | tf_op jit(solution)/shard_map/ppermute | solution.py:90
  343.3 23.9 %collective-permute-done.35 = bf16[256,2048]{1,0:T(8,128)(2,1)S(1)} collective-permute-done((bf16[256,2048]{1,0:T(8,128)(2,1)S(1)}, bf16[256,2048]{1,0:T(8,128)(2,1)S(1)}, u32[]{:S(2)}, u32[]{:S(2)}) %collective-permute-start.35) | collective-permute-done | bytes 1048608 | tf_op jit(solution)/shard_map/ppermute | solution.py:91
  369.6 22.7 %collective-permute-done.37 = bf16[256,2048]{1,0:T(8,128)(2,1)S(1)} collective-permute-done((bf16[256,2048]{1,0:T(8,128)(2,1)S(1)}, bf16[256,2048]{1,0:T(8,128)(2,1)S(1)}, u32[]{:S(2)}, u32[]{:S(2)}) %collective-permute-start.37) | collective-permute-done | bytes 1048608 | tf_op jit(solution)/shard_map/ppermute | solution.py:91
  402.9 22.2 %expert_rows.2 = (bf16[2,576,2048]{2,1,0:T(8,128)(2,1)}, bf16[2,576,768]{2,1,0:T(8,128)(2,1)}, bf16[2,576,1536]{2,1,0:T(8,128)(2,1)}, bf16[2,576,128]{2,1,0:T(8,128)(2,1)}) custom-call(s32[2]{0:T(128)} %pad_add_fusion.2.first_ref, bf16[1024,2048]{1,0:T(8,128)(2,1)} %pad_maximum_fusion.2.rows_ref, s32[2,4,256]{2,1,0:T(4,128)} %bitcast.154, ...), custom_call_target="tpu_custom_call" | custom-call | flops 11000000512 | bytes 1024 | tf_op jit(solution)/shard_map/expert_rows/pallas_call | solution.py:761
  425.1 22.5 %expert_rows.3 = (bf16[2,576,2048]{2,1,0:T(8,128)(2,1)}, bf16[2,576,768]{2,1,0:T(8,128)(2,1)}, bf16[2,576,1536]{2,1,0:T(8,128)(2,1)}, bf16[2,576,128]{2,1,0:T(8,128)(2,1)}) custom-call(s32[2]{0:T(128)} %pad_add_fusion.2.first_ref, bf16[1024,2048]{1,0:T(8,128)(2,1)} %collective-permute-done.38.rows_ref, s32[2,4,256]{2,1,0:T(4,128)} %bitcast.156, ...), custom_call_target="tpu_custom_call" | custom-call | flops 11000000512 | bytes 1024 | tf_op jit(solution)/shard_map/expert_rows/pallas_call | solution.py:761
  447.5 36.1 %expert_grads.1 = bf16[4,2,512,2304]{3,2,1,0:T(8,128)(2,1)} custom-call(bf16[2,576,2048]{2,1,0:T(8,128)(2,1)} %get-tuple-element.183.row_a, bf16[2,576,2048]{2,1,0:T(8,128)(2,1)} %get-tuple-element.184.row_b, bf16[2,576,2048]{2,1,0:T(8,128)(2,1)} %pick.2.cot_ref.cot_a, bf16[2,576,2048]{2,1,0:T(8,128)(2,1)} %pick.3.cot_ref.cot_b, ...), custom_call_target="tpu_custom_call" | custom-call | flops 17999998976 | bytes 1024 | tf_op jit(solution)/shard_map/expert_grads/pallas_call | solution.py:862
  485.3 18.1 %row_grads.2 = bf16[4,256,2176]{2,1,0:T(8,128)(2,1)} custom-call(bf16[2,576,1536]{2,1,0:T(8,128)(2,1)} %get-tuple-element.186.pre_b.left_ref, s32[1024,2]{1,0:T(8,128)} %bitcast.138, bf16[4,2,512,2304]{3,2,1,0:T(8,128)(2,1)} %bitcast.119, bf16[4,2,512,2304]{3,2,1,0:T(8,128)(2,1)} %bitcast.120, bf16[4,2,512,2304]{3,2,1,0:T(8,128)(2,1)} %bitcast.121, ...), custom_call_target="tpu_custom_call" | custom-call | flops 10000000000 | bytes 1024 | tf_op jit(solution)/shard_map/row_grads/pallas_call | solution.py:833
  504.5 18.0 %row_grads.3 = bf16[4,256,2176]{2,1,0:T(8,128)(2,1)} custom-call(bf16[2,576,1536]{2,1,0:T(8,128)(2,1)} %get-tuple-element.188.pre_a.left_ref, s32[1024,2]{1,0:T(8,128)} %bitcast.136, bf16[4,2,512,2304]{3,2,1,0:T(8,128)(2,1)} %bitcast.123, bf16[4,2,512,2304]{3,2,1,0:T(8,128)(2,1)} %bitcast.124, bf16[4,2,512,2304]{3,2,1,0:T(8,128)(2,1)} %bitcast.125, ...), custom_call_target="tpu_custom_call" | custom-call | flops 10000000000 | bytes 1024 | tf_op jit(solution)/shard_map/row_grads/pallas_call | solution.py:833
  602.9 14.0 %collective-permute-done.45 = bf16[256,2176]{1,0:T(8,128)(2,1)} collective-permute-done((bf16[256,2176]{1,0:T(8,128)(2,1)}, bf16[256,2176]{1,0:T(8,128)(2,1)}, u32[]{:S(2)}, u32[]{:S(2)}) %collective-permute-start.45) | collective-permute-done | bytes 1114144 | tf_op jit(solution)/shard_map/ppermute | solution.py:114
  667.3 20.2 %collective-permute-done.48 = bf16[256,2048]{1,0:T(8,128)(2,1)} collective-permute-done((bf16[256,2048]{1,0:T(8,128)(2,1)}, bf16[256,2048]{1,0:T(8,128)(2,1)}, u32[]{:S(2)}, u32[]{:S(2)}) %collective-permute-start.48) | collective-permute-done | bytes 1048608 | tf_op jit(solution)/shard_map/ppermute | solution.py:114
  687.5 19.0 %attend_back.4 = (bf16[256,1024]{1,0:T(8,128)(2,1)}, bf16[2048,256]{1,0:T(8,128)(2,1)}, f32[8,128]{1,0:T(8,128)}) custom-call(s32[12]{0:T(128)} %pad_add_fusion.place, f32[256,5120]{1,0:T(8,128)} %dense_matmul.2.raw_ref, bf16[1024,1024]{1,0:T(8,128)(2,1)} %copy-done.4, bf16[1024,1024]{1,0:T(8,128)(2,1)} %collective-permute-done.25.key_b.value_b, ...), custom_call_target="tpu_custom_call" | custom-call | flops 8999999488 | bytes 1024 | tf_op jit(solution)/shard_map/attend_back/pallas_call | solution.py:630
  717.7 18.4 %attend_back.5 = (bf16[256,1024]{1,0:T(8,128)(2,1)}, bf16[2048,256]{1,0:T(8,128)(2,1)}, f32[8,128]{1,0:T(8,128)}) custom-call(s32[12]{0:T(128)} %pad_add_fusion.place, f32[256,5120]{1,0:T(8,128)} %dense_matmul.2.raw_ref, bf16[1024,1024]{1,0:T(8,128)(2,1)} %copy-done.4, bf16[1024,1024]{1,0:T(8,128)(2,1)} %collective-permute-done.25.key_b.value_b, ...), custom_call_target="tpu_custom_call" | custom-call | flops 8999999488 | bytes 1024 | tf_op jit(solution)/shard_map/attend_back/pallas_call | solution.py:630
  752.6 18.4 %attend_back.6 = (bf16[256,1024]{1,0:T(8,128)(2,1)}, bf16[2048,256]{1,0:T(8,128)(2,1)}, f32[8,128]{1,0:T(8,128)}) custom-call(s32[12]{0:T(128)} %pad_add_fusion.place, f32[256,5120]{1,0:T(8,128)} %dense_matmul.2.raw_ref, bf16[1024,1024]{1,0:T(8,128)(2,1)} %copy-done.4, bf16[1024,1024]{1,0:T(8,128)(2,1)} %collective-permute-done.25.key_b.value_b, ...), custom_call_target="tpu_custom_call" | custom-call | flops 8999999488 | bytes 1024 | tf_op jit(solution)/shard_map/attend_back/pallas_call | solution.py:630
  777.8 18.4 %attend_back.7 = (bf16[256,1024]{1,0:T(8,128)(2,1)}, bf16[2048,256]{1,0:T(8,128)(2,1)}, f32[8,128]{1,0:T(8,128)}) custom-call(s32[12]{0:T(128)} %pad_add_fusion.place, f32[256,5120]{1,0:T(8,128)} %dense_matmul.2.raw_ref, bf16[1024,1024]{1,0:T(8,128)(2,1)} %copy-done.4, bf16[1024,1024]{1,0:T(8,128)(2,1)} %collective-permute-done.25.key_b.value_b, ...), custom_call_target="tpu_custom_call" | custom-call | flops 8999999488 | bytes 1024 | tf_op jit(solution)/shard_map/attend_back/pallas_call | solution.py:630
  854.7 47.2 %all-reduce.6.cloned.1.call-done = bf16[512,2048]{1,0:T(8,128)(2,1)} async-done(((bf16[512,2048]{1,0:T(8,128)(2,1)}), bf16[512,2048]{1,0:T(8,128)(2,1)}) %all-reduce.6.cloned.1.call-update) | async-done | bytes 2097168 | tf_op jit(solution)/shard_map/psum | solution.py:138
  931.7 14.1 %collective-permute-start.65 = (bf16[256,1024]{1,0:T(8,128)(2,1)S(1)}, bf16[256,1024]{1,0:T(8,128)(2,1)S(1)}, u32[]{:S(2)}, u32[]{:S(2)}) collective-permute-start(bf16[256,1024]{1,0:T(8,128)(2,1)S(1)} %add_convert_fusion.29), channel_id=1, source_target_pairs={{0,2},{2,4},{4,6},{1,3},{3,5},{5,7},{8,10},{10,12},{12,14},{9,11},... | collective-permute-start | bytes 1572872 | tf_op jit(solution)/shard_map/ppermute | solution.py:114
  974.1 15.5 %dense_back.3 = f32[256,2048]{1,0:T(8,128)} custom-call(bf16[256,5120]{1,0:T(8,128)(2,1)} %constant_dynamic-update-slice_fusion.4.left_ref, bf16[256,5120]{1,0:T(8,128)(2,1)} %pad_maximum_fusion.4.refs_2_.refs_0_, bf16[256,5120]{1,0:T(8,128)(2,1)} %collective-permute-done.2.refs_3_.refs_1_, bf16[256,5120]{1,0:T(8,128)(2,1)} %collective-permute-done.3.refs_4_.refs_2_, ...), custom_call_target="tpu_custom_call" | custom-call | flops 6000000000 | bytes 1024 | tf_op jit(solution)/shard_map/dense_back/pallas_call | solution.py:356
  1032.4 56.0 %all-reduce.8.cloned.1.call-done = (bf16[256,2048]{1,0:T(8,128)(2,1)}, bf16[256,2048]{1,0:T(8,128)(2,1)}) async-done(((bf16[256,2048]{1,0:T(8,128)(2,1)}, bf16[256,2048]{1,0:T(8,128)(2,1)}), (bf16[256,2048]{1,0:T(8,128)(2,1)}, bf16[256,2048]{1,0:T(8,128)(2,1)})) %all-reduce.8.cloned.1.call-update) | async-done | bytes 2097168 | tf_op jit(solution)/shard_map/psum | solution.py:138
  (604 shorter events, 588.9 us)
Async XLA Ops:
  7.2 393.0 %all-gather.3.cloned.1.call-start = ((), (), s32[]{:S(2)}) async-start(), calls=%async_computation.4 | async-start | bytes 23592960 | tf_op jit(solution)/shard_map/all_gather | solution.py:992
  35.3 58.5 %collective-permute-start.2 = (bf16[256,5120]{1,0:T(8,128)(2,1)}, bf16[256,5120]{1,0:T(8,128)(2,1)}, u32[]{:S(2)}, u32[]{:S(2)}) collective-permute-start(bf16[256,5120]{1,0:T(8,128)(2,1)} %pad_maximum_fusion.4.refs_2_.refs_0_), channel_id=1, source_target_pairs={{0,8},{8,0},{16,24},{24,16},{1,9},{9,1},{17,25},{25,17},{2,10},{10... | collective-permute-start | bytes 7864328 | tf_op jit(solution)/shard_map/ppermute | solution.py:72
  38.2 64.7 %collective-permute-start.3 = (bf16[256,5120]{1,0:T(8,128)(2,1)}, bf16[256,5120]{1,0:T(8,128)(2,1)}, u32[]{:S(2)}, u32[]{:S(2)}) collective-permute-start(bf16[256,5120]{1,0:T(8,128)(2,1)} %pad_maximum_fusion.4.refs_2_.refs_0_), channel_id=1, source_target_pairs={{0,16},{8,24},{16,0},{24,8},{1,17},{9,25},{17,1},{25,9},{2,18},{10... | collective-permute-start | bytes 7864328 | tf_op jit(solution)/shard_map/ppermute | solution.py:72
  93.8 44.9 %collective-permute-start.10 = (bf16[256,5120]{1,0:T(8,128)(2,1)}, bf16[256,5120]{1,0:T(8,128)(2,1)S(1)}, u32[]{:S(2)}, u32[]{:S(2)}) collective-permute-start(bf16[256,5120]{1,0:T(8,128)(2,1)} %collective-permute-done.2.refs_3_.refs_1_), channel_id=1, source_target_pairs={{0,1},{1,0},{2,3},{3,2},{4,5},{5,4},{6,7},{7,6},{8,9},{9,8},{10,11... | collective-permute-start | bytes 7864328 | tf_op jit(solution)/shard_map/ppermute | solution.py:68
  105.9 40.1 %collective-permute-start.11 = (bf16[256,5120]{1,0:T(8,128)(2,1)}, bf16[256,5120]{1,0:T(8,128)(2,1)}, u32[]{:S(2)}, u32[]{:S(2)}) collective-permute-start(bf16[256,5120]{1,0:T(8,128)(2,1)} %collective-permute-done.3.refs_4_.refs_2_), channel_id=1, source_target_pairs={{0,1},{1,0},{2,3},{3,2},{4,5},{5,4},{6,7},{7,6},{8,9},{9,8},{10,11... | collective-permute-start | bytes 7864328 | tf_op jit(solution)/shard_map/ppermute | solution.py:68
  138.4 62.2 %collective-permute-start.21 = (bf16[512,2048]{1,0:T(8,128)(2,1)}, bf16[512,2048]{1,0:T(8,128)(2,1)}, u32[]{:S(2)}, u32[]{:S(2)}) collective-permute-start(bf16[512,2048]{1,0:T(8,128)(2,1)} %get-tuple-element.161.refs_2_.refs_0_), channel_id=1, source_target_pairs={{0,8},{8,0},{16,24},{24,16},{1,9},{9,1},{17,25},{25,17},{2,10},{10... | collective-permute-start | bytes 6291464 | tf_op jit(solution)/shard_map/ppermute | solution.py:72
  138.7 61.9 %collective-permute-start.22 = (bf16[512,2048]{1,0:T(8,128)(2,1)}, bf16[512,2048]{1,0:T(8,128)(2,1)}, u32[]{:S(2)}, u32[]{:S(2)}) collective-permute-start(bf16[512,2048]{1,0:T(8,128)(2,1)} %get-tuple-element.161.refs_2_.refs_0_), channel_id=1, source_target_pairs={{0,16},{8,24},{16,0},{24,8},{1,17},{9,25},{17,1},{25,9},{2,18},{10... | collective-permute-start | bytes 6291464 | tf_op jit(solution)/shard_map/ppermute | solution.py:72
  200.6 486.8 %reduce-scatter.7.cloned.1.call-start = ((), (), s32[]{:S(2)}) async-start(), calls=%async_computation.5 | async-start | bytes 23592960
  244.3 46.8 %collective-permute-start.26 = (bf16[256,2048]{1,0:T(8,128)(2,1)}, bf16[256,2048]{1,0:T(8,128)(2,1)}, u32[]{:S(2)}, u32[]{:S(2)}) collective-permute-start(bf16[256,2048]{1,0:T(8,128)(2,1)} %slice.420), channel_id=1, source_target_pairs={{0,16},{8,24},{16,0},{24,8},{1,17},{9,25},{17,1},{25,9},{2,18},{10... | collective-permute-start | bytes 3145736 | tf_op jit(solution)/shard_map/ppermute | solution.py:72
  245.4 46.4 %collective-permute-start.27 = (bf16[256,2048]{1,0:T(8,128)(2,1)}, bf16[256,2048]{1,0:T(8,128)(2,1)}, u32[]{:S(2)}, u32[]{:S(2)}) collective-permute-start(bf16[256,2048]{1,0:T(8,128)(2,1)} %slice.421), channel_id=1, source_target_pairs={{0,8},{8,0},{16,24},{24,16},{1,9},{9,1},{17,25},{25,17},{2,10},{10... | collective-permute-start | bytes 3145736 | tf_op jit(solution)/shard_map/ppermute | solution.py:72
  246.6 45.2 %collective-permute-start.28 = (bf16[512,2048]{1,0:T(8,128)(2,1)}, bf16[512,2048]{1,0:T(8,128)(2,1)}, u32[]{:S(2)}, u32[]{:S(2)}) collective-permute-start(bf16[512,2048]{1,0:T(8,128)(2,1)} %collective-permute-done.21.refs_3_.refs_1_), channel_id=1, source_target_pairs={{0,1},{1,0},{2,3},{3,2},{4,5},{5,4},{6,7},{7,6},{8,9},{9,8},{10,11... | collective-permute-start | bytes 6291464 | tf_op jit(solution)/shard_map/ppermute | solution.py:68
  247.9 44.0 %collective-permute-start.29 = (bf16[512,2048]{1,0:T(8,128)(2,1)}, bf16[512,2048]{1,0:T(8,128)(2,1)}, u32[]{:S(2)}, u32[]{:S(2)}) collective-permute-start(bf16[512,2048]{1,0:T(8,128)(2,1)} %collective-permute-done.22.refs_4_.refs_2_), channel_id=1, source_target_pairs={{0,1},{1,0},{2,3},{3,2},{4,5},{5,4},{6,7},{7,6},{8,9},{9,8},{10,11... | collective-permute-start | bytes 6291464 | tf_op jit(solution)/shard_map/ppermute | solution.py:68
  483.6 294.1 %reduce-scatter.5.cloned.1.call-start = ((), (), s32[]{:S(2)}) async-start(), calls=%async_computation.2 | async-start | bytes 10485760 | tf_op jit(solution)/shard_map/reduce_scatter | solution.py:1101
  564.4 61.2 %collective-permute-start.42 = (bf16[4,256,2048]{2,1,0:T(8,128)(2,1)}, bf16[4,256,2048]{2,1,0:T(8,128)(2,1)}, u32[]{:S(2)}, u32[]{:S(2)}) collective-permute-start(bf16[4,256,2048]{2,1,0:T(8,128)(2,1)} %mixtures.3), channel_id=1, source_target_pairs={{0,1},{1,0},{2,3},{3,2},{4,5},{5,4},{6,7},{7,6},{8,9},{9,8},{10,11... | collective-permute-start | bytes 12582920 | tf_op jit(solution)/shard_map/ppermute | solution.py:68
  663.3 238.5 %all-reduce.6.cloned.1.call-start = ((), (), s32[]{:S(2)}) async-start(), calls=%async_computation.3 | async-start | bytes 4194304 | tf_op jit(solution)/shard_map/psum | solution.py:138
  743.8 68.6 %collective-permute-start.55 = (bf16[1024,2048]{1,0:T(8,128)(2,1)}, bf16[1024,2048]{1,0:T(8,128)(2,1)}, u32[]{:S(2)}, u32[]{:S(2)}) collective-permute-start(bf16[1024,2048]{1,0:T(8,128)(2,1)} %convolution_convert_fusion.2), channel_id=1, source_target_pairs={{0,1},{1,0},{2,3},{3,2},{4,5},{5,4},{6,7},{7,6},{8,9},{9,8},{10,11... | collective-permute-start | bytes 12582920 | tf_op jit(solution)/shard_map/ppermute | solution.py:68
  812.1 101.4 %collective-permute-start.60 = (bf16[1024,2048]{1,0:T(8,128)(2,1)}, bf16[1024,2048]{1,0:T(8,128)(2,1)}, u32[]{:S(2)}, u32[]{:S(2)}) collective-permute-start(bf16[1024,2048]{1,0:T(8,128)(2,1)} %convolution_convert_fusion.1), channel_id=1, source_target_pairs={{0,1},{1,0},{2,3},{3,2},{4,5},{5,4},{6,7},{7,6},{8,9},{9,8},{10,11... | collective-permute-start | bytes 12582920 | tf_op jit(solution)/shard_map/ppermute | solution.py:68
  812.1 276.3 %all-reduce.8.cloned.1.call-start = ((), (), s32[]{:S(2)}) async-start(), calls=%async_computation.6 | async-start | bytes 4194304 | tf_op jit(solution)/shard_map/psum | solution.py:138
  837.1 73.2 %collective-permute-start.57 = (bf16[256,2048]{1,0:T(8,128)(2,1)}, bf16[256,2048]{1,0:T(8,128)(2,1)}, u32[]{:S(2)}, u32[]{:S(2)}) collective-permute-start(bf16[256,2048]{1,0:T(8,128)(2,1)} %pad_maximum_fusion.8), channel_id=1, source_target_pairs={{0,8},{8,0},{16,24},{24,16},{1,9},{9,1},{17,25},{25,17},{2,10},{10... | collective-permute-start | bytes 3145736 | tf_op jit(solution)/shard_map/ppermute | solution.py:72
  838.5 71.8 %collective-permute-start.59 = (bf16[256,2048]{1,0:T(8,128)(2,1)}, bf16[256,2048]{1,0:T(8,128)(2,1)}, u32[]{:S(2)}, u32[]{:S(2)}) collective-permute-start(bf16[256,2048]{1,0:T(8,128)(2,1)} %pad_maximum_fusion.9), channel_id=1, source_target_pairs={{0,16},{8,24},{16,0},{24,8},{1,17},{9,25},{17,1},{25,9},{2,18},{10... | collective-permute-start | bytes 3145736 | tf_op jit(solution)/shard_map/ppermute | solution.py:72
  839.7 62.9 %collective-permute-start.61 = (bf16[256,1024]{1,0:T(8,128)(2,1)S(1)}, bf16[256,1024]{1,0:T(8,128)(2,1)}, u32[]{:S(2)}, u32[]{:S(2)}) collective-permute-start(bf16[256,1024]{1,0:T(8,128)(2,1)S(1)} %get-tuple-element.242), channel_id=1, source_target_pairs={{0,2},{1,3},{8,10},{9,11},{16,18},{17,19},{24,26},{25,27}} | collective-permute-start | bytes 1572872 | tf_op jit(solution)/shard_map/ppermute | solution.py:114
  948.1 41.5 %collective-permute-start.69 = (bf16[256,2048]{1,0:T(8,128)(2,1)S(1)}, bf16[256,2048]{1,0:T(8,128)(2,1)}, u32[]{:S(2)}, u32[]{:S(2)}) collective-permute-start(bf16[256,2048]{1,0:T(8,128)(2,1)S(1)} %pad_maximum_fusion.10), channel_id=1, source_target_pairs={{0,8},{8,0},{16,24},{24,16},{1,9},{9,1},{17,25},{25,17},{2,10},{10... | collective-permute-start | bytes 3145736 | tf_op jit(solution)/shard_map/ppermute | solution.py:72
  1090.6 44.5 %collective-permute-start.71 = (bf16[256,2048]{1,0:T(8,128)(2,1)S(1)}, bf16[256,2048]{1,0:T(8,128)(2,1)}, u32[]{:S(2)}, u32[]{:S(2)}) collective-permute-start(bf16[256,2048]{1,0:T(8,128)(2,1)S(1)} %copy-done.44), channel_id=1, source_target_pairs={{0,1},{1,0},{2,3},{3,2},{4,5},{5,4},{6,7},{7,6},{8,9},{9,8},{10,11... | collective-permute-start | bytes 3145736 | tf_op jit(solution)/shard_map/ppermute | solution.py:68
  1090.8 48.6 %collective-permute-start.72 = (bf16[256,2048]{1,0:T(8,128)(2,1)S(1)}, bf16[256,2048]{1,0:T(8,128)(2,1)}, u32[]{:S(2)}, u32[]{:S(2)}) collective-permute-start(bf16[256,2048]{1,0:T(8,128)(2,1)S(1)} %copy-done.43), channel_id=1, source_target_pairs={{0,1},{1,0},{2,3},{3,2},{4,5},{5,4},{6,7},{7,6},{8,9},{9,8},{10,11... | collective-permute-start | bytes 3145736 | tf_op jit(solution)/shard_map/ppermute | solution.py:68
  (176 other events, 2451.9 us)
Sparse Core Ops, SparseCore 0:
  200.7 199.3 all-gather.2
  483.7 170.3 reduce-scatter.6
  663.5 83.2 reduce-scatter.4
  812.2 89.6 all-reduce.5
  1003.7 84.7 all-reduce.7

commit v4 on v3

--- a/solution.py
+++ b/solution.py
@@ -1068,7 +1068,10 @@
     branch_grad = hidden_grad.astype(BF16)
     out_terms = [dot_tn(device_cols(a), branch_grad) for a in (att_mine, att_other)]
     out_terms[1] = out_terms[1].astype(BF16)
-    att_grads = pieces_back(after(branch_grad, out_terms[1]), out_mine + out_other, BF16)
+    held = [mix.step(*rows.held)]
+    att_grads = pieces_back(
+        after(branch_grad, out_terms[1], *held[0]), out_mine + out_other, BF16
+    )
     raw_grads, kv_grads, gain_grads = [], [], []
 
     def back(head, *before):
@@ -1094,7 +1097,6 @@
     def weight_terms(grad):
         return dot_tn(normed_mine, grad), dot_tn(normed_other, grad).astype(BF16)
 
-    held = [mix.step(*rows.held)]
     back(0, out_terms[1], expert_sum, *mix.sent)
     held.append(mix.step(raw_grads[0]))
     out_total = core_sum(*out_terms, before=[att_grads])
@@ -1115,11 +1117,11 @@
     kv_grad = after(jnp.concatenate(kv_grads, axis=1), *held[2])
     kv_grad = kv_grad.reshape(2, z_count, tok_count, 2 * kv_width)
     keys_values = LineSum(core_slots(kv_grad[0], kv_grad[1]))
-    keys_values.step(query_terms[1][1], *query_firsts[0])
+    out_all = z_all_sum(out_share)
+    keys_values.step(query_terms[1][1], *query_firsts[0], out_all)
     query_shares = [ga_sum_second(query_firsts[0])]
     query_totals.append(core_sum(*query_terms[1]))
-    out_all = z_all_sum(out_share)
-    keys_values.step(query_totals[1], out_all)
+    keys_values.step(query_totals[1])
     query_firsts.append(ga_sum_first(after(query_totals[1], query_shares[0])))
     keys_values.step(query_shares[0])
     kv_raw_grad, key_gain_grad = kv_back(

time: 1160 us -> 1160 us (level)
    unnamed x218 -> x226, local copies, waits for them, and re-layouts: 27.1 us -> 28.2 us
  transfers between devices with their start and end apart: 94 -> 94, of which waited for: 43 -> 42; matrix products, arithmetic and copies ran while one was open for 20% -> 20% of each run, Pallas kernels for 23% -> 23%
where the time goes in v4:
time: 1160 us; the launch traced here: 1150 us
  waiting for transfers between devices  410 us (35%)
  Pallas kernels  323 us (28%)
  starting transfers between devices  142 us (12%)
  other arithmetic  124 us (11%)
  local copies, waits for them, and re-layouts  87 us (8%)
  matrix products  43.4 us (4%)
  between operations  23.7 us (2%)
    psum x2, waiting for transfers between devices, z_all_sum(): return lax.psum(value, 'z')  114 us
    ppermute x9, waiting for transfers between devices, line_gather(): lax.ppermute(down, 'z', [(p, p - 1) for p in range(1, count - step + 1)])  113 us
    pallas_call x4, Pallas kernels, attend_back(): pl.pallas_call(attend_back_kernel, grid_spec=pltpu.PrefetchScalarGridSpec...  74.1 us
    pallas_call x4, Pallas kernels, rows_back(): pl.pallas_call(functools.partial(rows_back_kernel, cap, shards), grid=(ex...  60.7 us
    ppermute x9, waiting for transfers between devices, step(): up = lax.ppermute(up, 'z', [(p, p + 1) for p in range(self.done)])  59.2 us
    ppermute x30, waiting for transfers between devices, swap_axis(): lax.ppermute(value, axis, [(i, i ^ bit) for i in range(lax.axis_size(axis...  53.7 us
    ppermute x9, starting transfers between devices, step(): up = lax.ppermute(up, 'z', [(p, p + 1) for p in range(self.done)])  45.5 us
    pallas_call x2, Pallas kernels, expert_rows(): pl.pallas_call(functools.partial(expert_kernel, cap), grid_spec=pltpu.Pre...  44.7 us
  transfers between devices with their start and end apart: 94, of which 42 were waited for; matrix products, arithmetic and copies ran while one was open for 20% of the time, Pallas kernels for 23%

profile of v4, /device:TPU:1, one launch (start us, length us, event | category | flops | bytes accessed | tf_op | source)
XLA Modules:
  0.0 1153.6 jit_solution(2256336166041890460)
XLA Ops:
  39.5 14.1 %collective-permute-done.4 = bf16[256,2176]{1,0:T(8,128)(2,1)} collective-permute-done((bf16[256,2176]{1,0:T(8,128)(2,1)S(1)}, bf16[256,2176]{1,0:T(8,128)(2,1)}, u32[]{:S(2)}, u32[]{:S(2)}) %collective-permute-start.4) | collective-permute-done | bytes 1114144 | tf_op jit(solution)/shard_map/ppermute | solution.py:90
  70.5 16.0 %collective-permute-done.7 = bf16[256,2176]{1,0:T(8,128)(2,1)} collective-permute-done((bf16[256,2176]{1,0:T(8,128)(2,1)}, bf16[256,2176]{1,0:T(8,128)(2,1)}, u32[]{:S(2)}, u32[]{:S(2)}) %collective-permute-start.7) | collective-permute-done | bytes 1114144 | tf_op jit(solution)/shard_map/ppermute | solution.py:91
  109.6 18.5 %collective-permute-done.17 = bf16[256,2176]{1,0:T(8,128)(2,1)S(1)} collective-permute-done((bf16[256,2176]{1,0:T(8,128)(2,1)}, bf16[256,2176]{1,0:T(8,128)(2,1)S(1)}, u32[]{:S(2)}, u32[]{:S(2)}) %collective-permute-start.17) | collective-permute-done | bytes 1114144 | tf_op jit(solution)/shard_map/ppermute | solution.py:91
  150.2 14.1 %dense_matmul.2.raw_ref = f32[256,5120]{1,0:T(8,128)} custom-call(bf16[256,1024]{1,0:T(8,128)(2,1)} %pad_maximum_fusion.12.refs_0_, bf16[256,1024]{1,0:T(8,128)(2,1)} %pad_maximum_fusion.13.refs_1_, bf16[256,5120]{1,0:T(8,128)(2,1)} %pad_maximum_fusion.4.refs_2_.refs_0_, bf16[256,5120]{1,0:T(8,128)(2,1)} %collective-permute-done.2.refs_3_.refs_1_, ...), custom_call_target="tpu_custom_call" | custom-call | flops 6000000000 | bytes 1024 | tf_op jit(solution)/shard_map/dense_matmul/pallas_call | solution.py:321
  249.1 36.7 %attend.1 = (bf16[256,2048]{1,0:T(8,128)(2,1)}, bf16[256,2048]{1,0:T(8,128)(2,1)}, f32[4,8,256]{2,1,0:T(8,128)}) custom-call(s32[12]{0:T(128)} %pad_add_fusion.place, f32[256,5120]{1,0:T(8,128)} %dense_matmul.2.raw_ref, bf16[1024,1024]{1,0:T(8,128)(2,1)} %copy-done.4, bf16[1024,1024]{1,0:T(8,128)(2,1)} %collective-permute-done.25.key_b.value_b, ...), custom_call_target="tpu_custom_call" | custom-call | flops 2000000000 | bytes 1024 | tf_op jit(solution)/shard_map/attend/pallas_call | solution.py:524
  296.8 13.4 %dense_matmul.3 = f32[256,2048]{1,0:T(8,128)} custom-call(bf16[256,2048]{1,0:T(8,128)(2,1)} %get-tuple-element.166.refs_0_.out_mine, bf16[256,2048]{1,0:T(8,128)(2,1)} %get-tuple-element.167.refs_1_.out_other, bf16[512,2048]{1,0:T(8,128)(2,1)} %get-tuple-element.161.refs_2_.refs_0_, bf16[512,2048]{1,0:T(8,128)(2,1)} %collective-permute-done.21.refs_3_.refs_1_, ...), custom_call_target="tpu_custom_call" | custom-call | flops 6000000000 | bytes 1024 | tf_op jit(solution)/shard_map/dense_matmul/pallas_call | solution.py:321
  316.6 20.7 %collective-permute-done.32 = bf16[256,2048]{1,0:T(8,128)(2,1)S(1)} collective-permute-done((bf16[256,2048]{1,0:T(8,128)(2,1)S(1)}, bf16[256,2048]{1,0:T(8,128)(2,1)S(1)}, u32[]{:S(2)}, u32[]{:S(2)}) %collective-permute-start.32) | collective-permute-done | bytes 1048608 | tf_op jit(solution)/shard_map/ppermute | solution.py:90
  343.3 23.9 %collective-permute-done.35 = bf16[256,2048]{1,0:T(8,128)(2,1)S(1)} collective-permute-done((bf16[256,2048]{1,0:T(8,128)(2,1)S(1)}, bf16[256,2048]{1,0:T(8,128)(2,1)S(1)}, u32[]{:S(2)}, u32[]{:S(2)}) %collective-permute-start.35) | collective-permute-done | bytes 1048608 | tf_op jit(solution)/shard_map/ppermute | solution.py:91
  369.6 22.7 %collective-permute-done.37 = bf16[256,2048]{1,0:T(8,128)(2,1)S(1)} collective-permute-done((bf16[256,2048]{1,0:T(8,128)(2,1)S(1)}, bf16[256,2048]{1,0:T(8,128)(2,1)S(1)}, u32[]{:S(2)}, u32[]{:S(2)}) %collective-permute-start.37) | collective-permute-done | bytes 1048608 | tf_op jit(solution)/shard_map/ppermute | solution.py:91
  402.9 22.2 %expert_rows.2 = (bf16[2,576,2048]{2,1,0:T(8,128)(2,1)}, bf16[2,576,768]{2,1,0:T(8,128)(2,1)}, bf16[2,576,1536]{2,1,0:T(8,128)(2,1)}, bf16[2,576,128]{2,1,0:T(8,128)(2,1)}) custom-call(s32[2]{0:T(128)} %pad_add_fusion.2.first_ref, bf16[1024,2048]{1,0:T(8,128)(2,1)} %pad_maximum_fusion.2.rows_ref, s32[2,4,256]{2,1,0:T(4,128)} %bitcast.154, ...), custom_call_target="tpu_custom_call" | custom-call | flops 11000000512 | bytes 1024 | tf_op jit(solution)/shard_map/expert_rows/pallas_call | solution.py:761
  425.1 22.5 %expert_rows.3 = (bf16[2,576,2048]{2,1,0:T(8,128)(2,1)}, bf16[2,576,768]{2,1,0:T(8,128)(2,1)}, bf16[2,576,1536]{2,1,0:T(8,128)(2,1)}, bf16[2,576,128]{2,1,0:T(8,128)(2,1)}) custom-call(s32[2]{0:T(128)} %pad_add_fusion.2.first_ref, bf16[1024,2048]{1,0:T(8,128)(2,1)} %collective-permute-done.38.rows_ref, s32[2,4,256]{2,1,0:T(4,128)} %bitcast.156, ...), custom_call_target="tpu_custom_call" | custom-call | flops 11000000512 | bytes 1024 | tf_op jit(solution)/shard_map/expert_rows/pallas_call | solution.py:761
  447.5 36.1 %expert_grads.1 = bf16[4,2,512,2304]{3,2,1,0:T(8,128)(2,1)} custom-call(bf16[2,576,2048]{2,1,0:T(8,128)(2,1)} %get-tuple-element.183.row_a, bf16[2,576,2048]{2,1,0:T(8,128)(2,1)} %get-tuple-element.184.row_b, bf16[2,576,2048]{2,1,0:T(8,128)(2,1)} %pick.2.cot_ref.cot_a, bf16[2,576,2048]{2,1,0:T(8,128)(2,1)} %pick.3.cot_ref.cot_b, ...), custom_call_target="tpu_custom_call" | custom-call | flops 17999998976 | bytes 1024 | tf_op jit(solution)/shard_map/expert_grads/pallas_call | solution.py:862
  485.3 18.1 %row_grads.2 = bf16[4,256,2176]{2,1,0:T(8,128)(2,1)} custom-call(bf16[2,576,1536]{2,1,0:T(8,128)(2,1)} %get-tuple-element.186.pre_b.left_ref, s32[1024,2]{1,0:T(8,128)} %bitcast.138, bf16[4,2,512,2304]{3,2,1,0:T(8,128)(2,1)} %bitcast.119, bf16[4,2,512,2304]{3,2,1,0:T(8,128)(2,1)} %bitcast.120, bf16[4,2,512,2304]{3,2,1,0:T(8,128)(2,1)} %bitcast.121, ...), custom_call_target="tpu_custom_call" | custom-call | flops 10000000000 | bytes 1024 | tf_op jit(solution)/shard_map/row_grads/pallas_call | solution.py:833
  504.5 18.0 %row_grads.3 = bf16[4,256,2176]{2,1,0:T(8,128)(2,1)} custom-call(bf16[2,576,1536]{2,1,0:T(8,128)(2,1)} %get-tuple-element.188.pre_a.left_ref, s32[1024,2]{1,0:T(8,128)} %bitcast.136, bf16[4,2,512,2304]{3,2,1,0:T(8,128)(2,1)} %bitcast.123, bf16[4,2,512,2304]{3,2,1,0:T(8,128)(2,1)} %bitcast.124, bf16[4,2,512,2304]{3,2,1,0:T(8,128)(2,1)} %bitcast.125, ...), custom_call_target="tpu_custom_call" | custom-call | flops 10000000000 | bytes 1024 | tf_op jit(solution)/shard_map/row_grads/pallas_call | solution.py:833
  602.9 13.9 %collective-permute-done.45 = bf16[256,2176]{1,0:T(8,128)(2,1)} collective-permute-done((bf16[256,2176]{1,0:T(8,128)(2,1)}, bf16[256,2176]{1,0:T(8,128)(2,1)}, u32[]{:S(2)}, u32[]{:S(2)}) %collective-permute-start.45) | collective-permute-done | bytes 1114144 | tf_op jit(solution)/shard_map/ppermute | solution.py:114
  646.2 20.9 %collective-permute-done.47 = bf16[256,2048]{1,0:T(8,128)(2,1)S(1)} collective-permute-done((bf16[256,2048]{1,0:T(8,128)(2,1)S(1)}, bf16[256,2048]{1,0:T(8,128)(2,1)S(1)}, u32[]{:S(2)}, u32[]{:S(2)}) %collective-permute-start.47) | collective-permute-done | bytes 1048608 | tf_op jit(solution)/shard_map/ppermute | solution.py:114
  685.8 18.7 %attend_back.4 = (bf16[256,1024]{1,0:T(8,128)(2,1)}, bf16[2048,256]{1,0:T(8,128)(2,1)}, f32[8,128]{1,0:T(8,128)}) custom-call(s32[12]{0:T(128)} %pad_add_fusion.place, f32[256,5120]{1,0:T(8,128)} %dense_matmul.2.raw_ref, bf16[1024,1024]{1,0:T(8,128)(2,1)} %copy-done.4, bf16[1024,1024]{1,0:T(8,128)(2,1)} %collective-permute-done.25.key_b.value_b, ...), custom_call_target="tpu_custom_call" | custom-call | flops 8999999488 | bytes 1024 | tf_op jit(solution)/shard_map/attend_back/pallas_call | solution.py:630
  714.6 18.6 %attend_back.5 = (bf16[256,1024]{1,0:T(8,128)(2,1)}, bf16[2048,256]{1,0:T(8,128)(2,1)}, f32[8,128]{1,0:T(8,128)}) custom-call(s32[12]{0:T(128)} %pad_add_fusion.place, f32[256,5120]{1,0:T(8,128)} %dense_matmul.2.raw_ref, bf16[1024,1024]{1,0:T(8,128)(2,1)} %copy-done.4, bf16[1024,1024]{1,0:T(8,128)(2,1)} %collective-permute-done.25.key_b.value_b, ...), custom_call_target="tpu_custom_call" | custom-call | flops 8999999488 | bytes 1024 | tf_op jit(solution)/shard_map/attend_back/pallas_call | solution.py:630
  746.9 18.4 %attend_back.6 = (bf16[256,1024]{1,0:T(8,128)(2,1)}, bf16[2048,256]{1,0:T(8,128)(2,1)}, f32[8,128]{1,0:T(8,128)}) custom-call(s32[12]{0:T(128)} %pad_add_fusion.place, f32[256,5120]{1,0:T(8,128)} %dense_matmul.2.raw_ref, bf16[1024,1024]{1,0:T(8,128)(2,1)} %copy-done.4, bf16[1024,1024]{1,0:T(8,128)(2,1)} %collective-permute-done.25.key_b.value_b, ...), custom_call_target="tpu_custom_call" | custom-call | flops 8999999488 | bytes 1024 | tf_op jit(solution)/shard_map/attend_back/pallas_call | solution.py:630
  772.5 18.4 %attend_back.7 = (bf16[256,1024]{1,0:T(8,128)(2,1)}, bf16[2048,256]{1,0:T(8,128)(2,1)}, f32[8,128]{1,0:T(8,128)}) custom-call(s32[12]{0:T(128)} %pad_add_fusion.place, f32[256,5120]{1,0:T(8,128)} %dense_matmul.2.raw_ref, bf16[1024,1024]{1,0:T(8,128)(2,1)} %copy-done.4, bf16[1024,1024]{1,0:T(8,128)(2,1)} %collective-permute-done.25.key_b.value_b, ...), custom_call_target="tpu_custom_call" | custom-call | flops 8999999488 | bytes 1024 | tf_op jit(solution)/shard_map/attend_back/pallas_call | solution.py:630
  834.3 57.6 %all-reduce.6.cloned.1.call-done = bf16[512,2048]{1,0:T(8,128)(2,1)} async-done(((bf16[512,2048]{1,0:T(8,128)(2,1)}), bf16[512,2048]{1,0:T(8,128)(2,1)}) %all-reduce.6.cloned.1.call-update) | async-done | bytes 2097168 | tf_op jit(solution)/shard_map/psum | solution.py:138
  933.6 14.9 %collective-permute-start.65 = (bf16[256,1024]{1,0:T(8,128)(2,1)S(1)}, bf16[256,1024]{1,0:T(8,128)(2,1)S(1)}, u32[]{:S(2)}, u32[]{:S(2)}) collective-permute-start(bf16[256,1024]{1,0:T(8,128)(2,1)S(1)} %add_convert_fusion.29), channel_id=1, source_target_pairs={{0,2},{2,4},{4,6},{1,3},{3,5},{5,7},{8,10},{10,12},{12,14},{9,11},... | collective-permute-start | bytes 1572872 | tf_op jit(solution)/shard_map/ppermute | solution.py:114
  976.8 15.5 %dense_back.3 = f32[256,2048]{1,0:T(8,128)} custom-call(bf16[256,5120]{1,0:T(8,128)(2,1)} %constant_dynamic-update-slice_fusion.4.left_ref, bf16[256,5120]{1,0:T(8,128)(2,1)} %pad_maximum_fusion.4.refs_2_.refs_0_, bf16[256,5120]{1,0:T(8,128)(2,1)} %collective-permute-done.2.refs_3_.refs_1_, bf16[256,5120]{1,0:T(8,128)(2,1)} %collective-permute-done.3.refs_4_.refs_2_, ...), custom_call_target="tpu_custom_call" | custom-call | flops 6000000000 | bytes 1024 | tf_op jit(solution)/shard_map/dense_back/pallas_call | solution.py:356
  1035.1 56.1 %all-reduce.8.cloned.1.call-done = (bf16[256,2048]{1,0:T(8,128)(2,1)}, bf16[256,2048]{1,0:T(8,128)(2,1)}) async-done(((bf16[256,2048]{1,0:T(8,128)(2,1)}, bf16[256,2048]{1,0:T(8,128)(2,1)}), (bf16[256,2048]{1,0:T(8,128)(2,1)}, bf16[256,2048]{1,0:T(8,128)(2,1)})) %all-reduce.8.cloned.1.call-update) | async-done | bytes 2097168 | tf_op jit(solution)/shard_map/psum | solution.py:138
  (612 shorter events, 579.8 us)
Async XLA Ops:
  7.2 393.0 %all-gather.3.cloned.1.call-start = ((), (), s32[]{:S(2)}) async-start(), calls=%async_computation.4 | async-start | bytes 23592960 | tf_op jit(solution)/shard_map/all_gather | solution.py:992
  35.3 58.5 %collective-permute-start.2 = (bf16[256,5120]{1,0:T(8,128)(2,1)}, bf16[256,5120]{1,0:T(8,128)(2,1)}, u32[]{:S(2)}, u32[]{:S(2)}) collective-permute-start(bf16[256,5120]{1,0:T(8,128)(2,1)} %pad_maximum_fusion.4.refs_2_.refs_0_), channel_id=1, source_target_pairs={{0,8},{8,0},{16,24},{24,16},{1,9},{9,1},{17,25},{25,17},{2,10},{10... | collective-permute-start | bytes 7864328 | tf_op jit(solution)/shard_map/ppermute | solution.py:72
  38.2 64.7 %collective-permute-start.3 = (bf16[256,5120]{1,0:T(8,128)(2,1)}, bf16[256,5120]{1,0:T(8,128)(2,1)}, u32[]{:S(2)}, u32[]{:S(2)}) collective-permute-start(bf16[256,5120]{1,0:T(8,128)(2,1)} %pad_maximum_fusion.4.refs_2_.refs_0_), channel_id=1, source_target_pairs={{0,16},{8,24},{16,0},{24,8},{1,17},{9,25},{17,1},{25,9},{2,18},{10... | collective-permute-start | bytes 7864328 | tf_op jit(solution)/shard_map/ppermute | solution.py:72
  93.8 44.9 %collective-permute-start.10 = (bf16[256,5120]{1,0:T(8,128)(2,1)}, bf16[256,5120]{1,0:T(8,128)(2,1)S(1)}, u32[]{:S(2)}, u32[]{:S(2)}) collective-permute-start(bf16[256,5120]{1,0:T(8,128)(2,1)} %collective-permute-done.2.refs_3_.refs_1_), channel_id=1, source_target_pairs={{0,1},{1,0},{2,3},{3,2},{4,5},{5,4},{6,7},{7,6},{8,9},{9,8},{10,11... | collective-permute-start | bytes 7864328 | tf_op jit(solution)/shard_map/ppermute | solution.py:68
  105.9 40.1 %collective-permute-start.11 = (bf16[256,5120]{1,0:T(8,128)(2,1)}, bf16[256,5120]{1,0:T(8,128)(2,1)}, u32[]{:S(2)}, u32[]{:S(2)}) collective-permute-start(bf16[256,5120]{1,0:T(8,128)(2,1)} %collective-permute-done.3.refs_4_.refs_2_), channel_id=1, source_target_pairs={{0,1},{1,0},{2,3},{3,2},{4,5},{5,4},{6,7},{7,6},{8,9},{9,8},{10,11... | collective-permute-start | bytes 7864328 | tf_op jit(solution)/shard_map/ppermute | solution.py:68
  138.4 62.2 %collective-permute-start.21 = (bf16[512,2048]{1,0:T(8,128)(2,1)}, bf16[512,2048]{1,0:T(8,128)(2,1)}, u32[]{:S(2)}, u32[]{:S(2)}) collective-permute-start(bf16[512,2048]{1,0:T(8,128)(2,1)} %get-tuple-element.161.refs_2_.refs_0_), channel_id=1, source_target_pairs={{0,8},{8,0},{16,24},{24,16},{1,9},{9,1},{17,25},{25,17},{2,10},{10... | collective-permute-start | bytes 6291464 | tf_op jit(solution)/shard_map/ppermute | solution.py:72
  138.7 61.9 %collective-permute-start.22 = (bf16[512,2048]{1,0:T(8,128)(2,1)}, bf16[512,2048]{1,0:T(8,128)(2,1)}, u32[]{:S(2)}, u32[]{:S(2)}) collective-permute-start(bf16[512,2048]{1,0:T(8,128)(2,1)} %get-tuple-element.161.refs_2_.refs_0_), channel_id=1, source_target_pairs={{0,16},{8,24},{16,0},{24,8},{1,17},{9,25},{17,1},{25,9},{2,18},{10... | collective-permute-start | bytes 6291464 | tf_op jit(solution)/shard_map/ppermute | solution.py:72
  200.6 485.2 %reduce-scatter.7.cloned.1.call-start = ((), (), s32[]{:S(2)}) async-start(), calls=%async_computation.5 | async-start | bytes 23592960
  244.3 46.8 %collective-permute-start.26 = (bf16[256,2048]{1,0:T(8,128)(2,1)}, bf16[256,2048]{1,0:T(8,128)(2,1)}, u32[]{:S(2)}, u32[]{:S(2)}) collective-permute-start(bf16[256,2048]{1,0:T(8,128)(2,1)} %slice.420), channel_id=1, source_target_pairs={{0,16},{8,24},{16,0},{24,8},{1,17},{9,25},{17,1},{25,9},{2,18},{10... | collective-permute-start | bytes 3145736 | tf_op jit(solution)/shard_map/ppermute | solution.py:72
  245.4 46.4 %collective-permute-start.27 = (bf16[256,2048]{1,0:T(8,128)(2,1)}, bf16[256,2048]{1,0:T(8,128)(2,1)}, u32[]{:S(2)}, u32[]{:S(2)}) collective-permute-start(bf16[256,2048]{1,0:T(8,128)(2,1)} %slice.421), channel_id=1, source_target_pairs={{0,8},{8,0},{16,24},{24,16},{1,9},{9,1},{17,25},{25,17},{2,10},{10... | collective-permute-start | bytes 3145736 | tf_op jit(solution)/shard_map/ppermute | solution.py:72
  246.6 45.3 %collective-permute-start.28 = (bf16[512,2048]{1,0:T(8,128)(2,1)}, bf16[512,2048]{1,0:T(8,128)(2,1)}, u32[]{:S(2)}, u32[]{:S(2)}) collective-permute-start(bf16[512,2048]{1,0:T(8,128)(2,1)} %collective-permute-done.21.refs_3_.refs_1_), channel_id=1, source_target_pairs={{0,1},{1,0},{2,3},{3,2},{4,5},{5,4},{6,7},{7,6},{8,9},{9,8},{10,11... | collective-permute-start | bytes 6291464 | tf_op jit(solution)/shard_map/ppermute | solution.py:68
  247.9 44.0 %collective-permute-start.29 = (bf16[512,2048]{1,0:T(8,128)(2,1)}, bf16[512,2048]{1,0:T(8,128)(2,1)}, u32[]{:S(2)}, u32[]{:S(2)}) collective-permute-start(bf16[512,2048]{1,0:T(8,128)(2,1)} %collective-permute-done.22.refs_4_.refs_2_), channel_id=1, source_target_pairs={{0,1},{1,0},{2,3},{3,2},{4,5},{5,4},{6,7},{7,6},{8,9},{9,8},{10,11... | collective-permute-start | bytes 6291464 | tf_op jit(solution)/shard_map/ppermute | solution.py:68
  483.6 288.8 %reduce-scatter.5.cloned.1.call-start = ((), (), s32[]{:S(2)}) async-start(), calls=%async_computation.2 | async-start | bytes 10485760 | tf_op jit(solution)/shard_map/reduce_scatter | solution.py:1103
  564.3 61.2 %collective-permute-start.42 = (bf16[4,256,2048]{2,1,0:T(8,128)(2,1)}, bf16[4,256,2048]{2,1,0:T(8,128)(2,1)}, u32[]{:S(2)}, u32[]{:S(2)}) collective-permute-start(bf16[4,256,2048]{2,1,0:T(8,128)(2,1)} %mixtures.3), channel_id=1, source_target_pairs={{0,1},{1,0},{2,3},{3,2},{4,5},{5,4},{6,7},{7,6},{8,9},{9,8},{10,11... | collective-permute-start | bytes 12582920 | tf_op jit(solution)/shard_map/ppermute | solution.py:68
  685.7 206.1 %all-reduce.6.cloned.1.call-start = ((), (), s32[]{:S(2)}) async-start(), calls=%async_computation.3 | async-start | bytes 4194304 | tf_op jit(solution)/shard_map/psum | solution.py:138
  740.9 66.0 %collective-permute-start.55 = (bf16[1024,2048]{1,0:T(8,128)(2,1)}, bf16[1024,2048]{1,0:T(8,128)(2,1)}, u32[]{:S(2)}, u32[]{:S(2)}) collective-permute-start(bf16[1024,2048]{1,0:T(8,128)(2,1)} %convolution_convert_fusion.2), channel_id=1, source_target_pairs={{0,1},{1,0},{2,3},{3,2},{4,5},{5,4},{6,7},{7,6},{8,9},{9,8},{10,11... | collective-permute-start | bytes 12582920 | tf_op jit(solution)/shard_map/ppermute | solution.py:68
  806.7 110.9 %collective-permute-start.60 = (bf16[1024,2048]{1,0:T(8,128)(2,1)}, bf16[1024,2048]{1,0:T(8,128)(2,1)}, u32[]{:S(2)}, u32[]{:S(2)}) collective-permute-start(bf16[1024,2048]{1,0:T(8,128)(2,1)} %convolution_convert_fusion.1), channel_id=1, source_target_pairs={{0,1},{1,0},{2,3},{3,2},{4,5},{5,4},{6,7},{7,6},{8,9},{9,8},{10,11... | collective-permute-start | bytes 12582920 | tf_op jit(solution)/shard_map/ppermute | solution.py:68
  806.7 284.5 %all-reduce.8.cloned.1.call-start = ((), (), s32[]{:S(2)}) async-start(), calls=%async_computation.6 | async-start | bytes 4194304 | tf_op jit(solution)/shard_map/psum | solution.py:138
  831.7 82.6 %collective-permute-start.57 = (bf16[256,2048]{1,0:T(8,128)(2,1)}, bf16[256,2048]{1,0:T(8,128)(2,1)}, u32[]{:S(2)}, u32[]{:S(2)}) collective-permute-start(bf16[256,2048]{1,0:T(8,128)(2,1)} %pad_maximum_fusion.8), channel_id=1, source_target_pairs={{0,8},{8,0},{16,24},{24,16},{1,9},{9,1},{17,25},{25,17},{2,10},{10... | collective-permute-start | bytes 3145736 | tf_op jit(solution)/shard_map/ppermute | solution.py:72
  833.1 81.2 %collective-permute-start.59 = (bf16[256,2048]{1,0:T(8,128)(2,1)}, bf16[256,2048]{1,0:T(8,128)(2,1)}, u32[]{:S(2)}, u32[]{:S(2)}) collective-permute-start(bf16[256,2048]{1,0:T(8,128)(2,1)} %pad_maximum_fusion.9), channel_id=1, source_target_pairs={{0,16},{8,24},{16,0},{24,8},{1,17},{9,25},{17,1},{25,9},{2,18},{10... | collective-permute-start | bytes 3145736 | tf_op jit(solution)/shard_map/ppermute | solution.py:72
  950.8 41.5 %collective-permute-start.69 = (bf16[256,2048]{1,0:T(8,128)(2,1)S(1)}, bf16[256,2048]{1,0:T(8,128)(2,1)}, u32[]{:S(2)}, u32[]{:S(2)}) collective-permute-start(bf16[256,2048]{1,0:T(8,128)(2,1)S(1)} %pad_maximum_fusion.10), channel_id=1, source_target_pairs={{0,8},{8,0},{16,24},{24,16},{1,9},{9,1},{17,25},{25,17},{2,10},{10... | collective-permute-start | bytes 3145736 | tf_op jit(solution)/shard_map/ppermute | solution.py:72
  953.2 39.2 %collective-permute-start.70 = (bf16[256,2048]{1,0:T(8,128)(2,1)}, bf16[256,2048]{1,0:T(8,128)(2,1)}, u32[]{:S(2)}, u32[]{:S(2)}) collective-permute-start(bf16[256,2048]{1,0:T(8,128)(2,1)} %pad_maximum_fusion.11), channel_id=1, source_target_pairs={{0,16},{8,24},{16,0},{24,8},{1,17},{9,25},{17,1},{25,9},{2,18},{10... | collective-permute-start | bytes 3145736 | tf_op jit(solution)/shard_map/ppermute | solution.py:72
  1093.4 44.5 %collective-permute-start.71 = (bf16[256,2048]{1,0:T(8,128)(2,1)S(1)}, bf16[256,2048]{1,0:T(8,128)(2,1)}, u32[]{:S(2)}, u32[]{:S(2)}) collective-permute-start(bf16[256,2048]{1,0:T(8,128)(2,1)S(1)} %copy-done.48), channel_id=1, source_target_pairs={{0,1},{1,0},{2,3},{3,2},{4,5},{5,4},{6,7},{7,6},{8,9},{9,8},{10,11... | collective-permute-start | bytes 3145736 | tf_op jit(solution)/shard_map/ppermute | solution.py:68
  1093.6 48.6 %collective-permute-start.72 = (bf16[256,2048]{1,0:T(8,128)(2,1)S(1)}, bf16[256,2048]{1,0:T(8,128)(2,1)}, u32[]{:S(2)}, u32[]{:S(2)}) collective-permute-start(bf16[256,2048]{1,0:T(8,128)(2,1)S(1)} %copy-done.47), channel_id=1, source_target_pairs={{0,1},{1,0},{2,3},{3,2},{4,5},{5,4},{6,7},{7,6},{8,9},{9,8},{10,11... | collective-permute-start | bytes 3145736 | tf_op jit(solution)/shard_map/ppermute | solution.py:68
  (180 other events, 2506.1 us)
Sparse Core Ops, SparseCore 0:
  200.7 199.3 all-gather.2
  483.7 170.3 reduce-scatter.6
  685.8 85.4 reduce-scatter.4
  806.8 84.9 all-reduce.5
  1006.5 84.7 all-reduce.7
